TPU v7x, 32 devices: a whole 2x2x4 slice. The times are simulated.
32 devices in a mesh: groups: 2 (over y), blk: 4 (over z), shard: 2 (over x), sub: 2 (over core).
Axes of the slice: x: 2, y: 2, z: 4, core: 2. Of those that a mesh axis runs over, the one named last changes fastest.
Arguments:
- head_table: float32 [4096, 400], P(('groups', 'blk', 'shard', 'sub')), parts along dimension 0, may hold values from -1.5 to 1.5
- head_accum: float32 [4096], P(('groups', 'blk', 'shard', 'sub')), parts along dimension 0, may hold values from 0.005 to 0.05
- tail_table: float32 [4096, 400], P(('groups', 'blk', 'shard', 'sub')), parts along dimension 0, may hold values from -1.5 to 1.5
- tail_accum: float32 [4096], P(('groups', 'blk', 'shard', 'sub')), parts along dimension 0, may hold values from 0.005 to 0.05
- relations: float32 [1536, 400], P('groups'), parts along dimension 0, may hold values from 0.5 to 1.5
- rel_accum: float32 [1536], P('groups'), parts along dimension 0, may hold values from 0.005 to 0.05
- head_ids: int32 [2, 8192], P(None, ('groups', 'blk', 'shard', 'sub')), parts along dimension 1, may hold values from 0 to 127
- tail_ids: int32 [2, 8192], P(None, ('groups', 'blk', 'shard', 'sub')), parts along dimension 1, may hold values from 0 to 127
- rel_ids: int32 [2, 8192], P(None, ('groups', 'blk', 'shard', 'sub')), parts along dimension 1, may hold values from 0 to 767, as said below
- neg_ids: int32 [2, 64, 128], P(None, ('groups', 'blk', 'shard', 'sub')), parts along dimension 1, may hold values from 0 to 127
Outputs:
- head_out: float32 [4096, 400], P(('groups', 'blk', 'shard', 'sub')), parts along dimension 0
- head_acc_out: float32 [4096], P(('groups', 'blk', 'shard', 'sub')), parts along dimension 0
- tail_out: float32 [4096, 400], P(('groups', 'blk', 'shard', 'sub')), parts along dimension 0
- tail_acc_out: float32 [4096], P(('groups', 'blk', 'shard', 'sub')), parts along dimension 0
- rel_out: float32 [1536, 400], P('groups'), parts along dimension 0
- rel_acc_out: float32 [1536], P('groups'), parts along dimension 0
There are 2 independent parts, one for each index of `groups`. A program takes and returns all parts, laid end to end along the dimension named above; each array names one. Nothing has to cross between parts.
Inputs may be any that keep to these rules, and one draw needn't show every extreme that they name: `rel_ids`: relation type of each edge; about half of a slice's edges use 768 // 16 relations tied to that slice.
All inputs are finite; a program needn't handle non-finite values.
Results may differ from a plain program's by a relative error of at most 0.0001.
Values sent between devices are 32-bit elements; how exact they have to be, the bound alone decides.
No kernel may reach another device: no remote copies, remote signals or barrier semaphores. Data moves between devices by JAX's collectives and lax.ppermute only.
A program may use at most 64 MiB of HBM per device.

v0:
```python
import jax
import jax.numpy as jnp
from jax import lax
from jax.sharding import PartitionSpec as P

HIGH = lax.Precision.HIGHEST
RATE = 0.1


def from_behind(block, axis, distance):
    devices = range(lax.axis_size(axis))
    route = [((i - distance) % len(devices), i) for i in devices]
    return lax.ppermute(block, axis, route)


def adagrad(weights, accum, grads):
    accum = accum + jnp.mean(grads * grads, axis=-1)
    return (weights - RATE * grads / jnp.sqrt(accum)[..., None], accum)


def row_sums(indices, values, rows):
    selector = (
        lax.broadcasted_iota(jnp.int32, (rows, indices.shape[0]), 0) == indices[None, :]
    ).astype(jnp.float32)
    return jnp.dot(selector, values, precision=HIGH, preferred_element_type=jnp.float32)


def bucket_grads(left, right, rel_table, left_ids, right_ids, kinds, negative):
    width = left.shape[1]
    rows = left.shape[0]
    heads = left[left_ids]
    tails = right[right_ids]
    rel_rows = rel_table[kinds]
    query = heads * rel_rows
    pos = jnp.sum(query * tails, axis=-1)
    count = negative.shape[0]
    qgroup = query.reshape(count, -1, width)
    negrows = right[negative]
    scores = jnp.einsum("cid,cjd->cij", qgroup, negrows, precision=HIGH)
    gpos = -jax.nn.sigmoid(-pos)
    gneg = jax.nn.sigmoid(scores) / negative.shape[1]
    gquery = gpos[:, None] * tails + jnp.einsum(
        "cij,cjd->cid", gneg, negrows, precision=HIGH
    ).reshape(-1, width)
    gnegrows = jnp.einsum("cij,cid->cjd", gneg, qgroup, precision=HIGH).reshape(-1, width)
    grad_left = row_sums(left_ids, gquery * rel_rows, rows)
    right_all = jnp.concatenate([right_ids, negative.reshape(-1)], axis=0)
    right_vals = jnp.concatenate([gpos[:, None] * query, gnegrows], axis=0)
    grad_right = row_sums(right_all, right_vals, rows)
    grad_rel = row_sums(kinds, gquery * heads, rel_table.shape[0])
    return (grad_left, grad_right, grad_rel)


def shards(
    head_table,
    head_accum,
    tail_table,
    tail_accum,
    relations,
    rel_accum,
    head_ids,
    tail_ids,
    rel_ids,
    neg_ids,
):
    heads, hacc = (head_table, head_accum)
    tails, tacc = (tail_table, tail_accum)
    rel_table, racc = (relations, rel_accum)
    steps_all = head_ids.shape[0]
    for step in range(steps_all):
        grad_left, grad_right, grad_rel = bucket_grads(
            heads, tails, rel_table, head_ids[step], tail_ids[step], rel_ids[step], neg_ids[step]
        )
        heads, hacc = adagrad(heads, hacc, grad_left)
        tails, tacc = adagrad(tails, tacc, grad_right)
        summed = lax.psum(grad_rel, ("blk", "shard", "sub"))
        rel_table, racc = adagrad(rel_table, racc, summed)
        if step + 1 < steps_all:
            tails, tacc = from_behind((tails, tacc), "blk", 1)
    return (heads, hacc, tails, tacc, rel_table, racc)


def solution(mesh):
    return jax.shard_map(
        shards,
        mesh=mesh,
        in_specs=(
            P(("groups", "blk", "shard", "sub"), None),
            P(("groups", "blk", "shard", "sub")),
            P(("groups", "blk", "shard", "sub"), None),
            P(("groups", "blk", "shard", "sub")),
            P("groups", None),
            P("groups"),
            P(None, ("groups", "blk", "shard", "sub")),
            P(None, ("groups", "blk", "shard", "sub")),
            P(None, ("groups", "blk", "shard", "sub")),
            P(None, ("groups", "blk", "shard", "sub"), None),
        ),
        out_specs=(
            P(("groups", "blk", "shard", "sub"), None),
            P(("groups", "blk", "shard", "sub")),
            P(("groups", "blk", "shard", "sub"), None),
            P(("groups", "blk", "shard", "sub")),
            P("groups", None),
            P("groups"),
        ),
        check_vma=False,
    )
```

profile of v0, /device:TPU:0, one launch (start us, length us, event | category | flops | bytes accessed | tf_op | source)
XLA Modules:
  0.0 236.9 jit_solution(17960086821000875730)
XLA Ops:
  7.2 1.1 copy.34
  8.3 0.8 compare_select_fusion
  9.1 1.1 copy.32
  10.1 0.8 compare_select_fusion.2
  10.9 1.8 copy.33
  12.8 1.0 gather_fusion.2
  13.7 1.0 gather_fusion.3
  14.7 1.8 gather_fusion
  16.5 1.0 gather_fusion.1
  17.4 1.2 multiply_reduce_fusion.3
  20.8 1.0 multiply_reduce_fusion.6
  22.3 3.1 %collective-permute-start = (f32[128,400]{0,1:T(8,128)S(1)}, f32[128,400]{0,1:T(8,128)S(1)}, u32[]{:S(2)}, u32[]{:S(2)}) collective-permute-start(f32[128,400]{0,1:T(8,128)S(1)} %divide_subtract_fusion.4), channel_id=1, source_target_pairs={{12,0},{0,4},{4,8},{8,12},{13,1},{1,5},{5,9},{9,13},{14,2},{2,6},{... | collective-permute-start | bytes 614408 | tf_op jit(solution)/shard_map/ppermute | solution.py:13
  25.4 1.8 fusion.16
  27.3 1.8 collective-permute-start.1
  29.9 1.8 gather_fusion.4
  31.7 0.8 collective-permute-done
  32.7 1.0 gather_fusion.6
  33.6 1.8 gather_fusion.7
  35.4 85.7 %all-reduce.3.cloned.1.call-done = f32[768,400]{0,1:T(8,128)} async-done(((f32[768,400]{0,1:T(8,128)}), f32[768,400]{0,1:T(8,128)}) %all-reduce.3.cloned.1.call-update) | async-done | bytes 1228816 | tf_op jit(solution)/shard_map/psum | solution.py:76
  121.1 1.4 multiply_reduce_fusion.1
  122.5 1.4 divide_subtract_fusion.1
  124.4 1.8 gather_fusion.5
  126.2 1.4 multiply_reduce_fusion.2
  129.7 0.8 copy-done.5
  131.7 1.8 fusion.17
  133.5 1.0 multiply_reduce_fusion.4
  134.5 1.2 fusion.37
  135.7 0.7 divide_subtract_fusion.3
  136.4 0.7 divide_subtract_fusion.2
  137.1 89.7 %all-reduce.5.cloned.1.call-done = f32[768,400]{0,1:T(8,128)} async-done(((f32[768,400]{0,1:T(8,128)}), f32[768,400]{0,1:T(8,128)}) %all-reduce.5.cloned.1.call-update) | async-done | bytes 1228816 | tf_op jit(solution)/shard_map/psum | solution.py:76
  226.8 1.5 multiply_reduce_fusion
  228.9 1.2 divide_subtract_fusion
  (81 shorter events, 7.9 us)
Async XLA Ops:
  7.2 113.9 %all-reduce.3.cloned.1.call-start = ((), (), s32[]{:S(2)}) async-start(), calls=%async_computation | async-start | bytes 2457600 | tf_op jit(solution)/shard_map/psum | solution.py:76
  10.9 1.8 copy-start.13
  10.9 1.8 copy-start.11
  19.3 1.2 copy-start.12
  20.7 1.0 copy-start.19
  20.7 1.6 copy-start.6
  20.8 4.7 %copy-start.4 = (f32[256,400]{1,0:T(8,128)S(1)}, f32[256,400]{1,0:T(8,128)}, u32[]{:S(2)}) copy-start(f32[256,400]{1,0:T(8,128)} %gather_fusion) | copy-start | bytes 1228804
  22.3 10.2 %collective-permute-start = (f32[128,400]{0,1:T(8,128)S(1)}, f32[128,400]{0,1:T(8,128)S(1)}, u32[]{:S(2)}, u32[]{:S(2)}) collective-permute-start(f32[128,400]{0,1:T(8,128)S(1)} %divide_subtract_fusion.4), channel_id=1, source_target_pairs={{12,0},{0,4},{4,8},{8,12},{13,1},{1,5},{5,9},{9,13},{14,2},{2,6},{... | collective-permute-start | bytes 614408 | tf_op jit(solution)/shard_map/ppermute | solution.py:13
  25.4 3.7 %copy-start.14 = (s32[2,256]{1,0:T(2,128)S(1)}, s32[2,256]{1,0:T(2,128)}, u32[]{:S(2)}) copy-start(s32[2,256]{1,0:T(2,128)} %param.16) | copy-start | bytes 6148
  27.2 2.5 %copy-start.17 = (f32[128]{0:T(128)S(1)}, f32[128]{0:T(128)}, u32[]{:S(2)}) copy-start(f32[128]{0:T(128)} %param.11) | copy-start | bytes 1540
  27.2 2.5 %copy-start.7 = (f32[128,400]{0,1:T(8,128)S(1)}, f32[128,400]{0,1:T(8,128)}, u32[]{:S(2)}) copy-start(f32[128,400]{0,1:T(8,128)} %param.10) | copy-start | bytes 614404
  27.2 199.6 %all-reduce.5.cloned.1.call-start = ((), (), s32[]{:S(2)}) async-start(), calls=%async_computation.1 | async-start | bytes 2457600 | tf_op jit(solution)/shard_map/psum | solution.py:76
  27.3 107.2 %collective-permute-start.1 = (f32[128]{0:T(128)}, f32[128]{0:T(128)}, u32[]{:S(2)}, u32[]{:S(2)}) collective-permute-start(f32[128]{0:T(128)} %get-tuple-element.15), channel_id=1, source_target_pairs={{12,0},{0,4},{4,8},{8,12},{13,1},{1,5},{5,9},{9,13},{14,2},{2,6},{... | collective-permute-start | bytes 1544 | tf_op jit(solution)/shard_map/ppermute | solution.py:13
  29.7 2.0 copy-start.15
  32.5 1.1 copy-start.8
  35.4 87.1 %copy-start.10 = (f32[768]{0:T(1024)S(1)}, f32[768]{0:T(1024)}, u32[]{:S(2)}) copy-start(f32[768]{0:T(1024)} %param.15) | copy-start | bytes 9220
  35.4 87.1 %copy-start = (f32[768,400]{0,1:T(8,128)S(1)}, f32[768,400]{0,1:T(8,128)}, u32[]{:S(2)}) copy-start(f32[768,400]{0,1:T(8,128)} %param.14) | copy-start | bytes 3686404
  126.2 1.4 copy-start.2
  129.5 1.0 copy-start.5
  129.7 1.5 copy-start.16
  129.7 1.4 copy-start.18
  129.7 2.0 copy-start.3
  133.5 2.9 %copy-start.9 = (f32[128,400]{0,1:T(8,128)S(1)}, f32[128,400]{0,1:T(8,128)}, u32[]{:S(2)}) copy-start(f32[128,400]{0,1:T(8,128)} %copy-done.8) | copy-start | bytes 614404
  226.8 2.1 copy-start.1
Sparse Core Ops, SparseCore 0:
  27.4 93.6 all-reduce.2
  133.6 93.1 all-reduce.4
where the time goes:
time: 237 us
  waiting for transfers between devices  176 us (74%)
  local copies, waits for them, and re-layouts  16.5 us (7%)
  between operations  14.5 us (6%)
  other arithmetic  14.4 us (6%)
  matrix products  10.4 us (4%)
  starting transfers between devices  4.96 us (2%)
    psum x2, waiting for transfers between devices, shards(): summed = lax.psum(grad_rel, ('blk', 'shard', 'sub'))  175 us
    dot_general x6, matrix products, row_sums(): jnp.dot(selector, values, precision=HIGH, preferred_element_type=jnp.floa...  6.72 us
    ppermute x2, starting transfers between devices, from_behind(): return lax.ppermute(block, axis, route)  4.88 us
    unnamed x43, local copies, waits for them, and re-layouts  4.82 us
  transfers between devices with their start and end apart: 4, of which 3 were waited for; matrix products, arithmetic and copies ran while one was open for 9% of the time, Pallas kernels for 0%

commit v1 on v0

v1 whole, which is shorter than its diff:
```python
import functools

import jax
import jax.numpy as jnp
from jax import lax
from jax.experimental import pallas as pl
from jax.experimental.pallas import tpu as pltpu
from jax.sharding import PartitionSpec as P

RATE = 0.1
AXES = ("blk", "shard", "sub")
LANES = 128
PIECES = 8
F32 = jnp.float32
BF16 = jnp.bfloat16


def halves(x):
    high = x.astype(BF16)
    return high, (x - high.astype(F32)).astype(BF16)


def nn(a, b):
    return lax.dot_general(a, b, (((1,), (0,)), ((), ())), preferred_element_type=F32)


def nt(a, b):
    return lax.dot_general(a, b, (((1,), (1,)), ((), ())), preferred_element_type=F32)


def times_selector(dot, x, selector):
    high, low = halves(x)
    rows = x.shape[0]
    both = dot(jnp.concatenate([high, low], axis=0), selector)
    return both[:rows] + both[rows:]


def times(dot, a, b):
    a_high, a_low = halves(a)
    b_high, b_low = halves(b)
    rows = a.shape[0]
    both = dot(jnp.concatenate([a_high, a_low], axis=0), b_high)
    return both[:rows] + (both[rows:] + dot(a_high, b_low))


def selector(ids, rows):
    return (lax.broadcasted_iota(jnp.int32, (rows, ids.shape[1]), 0) == ids).astype(F32)


def adagrad(weights, accum, grads):
    accum = accum + jnp.sum(grads * grads, axis=0, keepdims=True) * (1.0 / grads.shape[0])
    return weights - grads * (RATE / jnp.sqrt(accum)), accum


def bucket(left, right, rel, head_ids, tail_ids, kinds, negative):
    rows = left.shape[1]
    edges = head_ids.shape[1]
    count, negs = negative.shape
    head_sel = selector(head_ids, rows)
    tail_sel = selector(tail_ids, rows)
    kind_sel = selector(kinds, rel.shape[1]).astype(BF16)
    heads = times_selector(nn, left, head_sel.astype(BF16))
    rel_rows = times_selector(nn, rel, kind_sel)
    query = heads * rel_rows
    scores = times(nn, right.T, query)
    tiny = jnp.exp(-jnp.abs(scores))
    inverse = 1.0 / (1.0 + tiny)
    up = scores >= 0
    sig = jnp.where(up, 1.0, tiny) * inverse
    sig_minus = jnp.where(up, tiny, 1.0) * inverse
    named = []
    for c in range(count):
        hits = lax.broadcasted_iota(jnp.int32, (rows, negs), 0) == negative[c : c + 1]
        times_named = jnp.sum(hits.astype(F32), axis=1, keepdims=True) * (1.0 / negs)
        named.append(jnp.broadcast_to(times_named, (rows, edges // count)))
    weight = jnp.concatenate(named, axis=1) * sig - tail_sel * sig_minus
    grad_query = times(nn, right, weight)
    grad_right = times(nt, query, weight)
    grad_left = times_selector(nt, grad_query * rel_rows, head_sel.astype(BF16))
    return grad_left, grad_right, grad_query * heads, kind_sel


def put_rel_grad(terms, kind_sel, out_ref):
    width = terms.shape[0]
    grad = times_selector(nt, terms, kind_sel)
    blocks = grad.shape[1] // LANES
    for j in range(blocks):
        out_ref[width * j : width * (j + 1), :] = grad[:, LANES * j : LANES * (j + 1)]
    rest = out_ref.shape[0] - width * blocks
    if rest:
        out_ref[width * blocks :, :] = jnp.zeros((rest, LANES), F32)


def take_rel_grad(place_ref, mine_ref, other_ref, all_ref, width, blocks):
    square, core = place_ref[0], place_ref[1]
    for i in range(PIECES // 2):
        piece = jnp.bitwise_xor(square, i)
        all_ref[core * (PIECES // 2) + piece] = mine_ref[i]
        all_ref[(1 - core) * (PIECES // 2) + piece] = other_ref[i]
    flat = all_ref[...].reshape(-1, LANES)
    return jnp.concatenate([flat[width * j : width * (j + 1)] for j in range(blocks)], axis=1)


def first_kernel(
    left_ref, lacc_ref, right_ref, racc_ref, rel_ref, hid_ref, tid_ref, kid_ref, nid_ref,
    left_out, lacc_out, right_out, grad_out,
):
    left, right = left_ref[...], right_ref[...]
    width = left.shape[0]
    grad_left, grad_right, terms, kind_sel = bucket(
        left, right, rel_ref[...], hid_ref[0:1], tid_ref[0:1], kid_ref[0:1], nid_ref[0]
    )
    put_rel_grad(terms, kind_sel, grad_out)
    left_out[...], lacc_out[...] = adagrad(left, lacc_ref[...], grad_left)
    right, acc = adagrad(right, racc_ref[...], grad_right)
    right_out[:width] = right
    right_out[width:] = jnp.broadcast_to(acc, (8, acc.shape[1]))


def next_kernel(
    step,
    place_ref, left_ref, lacc_ref, right_ref, rel_ref, relacc_ref, mine_ref, other_ref,
    hid_ref, tid_ref, kid_ref, nid_ref,
    left_out, lacc_out, right_out, rel_out, relacc_out, grad_out,
    all_ref,
):
    left = left_ref[...]
    width = left.shape[0]
    rel = rel_ref[...]
    summed = take_rel_grad(place_ref, mine_ref, other_ref, all_ref, width, rel.shape[1] // LANES)
    rel, relacc = adagrad(rel, relacc_ref[...], summed)
    rel_out[...] = rel
    relacc_out[...] = relacc
    right = right_ref[:width]
    grad_left, grad_right, terms, kind_sel = bucket(
        left, right, rel,
        hid_ref[step : step + 1], tid_ref[step : step + 1], kid_ref[step : step + 1], nid_ref[step],
    )
    put_rel_grad(terms, kind_sel, grad_out)
    left_out[...], lacc_out[...] = adagrad(left, lacc_ref[...], grad_left)
    right, acc = adagrad(right, right_ref[width : width + 1], grad_right)
    right_out[:width] = right
    right_out[width:] = jnp.broadcast_to(acc, (8, acc.shape[1]))


def last_kernel(place_ref, rel_ref, relacc_ref, mine_ref, other_ref, rel_out, relacc_out, all_ref):
    rel = rel_ref[...]
    summed = take_rel_grad(place_ref, mine_ref, other_ref, all_ref, rel.shape[0], rel.shape[1] // LANES)
    rel_out[...], relacc_out[...] = adagrad(rel, relacc_ref[...], summed)


VMEM = pl.BlockSpec(memory_space=pltpu.VMEM)
SMEM = pl.BlockSpec(memory_space=pltpu.SMEM)
PARAMS = pltpu.CompilerParams(vmem_limit_bytes=40 * 1024 * 1024)


def call(kernel, outs, placed, scratch=()):
    return pl.pallas_call(
        kernel,
        out_shape=[jax.ShapeDtypeStruct(shape, F32) for shape in outs],
        in_specs=[SMEM] * placed[0] + [VMEM] * placed[1],
        out_specs=[VMEM] * len(outs),
        scratch_shapes=[pltpu.VMEM(shape, F32) for shape in scratch],
        compiler_params=PARAMS,
    )


def swap(x, sizes, blk=0, shard=0, sub=0):
    n_blk, n_shard, n_sub = sizes

    def number(b, k, u):
        return (b * n_shard + k) * n_sub + u

    route = [
        (number(b, k, u), number(b ^ blk, k ^ shard, u ^ sub))
        for b in range(n_blk)
        for k in range(n_shard)
        for u in range(n_sub)
    ]
    return lax.ppermute(x, AXES, route)


def gray(i):
    return jnp.bitwise_and(jnp.bitwise_xor(i, i >> 1), 1)


def sum_pieces(grad, sizes, square, core):
    half = PIECES // 2
    pieces = grad.reshape(2, half, -1, LANES)
    kept = lax.dynamic_index_in_dim(pieces, core, 0, keepdims=False)
    sent = lax.dynamic_index_in_dim(pieces, 1 - core, 0, keepdims=False)
    kept = kept + swap(sent, sizes, sub=1)

    def piece(i):
        return lax.dynamic_index_in_dim(kept, jnp.bitwise_xor(square, i), 0, keepdims=False)

    total = piece(0)
    for i in range(1, half):
        total = total + swap(piece(i), sizes, blk=i & 1, shard=i >> 1)
    reach = 4
    while reach <= sizes[0]:
        total = total + swap(total, sizes, blk=reach - 1)
        reach *= 2
    reach = 4
    while reach <= sizes[1]:
        total = total + swap(total, sizes, shard=reach - 1)
        reach *= 2
    mine = jnp.stack([total] + [swap(total, sizes, blk=i & 1, shard=i >> 1) for i in range(1, half)])
    return mine, swap(mine, sizes, sub=1)


def from_behind(block, axis):
    n = lax.axis_size(axis)
    return lax.ppermute(block, axis, [((i - 1) % n, i) for i in range(n)])


def shards(
    head_table, head_accum, tail_table, tail_accum, relations, rel_accum, head_ids, tail_ids, rel_ids, neg_ids
):
    sizes = tuple(lax.axis_size(a) for a in AXES)
    steps = head_ids.shape[0]
    rows, width = head_table.shape
    kinds = relations.shape[0]
    core = lax.axis_index("sub")
    square = gray(lax.axis_index("shard")) * 2 + gray(lax.axis_index("blk"))
    place = jnp.stack([square, core]).astype(jnp.int32)
    tile = 8 * PIECES
    grad_rows = -(-(width * kinds // LANES) // tile) * tile
    pieces = (PIECES, grad_rows // PIECES, LANES)

    left, lacc = head_table.T, head_accum[None]
    rel, relacc = relations.T, rel_accum[None]
    ids = (head_ids, tail_ids, rel_ids, neg_ids)
    step_outs = [(width, rows), (1, rows), (width + 8, rows)]
    rel_outs = [(width, kinds), (1, kinds)]
    left, lacc, right, grad = call(first_kernel, step_outs + [(grad_rows, LANES)], (0, 9))(
        left, lacc, tail_table.T, tail_accum[None], rel, *ids
    )
    for step in range(1, steps):
        right = from_behind(right, "blk")
        mine, other = sum_pieces(grad, sizes, square, core)
        left, lacc, right, rel, relacc, grad = call(
            functools.partial(next_kernel, step), step_outs + rel_outs + [(grad_rows, LANES)], (1, 11), [pieces]
        )(place, left, lacc, right, rel, relacc, mine, other, *ids)
    mine, other = sum_pieces(grad, sizes, square, core)
    rel, relacc = call(last_kernel, rel_outs, (1, 4), [pieces])(place, rel, relacc, mine, other)
    return (left.T, lacc[0], right[:width].T, right[width], rel.T, relacc[0])


def solution(mesh):
    every = ("groups", "blk", "shard", "sub")
    return jax.shard_map(
        shards,
        mesh=mesh,
        in_specs=(
            P(every, None),
            P(every),
            P(every, None),
            P(every),
            P("groups", None),
            P("groups"),
            P(None, every),
            P(None, every),
            P(None, every),
            P(None, every, None),
        ),
        out_specs=(P(every, None), P(every), P(every, None), P(every), P("groups", None), P("groups")),
        check_vma=False,
    )
```

time: 237 us -> 90.3 us (0.38)
  waiting for transfers between devices: 176 us -> 49.8 us
  starting transfers between devices: 4.96 us -> 22.1 us
  between operations: 14.5 us -> 0.81 us
  other arithmetic: 14.4 us -> 1.06 us
  matrix products: 10.4 us -> 0 us
  local copies, waits for them, and re-layouts: 16.5 us -> 8.59 us
  Pallas kernels: 0 us -> 7.69 us
    psum x2 -> x0, waiting for transfers between devices: 175 us -> none  [shards(): summed = lax.psum(grad_rel, ('blk', 'shard', 'sub'))]
    ppermute x2 -> x19, waiting for transfers between devices: 0.79 us -> 49.8 us  [the longest x18 42.3 us: swap(): return lax.ppermute(x, AXES, route)]
    ppermute x2 -> x19, starting transfers between devices: 4.88 us -> 22.1 us  [the longest x18 20.3 us: swap(): return lax.ppermute(x, AXES, route)]
    gather x8 -> x0, local copies, waits for them, and re-layouts: 10.9 us -> none  [the longest x2 3.54 us: bucket_grads(): heads = left[left_ids]]
    dot_general x8 -> x0, matrix products: 8.03 us -> none  [the longest x6 6.72 us: row_sums(): jnp.dot(selector, values, precision=HIGH, preferred_element_type=jnp.floa...]
    pallas_call x0 -> x3, Pallas kernels: none -> 7.69 us  [the longest x1 3.36 us: shards(): call(functools.partial(next_kernel, step), step_outs + rel_outs + [(grad_...]
    reduce_sum x4 -> x0, other arithmetic: 5.51 us -> none  [the longest x2 2.91 us: adagrad(): accum = accum + jnp.mean(grads * grads, axis=-1)]
    sub x6 -> x0, other arithmetic: 4.13 us -> none  [adagrad(): return (weights - RATE * grads / jnp.sqrt(accum)[..., None], accum)]
  transfers between devices with their start and end apart: 4 -> 19, of which waited for: 3 -> 17; matrix products, arithmetic and copies ran while one was open for 9% -> 1% of each run, Pallas kernels for 0% -> 0%
where the time goes in v1:
time: 90.3 us; the launch traced here: 90 us
  waiting for transfers between devices  49.8 us (55%)
  starting transfers between devices  22.1 us (24%)
  local copies, waits for them, and re-layouts  8.59 us (10%)
  Pallas kernels  7.69 us (9%)
  other arithmetic  1.06 us (1%)
    ppermute x18, waiting for transfers between devices, swap(): return lax.ppermute(x, AXES, route)  42.3 us
    ppermute x18, starting transfers between devices, swap(): return lax.ppermute(x, AXES, route)  20.3 us
    ppermute x1, waiting for transfers between devices, from_behind(): return lax.ppermute(block, axis, [((i - 1) % n, i) for i in range(n)])  7.49 us
    unnamed x30, local copies, waits for them, and re-layouts  7.2 us
    pallas_call x1, Pallas kernels, shards(): call(functools.partial(next_kernel, step), step_outs + rel_outs + [(grad_...  3.36 us
    pallas_call x1, Pallas kernels, shards(): call(first_kernel, step_outs + [(grad_rows, LANES)], (0, 9))  2.36 us
    pallas_call x1, Pallas kernels, shards(): call(last_kernel, rel_outs, (1, 4), [pieces])  1.97 us
  transfers between devices with their start and end apart: 19, of which 17 were waited for; matrix products, arithmetic and copies ran while one was open for 1% of the time, Pallas kernels for 0%

profile of v1, /device:TPU:0, one launch (start us, length us, event | category | flops | bytes accessed | tf_op | source)
XLA Modules:
  0.0 90.0 jit_solution(4677065546640130595)
XLA Ops:
  0.6 1.3 %copy-done = f32[768,400]{0,1:T(8,128)S(1)} copy-done((f32[768,400]{0,1:T(8,128)S(1)}, f32[768,400]{0,1:T(8,128)}, u32[]{:S(2)}) %copy-start) | copy-done | bytes 1228824
  1.9 0.9 %copy-done.2 = f32[128,400]{0,1:T(8,128)S(1)} copy-done((f32[128,400]{0,1:T(8,128)S(1)}, f32[128,400]{0,1:T(8,128)}, u32[]{:S(2)}) %copy-start.2) | copy-done | bytes 204824
  2.9 0.9 %copy-done.3 = f32[128,400]{0,1:T(8,128)S(1)} copy-done((f32[128,400]{0,1:T(8,128)S(1)}, f32[128,400]{0,1:T(8,128)}, u32[]{:S(2)}) %copy-start.3) | copy-done | bytes 204824
  7.8 2.4 %shard_map.145 = (f32[400,128]{1,0:T(8,128)S(1)}, f32[1,128]{1,0:T(1,128)S(1)}, f32[408,128]{1,0:T(8,128)S(1)}, f32[2432,128]{1,0:T(8,128)S(1)}) custom-call(f32[400,128]{1,0:T(8,128)S(1)} %bitcast.62, f32[1,128]{1,0:T(1,128)S(1)} %bitcast.64, f32[400,128]{1,0:T(8,128)S(1)} %bitcast.63, f32[1,128]{1,0:T(1,128)S(1)} %bitcast.65, f32[400,768]{1,0:T(8,128)S(1)} %bitcast.56, ...), custom_call_target="tpu_custom_call" | custom-call | tf_op jit(solution)/shard_map/pallas_call | solution.py:236
  10.8 1.7 %collective-permute-done.1 = f32[4,304,128]{2,1,0:T(8,128)S(1)} collective-permute-done((f32[4,304,128]{2,1,0:T(8,128)S(1)}, f32[4,304,128]{2,1,0:T(8,128)S(1)}, u32[]{:S(2)}, u32[]{:S(2)}) %collective-permute-start.1) | collective-permute-done | bytes 622624 | tf_op jit(solution)/shard_map/ppermute | solution.py:180
  12.6 3.0 %collective-permute-start.2 = (f32[304,128]{1,0:T(8,128)S(1)}, f32[304,128]{1,0:T(8,128)S(1)}, u32[]{:S(2)}, u32[]{:S(2)}) collective-permute-start(f32[304,128]{1,0:T(8,128)S(1)} %get-tuple-element.33), channel_id=1, source_target_pairs={{0,4},{1,5},{2,6},{3,7},{4,0},{5,1},{6,2},{7,3},{8,12},{9,13},{10,... | collective-permute-start | bytes 466952 | tf_op jit(solution)/shard_map/ppermute | solution.py:180
  15.6 1.4 %collective-permute-start.4 = (f32[304,128]{1,0:T(8,128)S(1)}, f32[304,128]{1,0:T(8,128)S(1)}, u32[]{:S(2)}, u32[]{:S(2)}) collective-permute-start(f32[304,128]{1,0:T(8,128)S(1)} %get-tuple-element.34), channel_id=1, source_target_pairs={{0,6},{1,7},{2,4},{3,5},{4,2},{5,3},{6,0},{7,1},{8,14},{9,15},{10,... | collective-permute-start | bytes 466952 | tf_op jit(solution)/shard_map/ppermute | solution.py:180
  17.2 3.2 %collective-permute-done.2 = f32[304,128]{1,0:T(8,128)S(1)} collective-permute-done((f32[304,128]{1,0:T(8,128)S(1)}, f32[304,128]{1,0:T(8,128)S(1)}, u32[]{:S(2)}, u32[]{:S(2)}) %collective-permute-start.2) | collective-permute-done | bytes 155680 | tf_op jit(solution)/shard_map/ppermute | solution.py:180
  20.4 4.1 %collective-permute-done.4 = f32[304,128]{1,0:T(8,128)S(1)} collective-permute-done((f32[304,128]{1,0:T(8,128)S(1)}, f32[304,128]{1,0:T(8,128)S(1)}, u32[]{:S(2)}, u32[]{:S(2)}) %collective-permute-start.4) | collective-permute-done | bytes 155680 | tf_op jit(solution)/shard_map/ppermute | solution.py:180
  24.5 1.4 %collective-permute-done.3 = f32[304,128]{1,0:T(8,128)S(1)} collective-permute-done((f32[304,128]{1,0:T(8,128)S(1)}, f32[304,128]{1,0:T(8,128)S(1)}, u32[]{:S(2)}, u32[]{:S(2)}) %collective-permute-start.3) | collective-permute-done | bytes 155680 | tf_op jit(solution)/shard_map/ppermute | solution.py:180
  25.9 3.7 %collective-permute-start.5 = (f32[304,128]{1,0:T(8,128)S(1)}, f32[304,128]{1,0:T(8,128)S(1)}, u32[]{:S(2)}, u32[]{:S(2)}) collective-permute-start(f32[304,128]{1,0:T(8,128)S(1)} %fusion.3), channel_id=1, source_target_pairs={{0,12},{1,13},{2,14},{3,15},{4,8},{5,9},{6,10},{7,11},{8,4},{9,5},... | collective-permute-start | bytes 466952 | tf_op jit(solution)/shard_map/ppermute | solution.py:180
  29.5 3.5 %collective-permute-done.5 = f32[304,128]{1,0:T(8,128)S(1)} collective-permute-done((f32[304,128]{1,0:T(8,128)S(1)}, f32[304,128]{1,0:T(8,128)S(1)}, u32[]{:S(2)}, u32[]{:S(2)}) %collective-permute-start.5) | collective-permute-done | bytes 155680 | tf_op jit(solution)/shard_map/ppermute | solution.py:180
  33.0 2.6 %collective-permute-start.8 = (f32[304,128]{1,0:T(8,128)S(1)}, f32[304,128]{1,0:T(8,128)S(1)}, u32[]{:S(2)}, u32[]{:S(2)}) collective-permute-start(f32[304,128]{1,0:T(8,128)S(1)} %add.71), channel_id=1, source_target_pairs={{0,6},{1,7},{2,4},{3,5},{4,2},{5,3},{6,0},{7,1},{8,14},{9,15},{10,... | collective-permute-start | bytes 466952 | tf_op jit(solution)/shard_map/ppermute | solution.py:180
  35.6 1.5 %collective-permute-start.7 = (f32[304,128]{1,0:T(8,128)S(1)}, f32[304,128]{1,0:T(8,128)S(1)}, u32[]{:S(2)}, u32[]{:S(2)}) collective-permute-start(f32[304,128]{1,0:T(8,128)S(1)} %add.71), channel_id=1, source_target_pairs={{0,2},{1,3},{2,0},{3,1},{4,6},{5,7},{6,4},{7,5},{8,10},{9,11},{10,... | collective-permute-start | bytes 466952 | tf_op jit(solution)/shard_map/ppermute | solution.py:180
  37.1 3.2 %collective-permute-done.8 = f32[304,128]{1,0:T(8,128)S(1)} collective-permute-done((f32[304,128]{1,0:T(8,128)S(1)}, f32[304,128]{1,0:T(8,128)S(1)}, u32[]{:S(2)}, u32[]{:S(2)}) %collective-permute-start.8) | collective-permute-done | bytes 155680 | tf_op jit(solution)/shard_map/ppermute | solution.py:180
  40.3 2.0 %collective-permute-done.7 = f32[304,128]{1,0:T(8,128)S(1)} collective-permute-done((f32[304,128]{1,0:T(8,128)S(1)}, f32[304,128]{1,0:T(8,128)S(1)}, u32[]{:S(2)}, u32[]{:S(2)}) %collective-permute-start.7) | collective-permute-done | bytes 155680 | tf_op jit(solution)/shard_map/ppermute | solution.py:180
  42.5 1.8 %collective-permute-start = (f32[408,128]{1,0:T(8,128)S(1)}, f32[408,128]{1,0:T(8,128)S(1)}, u32[]{:S(2)}, u32[]{:S(2)}) collective-permute-start(f32[408,128]{1,0:T(8,128)S(1)} %get-tuple-element.20), channel_id=1, source_target_pairs={{12,0},{0,4},{4,8},{8,12},{13,1},{1,5},{5,9},{9,13},{14,2},{2,6},{... | collective-permute-start | bytes 626696 | tf_op jit(solution)/shard_map/ppermute | solution.py:214
  44.4 7.5 %collective-permute-done.right_ref = f32[408,128]{1,0:T(8,128)S(1)} collective-permute-done((f32[408,128]{1,0:T(8,128)S(1)}, f32[408,128]{1,0:T(8,128)S(1)}, u32[]{:S(2)}, u32[]{:S(2)}) %collective-permute-start) | collective-permute-done | bytes 208928 | tf_op jit(solution)/shard_map/ppermute | solution.py:214
  51.9 3.4 %shard_map.146 = (f32[400,128]{1,0:T(8,128)}, f32[1,128]{1,0:T(1,128)}, f32[408,128]{1,0:T(8,128)S(1)}, f32[400,768]{1,0:T(8,128)S(1)}, f32[1,768]{1,0:T(1,128)S(1)}, /*index=5*/f32[2432,128]{1,0:T(8,128)S(1)}) custom-call(s32[2]{0:T(128)S(1)} %pad_add_fusion.place_ref, f32[400,128]{1,0:T(8,128)S(1)} %get-tuple-element.18.left_ref, ...), custom_call_target="tpu_custom_call" | custom-call | tf_op jit(solution)/shard_map/pallas_call | solution.py:242
  55.4 2.0 %collective-permute-done.10 = f32[4,304,128]{2,1,0:T(8,128)S(1)} collective-permute-done((f32[4,304,128]{2,1,0:T(8,128)S(1)}, f32[4,304,128]{2,1,0:T(8,128)S(1)}, u32[]{:S(2)}, u32[]{:S(2)}) %collective-permute-start.10) | collective-permute-done | bytes 622624 | tf_op jit(solution)/shard_map/ppermute | solution.py:180
  57.6 2.8 %collective-permute-start.13 = (f32[304,128]{1,0:T(8,128)S(1)}, f32[304,128]{1,0:T(8,128)S(1)}, u32[]{:S(2)}, u32[]{:S(2)}) collective-permute-start(f32[304,128]{1,0:T(8,128)S(1)} %get-tuple-element.31), channel_id=1, source_target_pairs={{0,6},{1,7},{2,4},{3,5},{4,2},{5,3},{6,0},{7,1},{8,14},{9,15},{10,... | collective-permute-start | bytes 466952 | tf_op jit(solution)/shard_map/ppermute | solution.py:180
  61.1 3.4 %collective-permute-done.11 = f32[304,128]{1,0:T(8,128)S(1)} collective-permute-done((f32[304,128]{1,0:T(8,128)S(1)}, f32[304,128]{1,0:T(8,128)S(1)}, u32[]{:S(2)}, u32[]{:S(2)}) %collective-permute-start.11) | collective-permute-done | bytes 155680 | tf_op jit(solution)/shard_map/ppermute | solution.py:180
  64.5 3.5 %collective-permute-done.13 = f32[304,128]{1,0:T(8,128)S(1)} collective-permute-done((f32[304,128]{1,0:T(8,128)S(1)}, f32[304,128]{1,0:T(8,128)S(1)}, u32[]{:S(2)}, u32[]{:S(2)}) %collective-permute-start.13) | collective-permute-done | bytes 155680 | tf_op jit(solution)/shard_map/ppermute | solution.py:180
  67.9 1.4 %collective-permute-done.12 = f32[304,128]{1,0:T(8,128)S(1)} collective-permute-done((f32[304,128]{1,0:T(8,128)S(1)}, f32[304,128]{1,0:T(8,128)S(1)}, u32[]{:S(2)}, u32[]{:S(2)}) %collective-permute-start.12) | collective-permute-done | bytes 155680 | tf_op jit(solution)/shard_map/ppermute | solution.py:180
  69.5 8.0 %collective-permute-done.14 = f32[304,128]{1,0:T(8,128)S(1)} collective-permute-done((f32[304,128]{1,0:T(8,128)S(1)}, f32[304,128]{1,0:T(8,128)S(1)}, u32[]{:S(2)}, u32[]{:S(2)}) %collective-permute-start.14) | collective-permute-done | bytes 155680 | tf_op jit(solution)/shard_map/ppermute | solution.py:180
  77.5 0.9 collective-permute-start.17
  78.4 1.4 %collective-permute-start.16 = (f32[304,128]{1,0:T(8,128)S(1)}, f32[304,128]{1,0:T(8,128)S(1)}, u32[]{:S(2)}, u32[]{:S(2)}) collective-permute-start(f32[304,128]{1,0:T(8,128)S(1)} %add.76), channel_id=1, source_target_pairs={{0,2},{1,3},{2,0},{3,1},{4,6},{5,7},{6,4},{7,5},{8,10},{9,11},{10,... | collective-permute-start | bytes 466952 | tf_op jit(solution)/shard_map/ppermute | solution.py:180
  79.7 1.3 %collective-permute-start.15 = (f32[304,128]{1,0:T(8,128)S(1)}, f32[304,128]{1,0:T(8,128)S(1)}, u32[]{:S(2)}, u32[]{:S(2)}) collective-permute-start(f32[304,128]{1,0:T(8,128)S(1)} %add.76), channel_id=1, source_target_pairs={{0,4},{1,5},{2,6},{3,7},{4,0},{5,1},{6,2},{7,3},{8,12},{9,13},{10,... | collective-permute-start | bytes 466952 | tf_op jit(solution)/shard_map/ppermute | solution.py:180
  81.0 2.7 %collective-permute-done.17 = f32[304,128]{1,0:T(8,128)S(1)} collective-permute-done((f32[304,128]{1,0:T(8,128)S(1)}, f32[304,128]{1,0:T(8,128)S(1)}, u32[]{:S(2)}, u32[]{:S(2)}) %collective-permute-start.17) | collective-permute-done | bytes 155680 | tf_op jit(solution)/shard_map/ppermute | solution.py:180
  83.8 1.5 %collective-permute-done.16 = f32[304,128]{1,0:T(8,128)S(1)} collective-permute-done((f32[304,128]{1,0:T(8,128)S(1)}, f32[304,128]{1,0:T(8,128)S(1)}, u32[]{:S(2)}, u32[]{:S(2)}) %collective-permute-start.16) | collective-permute-done | bytes 155680 | tf_op jit(solution)/shard_map/ppermute | solution.py:180
  86.6 0.8 collective-permute-done.18.other_ref
  87.4 2.0 %shard_map.147 = (f32[400,768]{1,0:T(8,128)}, f32[1,768]{1,0:T(1,128)S(1)}) custom-call(s32[2]{0:T(128)S(1)} %pad_add_fusion.place_ref, f32[400,768]{1,0:T(8,128)S(1)} %get-tuple-element.25.rel_ref, f32[1,768]{1,0:T(1,128)S(1)} %get-tuple-element.26.relacc_ref, f32[4,304,128]{2,1,0:T(8,128)S(1)} %pad_maximum_fusion.1.mine_ref, ...), custom_call_target="tpu_custom_call" | custom-call | tf_op jit(solution)/shard_map/pallas_call | solution.py:246
  (56 shorter events, 8.4 us)
Async XLA Ops:
  0.6 1.3 %copy-start = (f32[768,400]{0,1:T(8,128)S(1)}, f32[768,400]{0,1:T(8,128)}, u32[]{:S(2)}) copy-start(f32[768,400]{0,1:T(8,128)} %param.14) | copy-start | bytes 3686404
  1.9 0.9 %copy-start.2 = (f32[128,400]{0,1:T(8,128)S(1)}, f32[128,400]{0,1:T(8,128)}, u32[]{:S(2)}) copy-start(f32[128,400]{0,1:T(8,128)} %param.10) | copy-start | bytes 614404
  2.9 0.9 %copy-start.3 = (f32[128,400]{0,1:T(8,128)S(1)}, f32[128,400]{0,1:T(8,128)}, u32[]{:S(2)}) copy-start(f32[128,400]{0,1:T(8,128)} %param.12) | copy-start | bytes 614404
  3.8 0.7 copy-start.4
  4.5 0.7 copy-start.6
  5.2 0.7 copy-start.8
  5.8 0.7 copy-start.10
  10.3 2.2 %collective-permute-start.1 = (f32[4,304,128]{2,1,0:T(8,128)S(1)}, f32[4,304,128]{2,1,0:T(8,128)S(1)}, u32[]{:S(2)}, u32[]{:S(2)}) collective-permute-start(f32[4,304,128]{2,1,0:T(8,128)S(1)} %dynamic-slice_bitcast_fusion.1), channel_id=1, source_target_pairs={{0,1},{1,0},{2,3},{3,2},{4,5},{5,4},{6,7},{7,6},{8,9},{9,8},{10,11... | collective-permute-start | bytes 1867784 | tf_op jit(solution)/shard_map/ppermute | solution.py:180
  12.6 7.8 %collective-permute-start.2 = (f32[304,128]{1,0:T(8,128)S(1)}, f32[304,128]{1,0:T(8,128)S(1)}, u32[]{:S(2)}, u32[]{:S(2)}) collective-permute-start(f32[304,128]{1,0:T(8,128)S(1)} %get-tuple-element.33), channel_id=1, source_target_pairs={{0,4},{1,5},{2,6},{3,7},{4,0},{5,1},{6,2},{7,3},{8,12},{9,13},{10,... | collective-permute-start | bytes 466952 | tf_op jit(solution)/shard_map/ppermute | solution.py:180
  15.6 8.9 %collective-permute-start.4 = (f32[304,128]{1,0:T(8,128)S(1)}, f32[304,128]{1,0:T(8,128)S(1)}, u32[]{:S(2)}, u32[]{:S(2)}) collective-permute-start(f32[304,128]{1,0:T(8,128)S(1)} %get-tuple-element.34), channel_id=1, source_target_pairs={{0,6},{1,7},{2,4},{3,5},{4,2},{5,3},{6,0},{7,1},{8,14},{9,15},{10,... | collective-permute-start | bytes 466952 | tf_op jit(solution)/shard_map/ppermute | solution.py:180
  17.0 8.8 %collective-permute-start.3 = (f32[304,128]{1,0:T(8,128)S(1)}, f32[304,128]{1,0:T(8,128)S(1)}, u32[]{:S(2)}, u32[]{:S(2)}) collective-permute-start(f32[304,128]{1,0:T(8,128)S(1)} %get-tuple-element.35), channel_id=1, source_target_pairs={{0,2},{1,3},{2,0},{3,1},{4,6},{5,7},{6,4},{7,5},{8,10},{9,11},{10,... | collective-permute-start | bytes 466952 | tf_op jit(solution)/shard_map/ppermute | solution.py:180
  17.1 27.1 %copy-start.14 = (f32[768]{0:T(1024)S(1)}, f32[768]{0:T(1024)}, u32[]{:S(2)}) copy-start(f32[768]{0:T(1024)} %param.15) | copy-start | bytes 9220
  17.1 34.7 %copy-start.1 = (f32[768,400]{0,1:T(8,128)S(1)}, f32[768,400]{0,1:T(8,128)}, u32[]{:S(2)}) copy-start(f32[768,400]{0,1:T(8,128)} %param.14) | copy-start | bytes 3686404
  17.1 34.7 %copy-start.5 = (s32[2,256]{1,0:T(2,128)S(1)}, s32[2,256]{1,0:T(2,128)}, u32[]{:S(2)}) copy-start(s32[2,256]{1,0:T(2,128)} %hid_ref.3) | copy-start | bytes 6148
  17.2 34.7 %copy-start.7 = (s32[2,256]{1,0:T(2,128)S(1)}, s32[2,256]{1,0:T(2,128)}, u32[]{:S(2)}) copy-start(s32[2,256]{1,0:T(2,128)} %tid_ref.3) | copy-start | bytes 6148
  17.2 34.7 %copy-start.9 = (s32[2,256]{1,0:T(2,128)S(1)}, s32[2,256]{1,0:T(2,128)}, u32[]{:S(2)}) copy-start(s32[2,256]{1,0:T(2,128)} %kid_ref.3) | copy-start | bytes 6148
  17.2 34.7 %copy-start.11 = (s32[2,2,128]{2,1,0:T(2,128)S(1)}, s32[2,2,128]{2,1,0:T(2,128)}, u32[]{:S(2)}) copy-start(s32[2,2,128]{2,1,0:T(2,128)} %nid_ref.3) | copy-start | bytes 6148
  25.9 7.2 %collective-permute-start.5 = (f32[304,128]{1,0:T(8,128)S(1)}, f32[304,128]{1,0:T(8,128)S(1)}, u32[]{:S(2)}, u32[]{:S(2)}) collective-permute-start(f32[304,128]{1,0:T(8,128)S(1)} %fusion.3), channel_id=1, source_target_pairs={{0,12},{1,13},{2,14},{3,15},{4,8},{5,9},{6,10},{7,11},{8,4},{9,5},... | collective-permute-start | bytes 466952 | tf_op jit(solution)/shard_map/ppermute | solution.py:180
  33.0 7.3 %collective-permute-start.8 = (f32[304,128]{1,0:T(8,128)S(1)}, f32[304,128]{1,0:T(8,128)S(1)}, u32[]{:S(2)}, u32[]{:S(2)}) collective-permute-start(f32[304,128]{1,0:T(8,128)S(1)} %add.71), channel_id=1, source_target_pairs={{0,6},{1,7},{2,4},{3,5},{4,2},{5,3},{6,0},{7,1},{8,14},{9,15},{10,... | collective-permute-start | bytes 466952 | tf_op jit(solution)/shard_map/ppermute | solution.py:180
  35.6 6.6 %collective-permute-start.7 = (f32[304,128]{1,0:T(8,128)S(1)}, f32[304,128]{1,0:T(8,128)S(1)}, u32[]{:S(2)}, u32[]{:S(2)}) collective-permute-start(f32[304,128]{1,0:T(8,128)S(1)} %add.71), channel_id=1, source_target_pairs={{0,2},{1,3},{2,0},{3,1},{4,6},{5,7},{6,4},{7,5},{8,10},{9,11},{10,... | collective-permute-start | bytes 466952 | tf_op jit(solution)/shard_map/ppermute | solution.py:180
  37.1 5.2 %collective-permute-start.6 = (f32[304,128]{1,0:T(8,128)S(1)}, f32[304,128]{1,0:T(8,128)S(1)}, u32[]{:S(2)}, u32[]{:S(2)}) collective-permute-start(f32[304,128]{1,0:T(8,128)S(1)} %add.71), channel_id=1, source_target_pairs={{0,4},{1,5},{2,6},{3,7},{4,0},{5,1},{6,2},{7,3},{8,12},{9,13},{10,... | collective-permute-start | bytes 466952 | tf_op jit(solution)/shard_map/ppermute | solution.py:180
  42.4 9.4 %collective-permute-start.9 = (f32[4,304,128]{2,1,0:T(8,128)S(1)}, f32[4,304,128]{2,1,0:T(8,128)S(1)}, u32[]{:S(2)}, u32[]{:S(2)}) collective-permute-start(f32[4,304,128]{2,1,0:T(8,128)S(1)} %pad_maximum_fusion.mine_ref), channel_id=1, source_target_pairs={{0,1},{1,0},{2,3},{3,2},{4,5},{5,4},{6,7},{7,6},{8,9},{9,8},{10,11... | collective-permute-start | bytes 1867784 | tf_op jit(solution)/shard_map/ppermute | solution.py:180
  42.5 9.4 %collective-permute-start = (f32[408,128]{1,0:T(8,128)S(1)}, f32[408,128]{1,0:T(8,128)S(1)}, u32[]{:S(2)}, u32[]{:S(2)}) collective-permute-start(f32[408,128]{1,0:T(8,128)S(1)} %get-tuple-element.20), channel_id=1, source_target_pairs={{12,0},{0,4},{4,8},{8,12},{13,1},{1,5},{5,9},{9,13},{14,2},{2,6},{... | collective-permute-start | bytes 626696 | tf_op jit(solution)/shard_map/ppermute | solution.py:214
  55.3 2.1 %collective-permute-start.10 = (f32[4,304,128]{2,1,0:T(8,128)S(1)}, f32[4,304,128]{2,1,0:T(8,128)S(1)}, u32[]{:S(2)}, u32[]{:S(2)}) collective-permute-start(f32[4,304,128]{2,1,0:T(8,128)S(1)} %dynamic-slice_bitcast_fusion), channel_id=1, source_target_pairs={{0,1},{1,0},{2,3},{3,2},{4,5},{5,4},{6,7},{7,6},{8,9},{9,8},{10,11... | collective-permute-start | bytes 1867784 | tf_op jit(solution)/shard_map/ppermute | solution.py:180
  57.5 6.9 %collective-permute-start.11 = (f32[304,128]{1,0:T(8,128)S(1)}, f32[304,128]{1,0:T(8,128)S(1)}, u32[]{:S(2)}, u32[]{:S(2)}) collective-permute-start(f32[304,128]{1,0:T(8,128)S(1)} %get-tuple-element.30), channel_id=1, source_target_pairs={{0,4},{1,5},{2,6},{3,7},{4,0},{5,1},{6,2},{7,3},{8,12},{9,13},{10,... | collective-permute-start | bytes 466952 | tf_op jit(solution)/shard_map/ppermute | solution.py:180
  57.6 10.3 %collective-permute-start.13 = (f32[304,128]{1,0:T(8,128)S(1)}, f32[304,128]{1,0:T(8,128)S(1)}, u32[]{:S(2)}, u32[]{:S(2)}) collective-permute-start(f32[304,128]{1,0:T(8,128)S(1)} %get-tuple-element.31), channel_id=1, source_target_pairs={{0,6},{1,7},{2,4},{3,5},{4,2},{5,3},{6,0},{7,1},{8,14},{9,15},{10,... | collective-permute-start | bytes 466952 | tf_op jit(solution)/shard_map/ppermute | solution.py:180
  60.4 8.8 %collective-permute-start.12 = (f32[304,128]{1,0:T(8,128)S(1)}, f32[304,128]{1,0:T(8,128)S(1)}, u32[]{:S(2)}, u32[]{:S(2)}) collective-permute-start(f32[304,128]{1,0:T(8,128)S(1)} %get-tuple-element.32), channel_id=1, source_target_pairs={{0,2},{1,3},{2,0},{3,1},{4,6},{5,7},{6,4},{7,5},{8,10},{9,11},{10,... | collective-permute-start | bytes 466952 | tf_op jit(solution)/shard_map/ppermute | solution.py:180
  69.3 8.1 %collective-permute-start.14 = (f32[304,128]{1,0:T(8,128)S(1)}, f32[304,128]{1,0:T(8,128)S(1)}, u32[]{:S(2)}, u32[]{:S(2)}) collective-permute-start(f32[304,128]{1,0:T(8,128)S(1)} %fusion.1), channel_id=1, source_target_pairs={{0,12},{1,13},{2,14},{3,15},{4,8},{5,9},{6,10},{7,11},{8,4},{9,5},... | collective-permute-start | bytes 466952 | tf_op jit(solution)/shard_map/ppermute | solution.py:180
  77.5 6.3 %collective-permute-start.17 = (f32[304,128]{1,0:T(8,128)S(1)}, f32[304,128]{1,0:T(8,128)S(1)}, u32[]{:S(2)}, u32[]{:S(2)}) collective-permute-start(f32[304,128]{1,0:T(8,128)S(1)} %add.76), channel_id=1, source_target_pairs={{0,6},{1,7},{2,4},{3,5},{4,2},{5,3},{6,0},{7,1},{8,14},{9,15},{10,... | collective-permute-start | bytes 466952 | tf_op jit(solution)/shard_map/ppermute | solution.py:180
  78.4 6.9 %collective-permute-start.16 = (f32[304,128]{1,0:T(8,128)S(1)}, f32[304,128]{1,0:T(8,128)S(1)}, u32[]{:S(2)}, u32[]{:S(2)}) collective-permute-start(f32[304,128]{1,0:T(8,128)S(1)} %add.76), channel_id=1, source_target_pairs={{0,2},{1,3},{2,0},{3,1},{4,6},{5,7},{6,4},{7,5},{8,10},{9,11},{10,... | collective-permute-start | bytes 466952 | tf_op jit(solution)/shard_map/ppermute | solution.py:180
  79.7 5.5 %collective-permute-start.15 = (f32[304,128]{1,0:T(8,128)S(1)}, f32[304,128]{1,0:T(8,128)S(1)}, u32[]{:S(2)}, u32[]{:S(2)}) collective-permute-start(f32[304,128]{1,0:T(8,128)S(1)} %add.76), channel_id=1, source_target_pairs={{0,4},{1,5},{2,6},{3,7},{4,0},{5,1},{6,2},{7,3},{8,12},{9,13},{10,... | collective-permute-start | bytes 466952 | tf_op jit(solution)/shard_map/ppermute | solution.py:180
  85.3 2.1 %collective-permute-start.18 = (f32[4,304,128]{2,1,0:T(8,128)S(1)}, f32[4,304,128]{2,1,0:T(8,128)S(1)}, u32[]{:S(2)}, u32[]{:S(2)}) collective-permute-start(f32[4,304,128]{2,1,0:T(8,128)S(1)} %pad_maximum_fusion.1.mine_ref), channel_id=1, source_target_pairs={{0,1},{1,0},{2,3},{3,2},{4,5},{5,4},{6,7},{7,6},{8,9},{9,8},{10,11... | collective-permute-start | bytes 1867784 | tf_op jit(solution)/shard_map/ppermute | solution.py:180
  (2 other events, 1.3 us)

commit v2 on v1

--- a/solution.py
+++ b/solution.py
@@ -91,43 +91,47 @@
         out_ref[width * blocks :, :] = jnp.zeros((rest, LANES), F32)
 
 
-def take_rel_grad(place_ref, mine_ref, other_ref, all_ref, width, blocks):
+def take_rel_grad(place_ref, piece_refs, all_ref, width, blocks):
     square, core = place_ref[0], place_ref[1]
-    for i in range(PIECES // 2):
+    half = PIECES // 2
+    for i in range(half):
         piece = jnp.bitwise_xor(square, i)
-        all_ref[core * (PIECES // 2) + piece] = mine_ref[i]
-        all_ref[(1 - core) * (PIECES // 2) + piece] = other_ref[i]
+        all_ref[core * half + piece] = piece_refs[i][...]
+        all_ref[(1 - core) * half + piece] = piece_refs[half + i][...]
     flat = all_ref[...].reshape(-1, LANES)
     return jnp.concatenate([flat[width * j : width * (j + 1)] for j in range(blocks)], axis=1)
 
 
-def first_kernel(
-    left_ref, lacc_ref, right_ref, racc_ref, rel_ref, hid_ref, tid_ref, kid_ref, nid_ref,
-    left_out, lacc_out, right_out, grad_out,
-):
+def put_packed(out_ref, right, acc):
+    width = right.shape[0]
+    out_ref[:width] = right
+    out_ref[width:] = jnp.broadcast_to(acc, (8, acc.shape[1]))
+
+
+def first_kernel(*refs):
+    given, (left_out, lacc_out, right_out, grad_out), held, sems = refs[:9], refs[9:13], refs[13:22], refs[22]
+    copies = [pltpu.make_async_copy(a, b, sems.at[i]) for i, (a, b) in enumerate(zip(given, held))]
+    for copy in copies:
+        copy.start()
+    for copy in copies:
+        copy.wait()
+    left_ref, lacc_ref, right_ref, racc_ref, rel_ref, hid_ref, tid_ref, kid_ref, nid_ref = held
     left, right = left_ref[...], right_ref[...]
-    width = left.shape[0]
     grad_left, grad_right, terms, kind_sel = bucket(
         left, right, rel_ref[...], hid_ref[0:1], tid_ref[0:1], kid_ref[0:1], nid_ref[0]
     )
     put_rel_grad(terms, kind_sel, grad_out)
     left_out[...], lacc_out[...] = adagrad(left, lacc_ref[...], grad_left)
-    right, acc = adagrad(right, racc_ref[...], grad_right)
-    right_out[:width] = right
-    right_out[width:] = jnp.broadcast_to(acc, (8, acc.shape[1]))
-
-
-def next_kernel(
-    step,
-    place_ref, left_ref, lacc_ref, right_ref, rel_ref, relacc_ref, mine_ref, other_ref,
-    hid_ref, tid_ref, kid_ref, nid_ref,
-    left_out, lacc_out, right_out, rel_out, relacc_out, grad_out,
-    all_ref,
-):
+    put_packed(right_out, *adagrad(right, racc_ref[...], grad_right))
+
+
+def next_kernel(step, last, place_ref, left_ref, lacc_ref, right_ref, rel_ref, relacc_ref, *refs):
+    piece_refs, (hid_ref, tid_ref, kid_ref, nid_ref) = refs[:PIECES], refs[PIECES : PIECES + 4]
+    left_out, lacc_out, right_out, *racc_out, rel_out, relacc_out, grad_out, all_ref = refs[PIECES + 4 :]
     left = left_ref[...]
     width = left.shape[0]
     rel = rel_ref[...]
-    summed = take_rel_grad(place_ref, mine_ref, other_ref, all_ref, width, rel.shape[1] // LANES)
+    summed = take_rel_grad(place_ref, piece_refs, all_ref, width, rel.shape[1] // LANES)
     rel, relacc = adagrad(rel, relacc_ref[...], summed)
     rel_out[...] = rel
     relacc_out[...] = relacc
@@ -137,18 +141,25 @@
         hid_ref[step : step + 1], tid_ref[step : step + 1], kid_ref[step : step + 1], nid_ref[step],
     )
     put_rel_grad(terms, kind_sel, grad_out)
-    left_out[...], lacc_out[...] = adagrad(left, lacc_ref[...], grad_left)
-    right, acc = adagrad(right, right_ref[width : width + 1], grad_right)
-    right_out[:width] = right
-    right_out[width:] = jnp.broadcast_to(acc, (8, acc.shape[1]))
-
-
-def last_kernel(place_ref, rel_ref, relacc_ref, mine_ref, other_ref, rel_out, relacc_out, all_ref):
+    left_out[...], lacc = adagrad(left, lacc_ref[...], grad_left)
+    right, racc = adagrad(right, right_ref[width : width + 1], grad_right)
+    if last:
+        right_out[...] = right
+        lacc_out[...], racc_out[0][...] = lacc[0], racc[0]
+    else:
+        lacc_out[...] = lacc
+        put_packed(right_out, right, racc)
+
+
+def last_kernel(place_ref, rel_ref, relacc_ref, *refs):
+    piece_refs, (rel_out, relacc_out, all_ref) = refs[:PIECES], refs[PIECES:]
     rel = rel_ref[...]
-    summed = take_rel_grad(place_ref, mine_ref, other_ref, all_ref, rel.shape[0], rel.shape[1] // LANES)
-    rel_out[...], relacc_out[...] = adagrad(rel, relacc_ref[...], summed)
-
-
+    summed = take_rel_grad(place_ref, piece_refs, all_ref, rel.shape[0], rel.shape[1] // LANES)
+    rel_out[...], acc = adagrad(rel, relacc_ref[...], summed)
+    relacc_out[...] = acc[0]
+
+
+HBM = pl.BlockSpec(memory_space=pltpu.HBM)
 VMEM = pl.BlockSpec(memory_space=pltpu.VMEM)
 SMEM = pl.BlockSpec(memory_space=pltpu.SMEM)
 PARAMS = pltpu.CompilerParams(vmem_limit_bytes=40 * 1024 * 1024)
@@ -184,7 +195,7 @@
     return jnp.bitwise_and(jnp.bitwise_xor(i, i >> 1), 1)
 
 
-def sum_pieces(grad, sizes, square, core):
+def sum_pieces(grad, sizes, square, core, beside=()):
     half = PIECES // 2
     pieces = grad.reshape(2, half, -1, LANES)
     kept = lax.dynamic_index_in_dim(pieces, core, 0, keepdims=False)
@@ -195,8 +206,9 @@
         return lax.dynamic_index_in_dim(kept, jnp.bitwise_xor(square, i), 0, keepdims=False)
 
     total = piece(0)
-    for i in range(1, half):
-        total = total + swap(piece(i), sizes, blk=i & 1, shard=i >> 1)
+    got = [swap(piece(i), sizes, blk=i & 1, shard=i >> 1) for i in range(1, half)]
+    got[1], beside = lax.optimization_barrier((got[1], beside))
+    total = total + got[0] + got[1] + got[2]
     reach = 4
     while reach <= sizes[0]:
         total = total + swap(total, sizes, blk=reach - 1)
@@ -205,8 +217,8 @@
     while reach <= sizes[1]:
         total = total + swap(total, sizes, shard=reach - 1)
         reach *= 2
-    mine = jnp.stack([total] + [swap(total, sizes, blk=i & 1, shard=i >> 1) for i in range(1, half)])
-    return mine, swap(mine, sizes, sub=1)
+    mine = [total] + [swap(total, sizes, blk=i & 1, shard=i >> 1) for i in range(1, half)]
+    return mine + [swap(x, sizes, sub=1) for x in mine], beside
 
 
 def from_behind(block, axis):
@@ -231,20 +243,28 @@
     left, lacc = head_table.T, head_accum[None]
     rel, relacc = relations.T, rel_accum[None]
     ids = (head_ids, tail_ids, rel_ids, neg_ids)
+    given = (left, lacc, tail_table.T, tail_accum[None], rel, *ids)
     step_outs = [(width, rows), (1, rows), (width + 8, rows)]
-    rel_outs = [(width, kinds), (1, kinds)]
-    left, lacc, right, grad = call(first_kernel, step_outs + [(grad_rows, LANES)], (0, 9))(
-        left, lacc, tail_table.T, tail_accum[None], rel, *ids
-    )
+    last_outs = [(width, rows), (rows,), (width, rows), (rows,)]
+    left, lacc, right, grad = pl.pallas_call(
+        first_kernel,
+        out_shape=[jax.ShapeDtypeStruct(shape, F32) for shape in step_outs + [(grad_rows, LANES)]],
+        in_specs=[HBM] * len(given),
+        out_specs=[VMEM] * 4,
+        scratch_shapes=[pltpu.VMEM(x.shape, x.dtype) for x in given] + [pltpu.SemaphoreType.DMA((len(given),))],
+        compiler_params=PARAMS,
+    )(*[pltpu.with_memory_space_constraint(x, pltpu.HBM) for x in given])
     for step in range(1, steps):
+        last = step + 1 == steps
         right = from_behind(right, "blk")
-        mine, other = sum_pieces(grad, sizes, square, core)
-        left, lacc, right, rel, relacc, grad = call(
-            functools.partial(next_kernel, step), step_outs + rel_outs + [(grad_rows, LANES)], (1, 11), [pieces]
-        )(place, left, lacc, right, rel, relacc, mine, other, *ids)
-    mine, other = sum_pieces(grad, sizes, square, core)
-    rel, relacc = call(last_kernel, rel_outs, (1, 4), [pieces])(place, rel, relacc, mine, other)
-    return (left.T, lacc[0], right[:width].T, right[width], rel.T, relacc[0])
+        summed, right = sum_pieces(grad, sizes, square, core, right)
+        outs = (last_outs if last else step_outs) + [(width, kinds), (1, kinds), (grad_rows, LANES)]
+        left, lacc, right, *racc, rel, relacc, grad = call(
+            functools.partial(next_kernel, step, last), outs, (1, 9 + PIECES), [pieces]
+        )(place, left, lacc, right, rel, relacc, *summed, *ids)
+    summed, _ = sum_pieces(grad, sizes, square, core)
+    rel, relacc = call(last_kernel, [(width, kinds), (kinds,)], (1, 2 + PIECES), [pieces])(place, rel, relacc, *summed)
+    return (left.T, lacc, right.T, racc[0], rel.T, relacc)
 
 
 def solution(mesh):

time: 90.3 us -> 77.5 us (0.86)
  local copies, waits for them, and re-layouts: 8.59 us -> 0.21 us
  waiting for transfers between devices: 49.8 us -> 44.3 us
  Pallas kernels: 7.69 us -> 9.35 us
    unnamed x30 -> x12, local copies, waits for them, and re-layouts: 7.2 us -> 0.04 us
    ppermute x1, waiting for transfers between devices: 7.49 us -> 4.26 us  [from_behind(): return lax.ppermute(block, axis, [((i - 1) % n, i) for i in range(n)])]
    ppermute x18 -> x24, waiting for transfers between devices: 42.3 us -> 40.1 us  [swap(): return lax.ppermute(x, AXES, route)]
    pallas_call x3, Pallas kernels: 7.69 us -> 9.35 us  [the longest x1 3.99 us: shards(): pl.pallas_call(first_kernel, out_shape=[jax.ShapeDtypeStruct(shape, F32)...]
    ppermute x18 -> x24, starting transfers between devices: 20.3 us -> 19.7 us  [swap(): return lax.ppermute(x, AXES, route)]
  transfers between devices with their start and end apart: 19 -> 25, of which waited for: 17 -> 19; matrix products, arithmetic and copies ran while one was open for 1% -> 0% of each run, Pallas kernels for 0% -> 0%
where the time goes in v2:
time: 77.5 us; the launch traced here: 77.3 us
  waiting for transfers between devices  44.3 us (57%)
  starting transfers between devices  22.3 us (29%)
  Pallas kernels  9.35 us (12%)
  between operations  0.78 us (1%)
    ppermute x24, waiting for transfers between devices, swap(): return lax.ppermute(x, AXES, route)  40.1 us
    ppermute x24, starting transfers between devices, swap(): return lax.ppermute(x, AXES, route)  19.7 us
    ppermute x1, waiting for transfers between devices, from_behind(): return lax.ppermute(block, axis, [((i - 1) % n, i) for i in range(n)])  4.26 us
    pallas_call x1, Pallas kernels, shards(): pl.pallas_call(first_kernel, out_shape=[jax.ShapeDtypeStruct(shape, F32)...  3.99 us
    pallas_call x1, Pallas kernels, shards(): call(functools.partial(next_kernel, step, last), outs, (1, 9 + PIECES), [...  3.39 us
    ppermute x1, starting transfers between devices, from_behind(): return lax.ppermute(block, axis, [((i - 1) % n, i) for i in range(n)])  2.64 us
    pallas_call x1, Pallas kernels, shards(): call(last_kernel, [(width, kinds), (kinds,)], (1, 2 + PIECES), [pieces])  1.97 us
  transfers between devices with their start and end apart: 25, of which 19 were waited for; matrix products, arithmetic and copies ran while one was open for 0% of the time, Pallas kernels for 0%

profile of v2, /device:TPU:0, one launch (start us, length us, event | category | flops | bytes accessed | tf_op | source)
XLA Modules:
  0.0 77.3 jit_solution(518771231647194205)
XLA Ops:
  0.6 4.0 %shard_map.145 = (f32[400,128]{1,0:T(8,128)S(1)}, f32[1,128]{1,0:T(1,128)S(1)}, f32[408,128]{1,0:T(8,128)S(1)}, f32[2432,128]{1,0:T(8,128)S(1)}) custom-call(f32[400,128]{1,0:T(8,128)} %bitcast.50, f32[1,128]{1,0:T(1,128)} %bitcast.52, f32[400,128]{1,0:T(8,128)} %bitcast.51, f32[1,128]{1,0:T(1,128)} %bitcast.53, f32[400,768]{1,0:T(8,128)} %bitcast.44, ...), custom_call_target="tpu_custom_call" | custom-call | tf_op jit(solution)/shard_map/pallas_call | solution.py:249
  4.7 0.5 collective-permute-start
  5.2 2.6 %collective-permute-start.2 = (f32[408,128]{1,0:T(8,128)S(1)}, f32[408,128]{1,0:T(8,128)S(1)}, u32[]{:S(2)}, u32[]{:S(2)}) collective-permute-start(f32[408,128]{1,0:T(8,128)S(1)} %get-tuple-element.24), channel_id=1, source_target_pairs={{12,0},{0,4},{4,8},{8,12},{13,1},{1,5},{5,9},{9,13},{14,2},{2,6},{... | collective-permute-start | bytes 626696 | tf_op jit(solution)/shard_map/ppermute | solution.py:226
  8.1 2.0 %collective-permute-start.1 = (f32[304,128]{1,0:T(8,128)S(1)}, f32[304,128]{1,0:T(8,128)S(1)}, u32[]{:S(2)}, u32[]{:S(2)}) collective-permute-start(f32[304,128]{1,0:T(8,128)S(1)} %get-tuple-element.41), channel_id=1, source_target_pairs={{0,2},{1,3},{2,0},{3,1},{4,6},{5,7},{6,4},{7,5},{8,10},{9,11},{10,... | collective-permute-start | bytes 466952 | tf_op jit(solution)/shard_map/ppermute | solution.py:191
  10.0 1.6 %collective-permute-start.3 = (f32[304,128]{1,0:T(8,128)S(1)}, f32[304,128]{1,0:T(8,128)S(1)}, u32[]{:S(2)}, u32[]{:S(2)}) collective-permute-start(f32[304,128]{1,0:T(8,128)S(1)} %get-tuple-element.39), channel_id=1, source_target_pairs={{0,4},{1,5},{2,6},{3,7},{4,0},{5,1},{6,2},{7,3},{8,12},{9,13},{10,... | collective-permute-start | bytes 466952 | tf_op jit(solution)/shard_map/ppermute | solution.py:191
  11.6 4.3 %collective-permute-done.2.right_ref = f32[408,128]{1,0:T(8,128)S(1)} collective-permute-done((f32[408,128]{1,0:T(8,128)S(1)}, f32[408,128]{1,0:T(8,128)S(1)}, u32[]{:S(2)}, u32[]{:S(2)}) %collective-permute-start.2) | collective-permute-done | bytes 208928 | tf_op jit(solution)/shard_map/ppermute | solution.py:226
  15.9 3.2 %collective-permute-done.3 = f32[304,128]{1,0:T(8,128)S(1)} collective-permute-done((f32[304,128]{1,0:T(8,128)S(1)}, f32[304,128]{1,0:T(8,128)S(1)}, u32[]{:S(2)}, u32[]{:S(2)}) %collective-permute-start.3) | collective-permute-done | bytes 155680 | tf_op jit(solution)/shard_map/ppermute | solution.py:191
  19.1 4.2 %collective-permute-done.4 = f32[304,128]{1,0:T(8,128)S(1)} collective-permute-done((f32[304,128]{1,0:T(8,128)S(1)}, f32[304,128]{1,0:T(8,128)S(1)}, u32[]{:S(2)}, u32[]{:S(2)}) %collective-permute-start.4) | collective-permute-done | bytes 155680 | tf_op jit(solution)/shard_map/ppermute | solution.py:191
  23.3 1.8 %collective-permute-start.5 = (f32[304,128]{1,0:T(8,128)S(1)}, f32[304,128]{1,0:T(8,128)S(1)}, u32[]{:S(2)}, u32[]{:S(2)}) collective-permute-start(f32[304,128]{1,0:T(8,128)S(1)} %fusion.3), channel_id=1, source_target_pairs={{0,12},{1,13},{2,14},{3,15},{4,8},{5,9},{6,10},{7,11},{8,4},{9,5},... | collective-permute-start | bytes 466952 | tf_op jit(solution)/shard_map/ppermute | solution.py:191
  25.1 6.1 %collective-permute-done.5 = f32[304,128]{1,0:T(8,128)S(1)} collective-permute-done((f32[304,128]{1,0:T(8,128)S(1)}, f32[304,128]{1,0:T(8,128)S(1)}, u32[]{:S(2)}, u32[]{:S(2)}) %collective-permute-start.5) | collective-permute-done | bytes 155680 | tf_op jit(solution)/shard_map/ppermute | solution.py:191
  31.2 1.0 %collective-permute-start.8 = (f32[304,128]{1,0:T(8,128)S(1)}, f32[304,128]{1,0:T(8,128)S(1)}, u32[]{:S(2)}, u32[]{:S(2)}) collective-permute-start(f32[304,128]{1,0:T(8,128)S(1)} %add.71.refs_0_), channel_id=1, source_target_pairs={{0,6},{1,7},{2,4},{3,5},{4,2},{5,3},{6,0},{7,1},{8,14},{9,15},{10,... | collective-permute-start | bytes 466952 | tf_op jit(solution)/shard_map/ppermute | solution.py:191
  32.3 1.3 %collective-permute-start.7 = (f32[304,128]{1,0:T(8,128)S(1)}, f32[304,128]{1,0:T(8,128)S(1)}, u32[]{:S(2)}, u32[]{:S(2)}) collective-permute-start(f32[304,128]{1,0:T(8,128)S(1)} %add.71.refs_0_), channel_id=1, source_target_pairs={{0,2},{1,3},{2,0},{3,1},{4,6},{5,7},{6,4},{7,5},{8,10},{9,11},{10,... | collective-permute-start | bytes 466952 | tf_op jit(solution)/shard_map/ppermute | solution.py:191
  33.5 1.2 %collective-permute-start.6 = (f32[304,128]{1,0:T(8,128)S(1)}, f32[304,128]{1,0:T(8,128)S(1)}, u32[]{:S(2)}, u32[]{:S(2)}) collective-permute-start(f32[304,128]{1,0:T(8,128)S(1)} %add.71.refs_0_), channel_id=1, source_target_pairs={{0,4},{1,5},{2,6},{3,7},{4,0},{5,1},{6,2},{7,3},{8,12},{9,13},{10,... | collective-permute-start | bytes 466952 | tf_op jit(solution)/shard_map/ppermute | solution.py:191
  34.8 4.2 %collective-permute-done.8.refs_3_ = f32[304,128]{1,0:T(8,128)S(1)} collective-permute-done((f32[304,128]{1,0:T(8,128)S(1)}, f32[304,128]{1,0:T(8,128)S(1)}, u32[]{:S(2)}, u32[]{:S(2)}) %collective-permute-start.8) | collective-permute-done | bytes 155680 | tf_op jit(solution)/shard_map/ppermute | solution.py:191
  39.0 0.8 %collective-permute-done.7.refs_2_ = f32[304,128]{1,0:T(8,128)S(1)} collective-permute-done((f32[304,128]{1,0:T(8,128)S(1)}, f32[304,128]{1,0:T(8,128)S(1)}, u32[]{:S(2)}, u32[]{:S(2)}) %collective-permute-start.7) | collective-permute-done | bytes 155680 | tf_op jit(solution)/shard_map/ppermute | solution.py:191
  39.8 0.5 collective-permute-start.10
  40.4 0.8 %collective-permute-done.11.refs_6_ = f32[304,128]{1,0:T(8,128)S(1)} collective-permute-done((f32[304,128]{1,0:T(8,128)S(1)}, f32[304,128]{1,0:T(8,128)S(1)}, u32[]{:S(2)}, u32[]{:S(2)}) %collective-permute-start.11) | collective-permute-done | bytes 155680 | tf_op jit(solution)/shard_map/ppermute | solution.py:191
  41.4 3.4 %shard_map.146 = (f32[400,128]{1,0:T(8,128)}, f32[128]{0:T(128)}, f32[400,128]{1,0:T(8,128)}, f32[128]{0:T(128)}, f32[400,768]{1,0:T(8,128)S(1)}, /*index=5*/f32[1,768]{1,0:T(1,128)S(1)}, f32[2432,128]{1,0:T(8,128)S(1)}) custom-call(s32[2]{0:T(128)S(1)} %pad_add_fusion.place_ref, f32[400,128]{1,0:T(8,128)S(1)} %get-tuple-element.21.left_ref, ...), custom_call_target="tpu_custom_call" | custom-call | tf_op jit(solution)/shard_map/pallas_call | solution.py:262
  45.2 1.8 %collective-permute-done.13 = f32[4,304,128]{2,1,0:T(8,128)S(1)} collective-permute-done((f32[4,304,128]{2,1,0:T(8,128)S(1)}, f32[4,304,128]{2,1,0:T(8,128)S(1)}, u32[]{:S(2)}, u32[]{:S(2)}) %collective-permute-start.13) | collective-permute-done | bytes 622624 | tf_op jit(solution)/shard_map/ppermute | solution.py:191
  47.1 1.3 %collective-permute-start.15 = (f32[304,128]{1,0:T(8,128)S(1)}, f32[304,128]{1,0:T(8,128)S(1)}, u32[]{:S(2)}, u32[]{:S(2)}) collective-permute-start(f32[304,128]{1,0:T(8,128)S(1)} %get-tuple-element.38), channel_id=1, source_target_pairs={{0,2},{1,3},{2,0},{3,1},{4,6},{5,7},{6,4},{7,5},{8,10},{9,11},{10,... | collective-permute-start | bytes 466952 | tf_op jit(solution)/shard_map/ppermute | solution.py:191
  48.8 1.8 %collective-permute-start.16 = (f32[304,128]{1,0:T(8,128)S(1)}, f32[304,128]{1,0:T(8,128)S(1)}, u32[]{:S(2)}, u32[]{:S(2)}) collective-permute-start(f32[304,128]{1,0:T(8,128)S(1)} %get-tuple-element.37), channel_id=1, source_target_pairs={{0,6},{1,7},{2,4},{3,5},{4,2},{5,3},{6,0},{7,1},{8,14},{9,15},{10,... | collective-permute-start | bytes 466952 | tf_op jit(solution)/shard_map/ppermute | solution.py:191
  50.7 2.7 %collective-permute-done.15 = f32[304,128]{1,0:T(8,128)S(1)} collective-permute-done((f32[304,128]{1,0:T(8,128)S(1)}, f32[304,128]{1,0:T(8,128)S(1)}, u32[]{:S(2)}, u32[]{:S(2)}) %collective-permute-start.15) | collective-permute-done | bytes 155680 | tf_op jit(solution)/shard_map/ppermute | solution.py:191
  53.4 1.9 %collective-permute-done.14 = f32[304,128]{1,0:T(8,128)S(1)} collective-permute-done((f32[304,128]{1,0:T(8,128)S(1)}, f32[304,128]{1,0:T(8,128)S(1)}, u32[]{:S(2)}, u32[]{:S(2)}) %collective-permute-start.14) | collective-permute-done | bytes 155680 | tf_op jit(solution)/shard_map/ppermute | solution.py:191
  55.3 2.6 %collective-permute-done.16 = f32[304,128]{1,0:T(8,128)S(1)} collective-permute-done((f32[304,128]{1,0:T(8,128)S(1)}, f32[304,128]{1,0:T(8,128)S(1)}, u32[]{:S(2)}, u32[]{:S(2)}) %collective-permute-start.16) | collective-permute-done | bytes 155680 | tf_op jit(solution)/shard_map/ppermute | solution.py:191
  58.0 1.9 %collective-permute-start.17 = (f32[304,128]{1,0:T(8,128)S(1)}, f32[304,128]{1,0:T(8,128)S(1)}, u32[]{:S(2)}, u32[]{:S(2)}) collective-permute-start(f32[304,128]{1,0:T(8,128)S(1)} %fusion.1), channel_id=1, source_target_pairs={{0,12},{1,13},{2,14},{3,15},{4,8},{5,9},{6,10},{7,11},{8,4},{9,5},... | collective-permute-start | bytes 466952 | tf_op jit(solution)/shard_map/ppermute | solution.py:191
  59.8 5.3 %collective-permute-done.17 = f32[304,128]{1,0:T(8,128)S(1)} collective-permute-done((f32[304,128]{1,0:T(8,128)S(1)}, f32[304,128]{1,0:T(8,128)S(1)}, u32[]{:S(2)}, u32[]{:S(2)}) %collective-permute-start.17) | collective-permute-done | bytes 155680 | tf_op jit(solution)/shard_map/ppermute | solution.py:191
  65.1 2.5 %collective-permute-start.20 = (f32[304,128]{1,0:T(8,128)S(1)}, f32[304,128]{1,0:T(8,128)S(1)}, u32[]{:S(2)}, u32[]{:S(2)}) collective-permute-start(f32[304,128]{1,0:T(8,128)S(1)} %add.76.refs_0_), channel_id=1, source_target_pairs={{0,6},{1,7},{2,4},{3,5},{4,2},{5,3},{6,0},{7,1},{8,14},{9,15},{10,... | collective-permute-start | bytes 466952 | tf_op jit(solution)/shard_map/ppermute | solution.py:191
  67.6 1.1 %collective-permute-start.19 = (f32[304,128]{1,0:T(8,128)S(1)}, f32[304,128]{1,0:T(8,128)S(1)}, u32[]{:S(2)}, u32[]{:S(2)}) collective-permute-start(f32[304,128]{1,0:T(8,128)S(1)} %add.76.refs_0_), channel_id=1, source_target_pairs={{0,2},{1,3},{2,0},{3,1},{4,6},{5,7},{6,4},{7,5},{8,10},{9,11},{10,... | collective-permute-start | bytes 466952 | tf_op jit(solution)/shard_map/ppermute | solution.py:191
  68.7 4.3 %collective-permute-done.20.refs_3_ = f32[304,128]{1,0:T(8,128)S(1)} collective-permute-done((f32[304,128]{1,0:T(8,128)S(1)}, f32[304,128]{1,0:T(8,128)S(1)}, u32[]{:S(2)}, u32[]{:S(2)}) %collective-permute-start.20) | collective-permute-done | bytes 155680 | tf_op jit(solution)/shard_map/ppermute | solution.py:191
  73.0 0.7 collective-permute-done.19.refs_2_
  74.4 0.7 collective-permute-done.23.refs_6_
  75.4 2.0 %shard_map.147 = (f32[400,768]{1,0:T(8,128)}, f32[768]{0:T(1024)}) custom-call(s32[2]{0:T(128)S(1)} %pad_add_fusion.place_ref, f32[400,768]{1,0:T(8,128)S(1)} %get-tuple-element.31.rel_ref, f32[1,768]{1,0:T(1,128)S(1)} %get-tuple-element.32.relacc_ref, f32[304,128]{1,0:T(8,128)S(1)} %add.76.refs_0_, f32[304,128]{1,0:T(8,128)S(1)} %collective-permute-done.18.refs_1_, ...), custom_call_target="tpu_custom_call" | custom-call | tf_op jit(solution)/shard_map/pallas_call | solution.py:266
  (45 shorter events, 2.6 us)
Async XLA Ops:
  4.7 3.2 %collective-permute-start = (f32[4,304,128]{2,1,0:T(8,128)S(1)}, f32[4,304,128]{2,1,0:T(8,128)S(1)}, u32[]{:S(2)}, u32[]{:S(2)}) collective-permute-start(f32[4,304,128]{2,1,0:T(8,128)S(1)} %dynamic-slice_bitcast_fusion.1), channel_id=1, source_target_pairs={{0,1},{1,0},{2,3},{3,2},{4,5},{5,4},{6,7},{7,6},{8,9},{9,8},{10,11... | collective-permute-start | bytes 1867784 | tf_op jit(solution)/shard_map/ppermute | solution.py:191
  5.2 10.7 %collective-permute-start.2 = (f32[408,128]{1,0:T(8,128)S(1)}, f32[408,128]{1,0:T(8,128)S(1)}, u32[]{:S(2)}, u32[]{:S(2)}) collective-permute-start(f32[408,128]{1,0:T(8,128)S(1)} %get-tuple-element.24), channel_id=1, source_target_pairs={{12,0},{0,4},{4,8},{8,12},{13,1},{1,5},{5,9},{9,13},{14,2},{2,6},{... | collective-permute-start | bytes 626696 | tf_op jit(solution)/shard_map/ppermute | solution.py:226
  8.0 32.3 %copy-start.5 = (f32[768]{0:T(1024)S(1)}, f32[768]{0:T(1024)}, u32[]{:S(2)}) copy-start(f32[768]{0:T(1024)} %param.15) | copy-start | bytes 9220
  8.0 33.4 %copy-start = (f32[768,400]{0,1:T(8,128)S(1)}, f32[768,400]{0,1:T(8,128)}, u32[]{:S(2)}) copy-start(f32[768,400]{0,1:T(8,128)} %param.14) | copy-start | bytes 3686404
  8.0 33.4 %copy-start.1 = (s32[2,256]{1,0:T(2,128)S(1)}, s32[2,256]{1,0:T(2,128)}, u32[]{:S(2)}) copy-start(s32[2,256]{1,0:T(2,128)} %refs_8_.3) | copy-start | bytes 6148
  8.0 33.4 %copy-start.2 = (s32[2,256]{1,0:T(2,128)S(1)}, s32[2,256]{1,0:T(2,128)}, u32[]{:S(2)}) copy-start(s32[2,256]{1,0:T(2,128)} %refs_9_.1) | copy-start | bytes 6148
  8.0 33.4 %copy-start.3 = (s32[2,256]{1,0:T(2,128)S(1)}, s32[2,256]{1,0:T(2,128)}, u32[]{:S(2)}) copy-start(s32[2,256]{1,0:T(2,128)} %refs_10_.1) | copy-start | bytes 6148
  8.0 33.4 %copy-start.4 = (s32[2,2,128]{2,1,0:T(2,128)S(1)}, s32[2,2,128]{2,1,0:T(2,128)}, u32[]{:S(2)}) copy-start(s32[2,2,128]{2,1,0:T(2,128)} %refs_11_.1) | copy-start | bytes 6148
  8.1 7.8 %collective-permute-start.1 = (f32[304,128]{1,0:T(8,128)S(1)}, f32[304,128]{1,0:T(8,128)S(1)}, u32[]{:S(2)}, u32[]{:S(2)}) collective-permute-start(f32[304,128]{1,0:T(8,128)S(1)} %get-tuple-element.41), channel_id=1, source_target_pairs={{0,2},{1,3},{2,0},{3,1},{4,6},{5,7},{6,4},{7,5},{8,10},{9,11},{10,... | collective-permute-start | bytes 466952 | tf_op jit(solution)/shard_map/ppermute | solution.py:191
  10.0 9.0 %collective-permute-start.3 = (f32[304,128]{1,0:T(8,128)S(1)}, f32[304,128]{1,0:T(8,128)S(1)}, u32[]{:S(2)}, u32[]{:S(2)}) collective-permute-start(f32[304,128]{1,0:T(8,128)S(1)} %get-tuple-element.39), channel_id=1, source_target_pairs={{0,4},{1,5},{2,6},{3,7},{4,0},{5,1},{6,2},{7,3},{8,12},{9,13},{10,... | collective-permute-start | bytes 466952 | tf_op jit(solution)/shard_map/ppermute | solution.py:191
  11.6 11.6 %collective-permute-start.4 = (f32[304,128]{1,0:T(8,128)S(1)}, f32[304,128]{1,0:T(8,128)S(1)}, u32[]{:S(2)}, u32[]{:S(2)}) collective-permute-start(f32[304,128]{1,0:T(8,128)S(1)} %get-tuple-element.40), channel_id=1, source_target_pairs={{0,6},{1,7},{2,4},{3,5},{4,2},{5,3},{6,0},{7,1},{8,14},{9,15},{10,... | collective-permute-start | bytes 466952 | tf_op jit(solution)/shard_map/ppermute | solution.py:191
  23.3 7.9 %collective-permute-start.5 = (f32[304,128]{1,0:T(8,128)S(1)}, f32[304,128]{1,0:T(8,128)S(1)}, u32[]{:S(2)}, u32[]{:S(2)}) collective-permute-start(f32[304,128]{1,0:T(8,128)S(1)} %fusion.3), channel_id=1, source_target_pairs={{0,12},{1,13},{2,14},{3,15},{4,8},{5,9},{6,10},{7,11},{8,4},{9,5},... | collective-permute-start | bytes 466952 | tf_op jit(solution)/shard_map/ppermute | solution.py:191
  31.2 7.8 %collective-permute-start.8 = (f32[304,128]{1,0:T(8,128)S(1)}, f32[304,128]{1,0:T(8,128)S(1)}, u32[]{:S(2)}, u32[]{:S(2)}) collective-permute-start(f32[304,128]{1,0:T(8,128)S(1)} %add.71.refs_0_), channel_id=1, source_target_pairs={{0,6},{1,7},{2,4},{3,5},{4,2},{5,3},{6,0},{7,1},{8,14},{9,15},{10,... | collective-permute-start | bytes 466952 | tf_op jit(solution)/shard_map/ppermute | solution.py:191
  32.3 7.5 %collective-permute-start.7 = (f32[304,128]{1,0:T(8,128)S(1)}, f32[304,128]{1,0:T(8,128)S(1)}, u32[]{:S(2)}, u32[]{:S(2)}) collective-permute-start(f32[304,128]{1,0:T(8,128)S(1)} %add.71.refs_0_), channel_id=1, source_target_pairs={{0,2},{1,3},{2,0},{3,1},{4,6},{5,7},{6,4},{7,5},{8,10},{9,11},{10,... | collective-permute-start | bytes 466952 | tf_op jit(solution)/shard_map/ppermute | solution.py:191
  33.5 6.2 %collective-permute-start.6 = (f32[304,128]{1,0:T(8,128)S(1)}, f32[304,128]{1,0:T(8,128)S(1)}, u32[]{:S(2)}, u32[]{:S(2)}) collective-permute-start(f32[304,128]{1,0:T(8,128)S(1)} %add.71.refs_0_), channel_id=1, source_target_pairs={{0,4},{1,5},{2,6},{3,7},{4,0},{5,1},{6,2},{7,3},{8,12},{9,13},{10,... | collective-permute-start | bytes 466952 | tf_op jit(solution)/shard_map/ppermute | solution.py:191
  34.8 5.6 %collective-permute-start.9 = (f32[304,128]{1,0:T(8,128)S(1)}, f32[304,128]{1,0:T(8,128)S(1)}, u32[]{:S(2)}, u32[]{:S(2)}) collective-permute-start(f32[304,128]{1,0:T(8,128)S(1)} %add.71.refs_0_), channel_id=1, source_target_pairs={{0,1},{1,0},{2,3},{3,2},{4,5},{5,4},{6,7},{7,6},{8,9},{9,8},{10,11... | collective-permute-start | bytes 466952 | tf_op jit(solution)/shard_map/ppermute | solution.py:191
  39.0 1.4 %collective-permute-start.12 = (f32[304,128]{1,0:T(8,128)S(1)}, f32[304,128]{1,0:T(8,128)S(1)}, u32[]{:S(2)}, u32[]{:S(2)}) collective-permute-start(f32[304,128]{1,0:T(8,128)S(1)} %collective-permute-done.8.refs_3_), channel_id=1, source_target_pairs={{0,1},{1,0},{2,3},{3,2},{4,5},{5,4},{6,7},{7,6},{8,9},{9,8},{10,11... | collective-permute-start | bytes 466952 | tf_op jit(solution)/shard_map/ppermute | solution.py:191
  39.8 1.4 %collective-permute-start.11 = (f32[304,128]{1,0:T(8,128)S(1)}, f32[304,128]{1,0:T(8,128)S(1)}, u32[]{:S(2)}, u32[]{:S(2)}) collective-permute-start(f32[304,128]{1,0:T(8,128)S(1)} %collective-permute-done.7.refs_2_), channel_id=1, source_target_pairs={{0,1},{1,0},{2,3},{3,2},{4,5},{5,4},{6,7},{7,6},{8,9},{9,8},{10,11... | collective-permute-start | bytes 466952 | tf_op jit(solution)/shard_map/ppermute | solution.py:191
  39.8 1.6 %collective-permute-start.10 = (f32[304,128]{1,0:T(8,128)S(1)}, f32[304,128]{1,0:T(8,128)S(1)}, u32[]{:S(2)}, u32[]{:S(2)}) collective-permute-start(f32[304,128]{1,0:T(8,128)S(1)} %collective-permute-done.6.refs_1_), channel_id=1, source_target_pairs={{0,1},{1,0},{2,3},{3,2},{4,5},{5,4},{6,7},{7,6},{8,9},{9,8},{10,11... | collective-permute-start | bytes 466952 | tf_op jit(solution)/shard_map/ppermute | solution.py:191
  44.8 2.1 %collective-permute-start.13 = (f32[4,304,128]{2,1,0:T(8,128)S(1)}, f32[4,304,128]{2,1,0:T(8,128)S(1)}, u32[]{:S(2)}, u32[]{:S(2)}) collective-permute-start(f32[4,304,128]{2,1,0:T(8,128)S(1)} %dynamic-slice_bitcast_fusion), channel_id=1, source_target_pairs={{0,1},{1,0},{2,3},{3,2},{4,5},{5,4},{6,7},{7,6},{8,9},{9,8},{10,11... | collective-permute-start | bytes 1867784 | tf_op jit(solution)/shard_map/ppermute | solution.py:191
  47.1 6.3 %collective-permute-start.15 = (f32[304,128]{1,0:T(8,128)S(1)}, f32[304,128]{1,0:T(8,128)S(1)}, u32[]{:S(2)}, u32[]{:S(2)}) collective-permute-start(f32[304,128]{1,0:T(8,128)S(1)} %get-tuple-element.38), channel_id=1, source_target_pairs={{0,2},{1,3},{2,0},{3,1},{4,6},{5,7},{6,4},{7,5},{8,10},{9,11},{10,... | collective-permute-start | bytes 466952 | tf_op jit(solution)/shard_map/ppermute | solution.py:191
  48.4 6.9 %collective-permute-start.14 = (f32[304,128]{1,0:T(8,128)S(1)}, f32[304,128]{1,0:T(8,128)S(1)}, u32[]{:S(2)}, u32[]{:S(2)}) collective-permute-start(f32[304,128]{1,0:T(8,128)S(1)} %get-tuple-element.36), channel_id=1, source_target_pairs={{0,4},{1,5},{2,6},{3,7},{4,0},{5,1},{6,2},{7,3},{8,12},{9,13},{10,... | collective-permute-start | bytes 466952 | tf_op jit(solution)/shard_map/ppermute | solution.py:191
  48.8 9.1 %collective-permute-start.16 = (f32[304,128]{1,0:T(8,128)S(1)}, f32[304,128]{1,0:T(8,128)S(1)}, u32[]{:S(2)}, u32[]{:S(2)}) collective-permute-start(f32[304,128]{1,0:T(8,128)S(1)} %get-tuple-element.37), channel_id=1, source_target_pairs={{0,6},{1,7},{2,4},{3,5},{4,2},{5,3},{6,0},{7,1},{8,14},{9,15},{10,... | collective-permute-start | bytes 466952 | tf_op jit(solution)/shard_map/ppermute | solution.py:191
  58.0 7.1 %collective-permute-start.17 = (f32[304,128]{1,0:T(8,128)S(1)}, f32[304,128]{1,0:T(8,128)S(1)}, u32[]{:S(2)}, u32[]{:S(2)}) collective-permute-start(f32[304,128]{1,0:T(8,128)S(1)} %fusion.1), channel_id=1, source_target_pairs={{0,12},{1,13},{2,14},{3,15},{4,8},{5,9},{6,10},{7,11},{8,4},{9,5},... | collective-permute-start | bytes 466952 | tf_op jit(solution)/shard_map/ppermute | solution.py:191
  65.1 7.9 %collective-permute-start.20 = (f32[304,128]{1,0:T(8,128)S(1)}, f32[304,128]{1,0:T(8,128)S(1)}, u32[]{:S(2)}, u32[]{:S(2)}) collective-permute-start(f32[304,128]{1,0:T(8,128)S(1)} %add.76.refs_0_), channel_id=1, source_target_pairs={{0,6},{1,7},{2,4},{3,5},{4,2},{5,3},{6,0},{7,1},{8,14},{9,15},{10,... | collective-permute-start | bytes 466952 | tf_op jit(solution)/shard_map/ppermute | solution.py:191
  67.6 6.1 %collective-permute-start.19 = (f32[304,128]{1,0:T(8,128)S(1)}, f32[304,128]{1,0:T(8,128)S(1)}, u32[]{:S(2)}, u32[]{:S(2)}) collective-permute-start(f32[304,128]{1,0:T(8,128)S(1)} %add.76.refs_0_), channel_id=1, source_target_pairs={{0,2},{1,3},{2,0},{3,1},{4,6},{5,7},{6,4},{7,5},{8,10},{9,11},{10,... | collective-permute-start | bytes 466952 | tf_op jit(solution)/shard_map/ppermute | solution.py:191
  68.7 5.2 %collective-permute-start.18 = (f32[304,128]{1,0:T(8,128)S(1)}, f32[304,128]{1,0:T(8,128)S(1)}, u32[]{:S(2)}, u32[]{:S(2)}) collective-permute-start(f32[304,128]{1,0:T(8,128)S(1)} %add.76.refs_0_), channel_id=1, source_target_pairs={{0,4},{1,5},{2,6},{3,7},{4,0},{5,1},{6,2},{7,3},{8,12},{9,13},{10,... | collective-permute-start | bytes 466952 | tf_op jit(solution)/shard_map/ppermute | solution.py:191
  68.7 5.6 %collective-permute-start.21 = (f32[304,128]{1,0:T(8,128)S(1)}, f32[304,128]{1,0:T(8,128)S(1)}, u32[]{:S(2)}, u32[]{:S(2)}) collective-permute-start(f32[304,128]{1,0:T(8,128)S(1)} %add.76.refs_0_), channel_id=1, source_target_pairs={{0,1},{1,0},{2,3},{3,2},{4,5},{5,4},{6,7},{7,6},{8,9},{9,8},{10,11... | collective-permute-start | bytes 466952 | tf_op jit(solution)/shard_map/ppermute | solution.py:191
  73.0 1.4 %collective-permute-start.24 = (f32[304,128]{1,0:T(8,128)S(1)}, f32[304,128]{1,0:T(8,128)S(1)}, u32[]{:S(2)}, u32[]{:S(2)}) collective-permute-start(f32[304,128]{1,0:T(8,128)S(1)} %collective-permute-done.20.refs_3_), channel_id=1, source_target_pairs={{0,1},{1,0},{2,3},{3,2},{4,5},{5,4},{6,7},{7,6},{8,9},{9,8},{10,11... | collective-permute-start | bytes 466952 | tf_op jit(solution)/shard_map/ppermute | solution.py:191
  73.8 1.4 %collective-permute-start.23 = (f32[304,128]{1,0:T(8,128)S(1)}, f32[304,128]{1,0:T(8,128)S(1)}, u32[]{:S(2)}, u32[]{:S(2)}) collective-permute-start(f32[304,128]{1,0:T(8,128)S(1)} %collective-permute-done.19.refs_2_), channel_id=1, source_target_pairs={{0,1},{1,0},{2,3},{3,2},{4,5},{5,4},{6,7},{7,6},{8,9},{9,8},{10,11... | collective-permute-start | bytes 466952 | tf_op jit(solution)/shard_map/ppermute | solution.py:191
  73.9 1.4 %collective-permute-start.22 = (f32[304,128]{1,0:T(8,128)S(1)}, f32[304,128]{1,0:T(8,128)S(1)}, u32[]{:S(2)}, u32[]{:S(2)}) collective-permute-start(f32[304,128]{1,0:T(8,128)S(1)} %collective-permute-done.18.refs_1_), channel_id=1, source_target_pairs={{0,1},{1,0},{2,3},{3,2},{4,5},{5,4},{6,7},{7,6},{8,9},{9,8},{10,11... | collective-permute-start | bytes 466952 | tf_op jit(solution)/shard_map/ppermute | solution.py:191

commit v3 on v2

v3 whole, which is shorter than its diff:
```python
import functools
import math

import jax
import jax.numpy as jnp
from jax import lax
from jax.experimental import pallas as pl
from jax.experimental.pallas import tpu as pltpu
from jax.sharding import PartitionSpec as P

RATE = 0.1
AXES = ("blk", "shard", "sub")
LANES = 128
PIECES = 8
F32 = jnp.float32
BF16 = jnp.bfloat16


def halves(x):
    high = x.astype(BF16)
    return high, (x - high.astype(F32)).astype(BF16)


def nn(a, b):
    return lax.dot_general(a, b, (((1,), (0,)), ((), ())), preferred_element_type=F32)


def nt(a, b):
    return lax.dot_general(a, b, (((1,), (1,)), ((), ())), preferred_element_type=F32)


def times_selector(dot, x, selector):
    high, low = halves(x)
    rows = x.shape[0]
    both = dot(jnp.concatenate([high, low], axis=0), selector)
    return both[:rows] + both[rows:]


def times(dot, a, b):
    a_high, a_low = halves(a)
    b_high, b_low = halves(b)
    rows = a.shape[0]
    both = dot(jnp.concatenate([a_high, a_low], axis=0), b_high)
    return both[:rows] + (both[rows:] + dot(a_high, b_low))


def selector(ids, rows):
    return (lax.broadcasted_iota(jnp.int32, (rows, ids.shape[1]), 0) == ids).astype(F32)


def adagrad(weights, accum, grads):
    accum = accum + jnp.sum(grads * grads, axis=0, keepdims=True) * (1.0 / grads.shape[0])
    return weights - grads * (RATE / jnp.sqrt(accum)), accum


def score(right, rel_rows, heads, tail_ids, negative):
    rows = right.shape[1]
    count, negs = negative.shape
    query = heads * rel_rows
    scores = times(nn, right.T, query)
    tiny = jnp.exp(-jnp.abs(scores))
    inverse = 1.0 / (1.0 + tiny)
    up = scores >= 0
    sig = jnp.where(up, 1.0, tiny) * inverse
    sig_minus = jnp.where(up, tiny, 1.0) * inverse
    named = []
    for c in range(count):
        hits = lax.broadcasted_iota(jnp.int32, (rows, negs), 0) == negative[c : c + 1]
        share = jnp.sum(hits.astype(F32), axis=1, keepdims=True) * (1.0 / negs)
        named.append(jnp.broadcast_to(share, (rows, query.shape[1] // count)))
    weight = jnp.concatenate(named, axis=1) * sig - selector(tail_ids, rows) * sig_minus
    return query, weight


def cut(width):
    main = width // (8 * PIECES) * 8
    return main, width // PIECES - main


def put_terms(place_ref, terms, kinds, out_ref):
    square, core = place_ref[0], place_ref[1]
    width, edges = terms.shape
    half = PIECES // 2
    main, rest = cut(width)
    below = jnp.zeros((8 - rest - 1, LANES), F32)
    for c in range(PIECES):
        at = jnp.bitwise_xor(c // half, core) * half + jnp.bitwise_xor(c % half, square)
        last = main * PIECES + rest * c
        for j in range(edges // LANES):
            lanes = slice(LANES * j, LANES * (j + 1))
            top = (main + 8) * j
            out_ref[at, top : top + main] = terms[main * c : main * (c + 1), lanes]
            out_ref[at, top + main : top + main + 8] = jnp.concatenate(
                [terms[last : last + rest, lanes], kinds[:, lanes].astype(F32), below], axis=0
            )


def sum_terms(width, kinds, blocks_of_edges):
    main, rest = cut(width)
    total = None
    for i in range(0, len(blocks_of_edges), 2):
        pair = jnp.concatenate(blocks_of_edges[i : i + 2], axis=1)
        both = jnp.concatenate(halves(pair), axis=0)
        grad = nt(both, selector(pair[main + rest : main + rest + 1].astype(jnp.int32), kinds).astype(BF16))
        grad = grad[: main + 8] + grad[main + 8 :]
        total = grad if total is None else total + grad
    return total


def put_piece(grad, width, out_ref, before_ref=None):
    main, rest = cut(width)
    blocks = grad.shape[1] // LANES
    for j in range(blocks):
        lanes = slice(LANES * j, LANES * (j + 1))
        for rows, part in (
            (slice(main * j, main * (j + 1)), grad[:main, lanes]),
            (slice(main * blocks + rest * j, main * blocks + rest * (j + 1)), grad[main : main + rest, lanes]),
        ):
            out_ref[rows] = part if before_ref is None else before_ref[rows] + part
    end = (main + rest) * blocks
    out_ref[end:] = jnp.zeros((out_ref.shape[0] - end, LANES), F32)


def chip_kernel(width, kinds, own_ref, other_ref, out_ref):
    rows = cut(width)[0] + 8
    tiles = [ref[0, rows * j : rows * (j + 1)] for ref in (own_ref, other_ref) for j in range(ref.shape[1] // rows)]
    put_piece(sum_terms(width, kinds, tiles), width, out_ref)


def more_kernel(width, kinds, total_ref, terms_ref, out_ref):
    rows = cut(width)[0] + 8
    tiles = [terms_ref[rows * j : rows * (j + 1)] for j in range(terms_ref.shape[0] // rows)]
    put_piece(sum_terms(width, kinds, tiles), width, out_ref, total_ref)


def order_pieces(place_ref, piece_refs, all_ref):
    square, core = place_ref[0], place_ref[1]
    half = PIECES // 2
    for i in range(half):
        piece = jnp.bitwise_xor(square, i)
        all_ref[core * half + piece] = piece_refs[i][...]
        all_ref[(1 - core) * half + piece] = piece_refs[half + i][...]


def take_rel_grad(all_ref, j, width, blocks):
    main, rest = cut(width)
    first, last = main * j, main * blocks + rest * j
    return jnp.concatenate(
        [all_ref[c, first : first + main] for c in range(PIECES)]
        + [all_ref[c, last : last + rest] for c in range(PIECES)],
        axis=0,
    )


def next_accum(relacc_ref, all_ref, width):
    squares = []
    blocks = relacc_ref.shape[1] // LANES
    for j in range(blocks):
        grad = take_rel_grad(all_ref, j, width, blocks)
        squares.append(jnp.sum(grad * grad, axis=0, keepdims=True))
    accum = relacc_ref[...] + jnp.concatenate(squares, axis=1) * (1.0 / width)
    return accum, RATE / jnp.sqrt(accum)


def put_packed(out_ref, right, acc):
    width = right.shape[0]
    out_ref[:width] = right
    out_ref[width:] = jnp.broadcast_to(acc, (8, acc.shape[1]))


def first_kernel(place_ref, *refs):
    given, (right_out, terms_out, carry_out), held, sems = refs[:8], refs[8:11], refs[11:19], refs[19]
    copies = [pltpu.make_async_copy(a, b, sems.at[i]) for i, (a, b) in enumerate(zip(given, held))]
    for copy in copies:
        copy.start()
    hid_ref, tid_ref, kid_ref, nid_ref, left_ref, right_ref, racc_ref, rel_ref = held
    for copy in copies[:5]:
        copy.wait()
    head_sel = selector(hid_ref[0:1], left_ref.shape[1]).astype(BF16)
    kind_sel = selector(kid_ref[0:1], rel_ref.shape[1]).astype(BF16)
    heads = times_selector(nn, left_ref[...], head_sel)
    for copy in copies[5:]:
        copy.wait()
    right = right_ref[...]
    rel_rows = times_selector(nn, rel_ref[...], kind_sel)
    query, weight = score(right, rel_rows, heads, tid_ref[0:1], nid_ref[0])
    grad_query = times(nn, right, weight)
    put_terms(place_ref, grad_query * heads, kid_ref[0:1], terms_out)
    put_packed(right_out, *adagrad(right, racc_ref[...], times(nt, query, weight)))
    carry_out[...] = grad_query * rel_rows


def left_kernel(step, left_ref, lacc_ref, carry_ref, hid_ref, left_out, lacc_out, heads_out):
    rows = left_ref.shape[1]
    grad = times_selector(nt, carry_ref[...], selector(hid_ref[step : step + 1], rows).astype(BF16))
    left, lacc_out[...] = adagrad(left_ref[...], lacc_ref[...], grad)
    left_out[...] = left
    heads_out[...] = times_selector(nn, left, selector(hid_ref[step + 1 : step + 2], rows).astype(BF16))


def next_kernel(step, place_ref, heads_ref, right_ref, rel_ref, relacc_ref, *refs):
    piece_refs, (tid_ref, kid_ref, nid_ref) = refs[:PIECES], refs[PIECES : PIECES + 3]
    rel_out, relacc_out, terms_out, carry_out, query_out, weight_out, all_ref, split_ref = refs[PIECES + 3 :]
    width = heads_ref.shape[0]
    order_pieces(place_ref, piece_refs, all_ref)
    relacc_out[...], rate = next_accum(relacc_ref, all_ref, width)
    blocks = rel_ref.shape[1] // LANES
    for j in range(blocks):
        lanes = slice(LANES * j, LANES * (j + 1))
        rel = rel_ref[:, lanes] - take_rel_grad(all_ref, j, width, blocks) * rate[:, lanes]
        rel_out[:, lanes] = rel
        split_ref[:width, lanes], split_ref[width:, lanes] = halves(rel)
    kind_sel = selector(kid_ref[step : step + 1], rel_ref.shape[1]).astype(BF16)
    heads = heads_ref[...]
    both = nn(split_ref[...], kind_sel)
    rel_rows = both[:width] + both[width:]
    right = right_ref[:width]
    query, weight = score(right, rel_rows, heads, tid_ref[step : step + 1], nid_ref[step])
    grad_query = times(nn, right, weight)
    put_terms(place_ref, grad_query * heads, kid_ref[step : step + 1], terms_out)
    carry_out[...] = grad_query * rel_rows
    query_out[...] = query
    weight_out[...] = weight


def right_kernel(right_ref, query_ref, weight_ref, right_out):
    width = query_ref.shape[0]
    grad = times(nt, query_ref[...], weight_ref[...])
    put_packed(right_out, *adagrad(right_ref[:width], right_ref[width : width + 1], grad))


def update_kernel(
    step, left_ref, lacc_ref, carry_ref, hid_ref, right_ref, query_ref, weight_ref,
    left_out, lacc_out, right_out, racc_out,
):
    rows = left_ref.shape[1]
    grad = times_selector(nt, carry_ref[...], selector(hid_ref[step : step + 1], rows).astype(BF16))
    left_out[...], acc = adagrad(left_ref[...], lacc_ref[...], grad)
    lacc_out[...] = acc[0]
    width = left_ref.shape[0]
    grad = times(nt, query_ref[...], weight_ref[...])
    right_out[...], acc = adagrad(right_ref[:width], right_ref[width : width + 1], grad)
    racc_out[...] = acc[0]


def last_kernel(place_ref, rel_ref, relacc_ref, *refs):
    piece_refs, (rel_out, relacc_out, all_ref) = refs[:PIECES], refs[PIECES:]
    width = rel_ref.shape[0]
    order_pieces(place_ref, piece_refs, all_ref)
    accum, rate = next_accum(relacc_ref, all_ref, width)
    relacc_out[...] = accum[0]
    blocks = rel_ref.shape[1] // LANES
    for j in range(blocks):
        lanes = slice(LANES * j, LANES * (j + 1))
        rel_out[:, lanes] = rel_ref[:, lanes] - take_rel_grad(all_ref, j, width, blocks) * rate[:, lanes]


HBM = pl.BlockSpec(memory_space=pltpu.HBM)
VMEM = pl.BlockSpec(memory_space=pltpu.VMEM)
SMEM = pl.BlockSpec(memory_space=pltpu.SMEM)
PARAMS = pltpu.CompilerParams(vmem_limit_bytes=40 * 1024 * 1024)


def call(kernel, outs, scratch=(), smem=0, hbm_outs=(), name=None, flops=0):
    def run(*given):
        moved = sum(math.prod(x.shape) for x in given) + sum(math.prod(shape) for shape in outs)
        in_specs = [SMEM if i < smem else VMEM for i in range(len(given))]
        return pl.pallas_call(
            kernel,
            out_shape=[jax.ShapeDtypeStruct(shape, F32) for shape in outs],
            in_specs=in_specs,
            out_specs=[HBM if i in hbm_outs else VMEM for i in range(len(outs))],
            scratch_shapes=list(scratch),
            compiler_params=PARAMS,
            cost_estimate=pl.CostEstimate(flops=flops, bytes_accessed=4 * moved, transcendentals=0),
            name=name,
        )(*given)

    return run


def swap(x, sizes, blk=0, shard=0, sub=0):
    n_blk, n_shard, n_sub = sizes

    def number(b, k, u):
        return (b * n_shard + k) * n_sub + u

    route = [
        (number(b, k, u), number(b ^ blk, k ^ shard, u ^ sub))
        for b in range(n_blk)
        for k in range(n_shard)
        for u in range(n_sub)
    ]
    return lax.ppermute(x, AXES, route)


def gray(i):
    return jnp.bitwise_and(jnp.bitwise_xor(i, i >> 1), 1)


def sum_pieces(terms, sizes, width, kinds, beside=(), aside=()):
    half = PIECES // 2
    piece = (-(-(width // PIECES) * kinds // LANES // 8) * 8, LANES)
    other = swap(terms[half:], sizes, sub=1)
    got = [
        swap(jnp.concatenate([terms[i], other[i]], axis=0), sizes, blk=i & 1, shard=i >> 1) for i in range(1, half)
    ]
    got[1], beside = lax.optimization_barrier((got[1], beside))
    total = call(functools.partial(chip_kernel, width, kinds), [piece], name="chip_terms")(terms, other)[0]
    for more in (got[1], got[0], got[2]):
        total = call(functools.partial(more_kernel, width, kinds), [piece], name="more_terms")(total, more)[0]
    reach = 4
    while reach <= sizes[0]:
        total = total + swap(total, sizes, blk=reach - 1)
        reach *= 2
    reach = 4
    while reach <= sizes[1]:
        total = total + swap(total, sizes, shard=reach - 1)
        reach *= 2
    total, aside = lax.optimization_barrier((total, aside))
    mine = [total] + [swap(total, sizes, blk=i & 1, shard=i >> 1) for i in range(1, half)]
    return mine + [swap(x, sizes, sub=1) for x in mine], beside, aside


def from_behind(block, axis):
    n = lax.axis_size(axis)
    return lax.ppermute(block, axis, [((i - 1) % n, i) for i in range(n)])


def shards(
    head_table, head_accum, tail_table, tail_accum, relations, rel_accum, head_ids, tail_ids, rel_ids, neg_ids
):
    sizes = tuple(lax.axis_size(a) for a in AXES)
    steps = head_ids.shape[0]
    rows, width = head_table.shape
    kinds = relations.shape[0]
    core = lax.axis_index("sub")
    square = gray(lax.axis_index("shard")) * 2 + gray(lax.axis_index("blk"))
    place = jnp.stack([square, core]).astype(jnp.int32)

    left, lacc = head_table.T, head_accum[None]
    rel, relacc = relations.T, rel_accum[None]
    edges = head_ids.shape[1]
    table, state, each = (width, rows), (1, rows), (width, edges)
    cut_terms = (PIECES, edges // LANES * (cut(width)[0] + 8), LANES)
    given = (head_ids, tail_ids, rel_ids, neg_ids, left, tail_table.T, tail_accum[None], rel)
    right, terms, carry = pl.pallas_call(
        first_kernel,
        out_shape=[jax.ShapeDtypeStruct(shape, F32) for shape in [(width + 8, rows), cut_terms, each]],
        in_specs=[SMEM] + [HBM] * len(given),
        out_specs=[VMEM] * 3,
        scratch_shapes=[pltpu.VMEM(x.shape, x.dtype) for x in given] + [pltpu.SemaphoreType.DMA((len(given),))],
        compiler_params=PARAMS,
        name="first_step",
    )(place, *[pltpu.with_memory_space_constraint(x, pltpu.HBM) for x in given])
    all_pieces = pltpu.VMEM((PIECES, -(-(width // PIECES) * kinds // LANES // 8) * 8, LANES), F32)
    for step in range(1, steps):
        if step > 1:
            right = call(right_kernel, [(width + 8, rows)])(right, query, weight)
        right = from_behind(right, "blk")
        left, lacc, heads = call(functools.partial(left_kernel, step - 1), [table, state, each], name="left_update")(
            left, lacc, carry, head_ids
        )
        summed, right, (left, lacc, heads) = sum_pieces(terms, sizes, width, kinds, right, (left, lacc, heads))
        rel, relacc, terms, carry, query, weight = call(
            functools.partial(next_kernel, step),
            [(width, kinds), (1, kinds), cut_terms, each, each, (rows, edges)],
            [all_pieces, pltpu.VMEM((2 * width, kinds), BF16)],
            smem=1,
            name="next_step",
        )(place, heads, right, rel, relacc, *summed, tail_ids, rel_ids, neg_ids)
    updated = call(
        functools.partial(update_kernel, steps - 1), [table, (rows,), table, (rows,)], name="last_update"
    )(left, lacc, carry, head_ids, right, query, weight)
    summed, _, (left, lacc, right, racc) = sum_pieces(terms, sizes, width, kinds, aside=updated)
    rel, relacc = call(
        last_kernel,
        [(width, kinds), (kinds,)],
        [all_pieces],
        smem=1,
        name="last_relations",
    )(place, rel, relacc, *summed)
    return (left.T, lacc, right.T, racc, rel.T, relacc)


def solution(mesh):
    every = ("groups", "blk", "shard", "sub")
    return jax.shard_map(
        shards,
        mesh=mesh,
        in_specs=(
            P(every, None),
            P(every),
            P(every, None),
            P(every),
            P("groups", None),
            P("groups"),
            P(None, every),
            P(None, every),
            P(None, every),
            P(None, every, None),
        ),
        out_specs=(P(every, None), P(every), P(every, None), P(every), P("groups", None), P("groups")),
        check_vma=False,
    )
```

time: 77.5 us -> 72 us (0.929)
  waiting for transfers between devices: 44.3 us -> 36.5 us
  Pallas kernels: 9.35 us -> 13.1 us
  starting transfers between devices: 22.3 us -> 21.1 us
    ppermute x24, waiting for transfers between devices: 40.1 us -> 35 us  [swap(): return lax.ppermute(x, AXES, route)]
    pallas_call x2 -> x12, Pallas kernels: 5.36 us -> 9.35 us  [run(): pl.pallas_call(kernel, out_shape=[jax.ShapeDtypeStruct(shape, F32) for sh...]
    ppermute x1, waiting for transfers between devices: 4.26 us -> 1.48 us  [from_behind(): return lax.ppermute(block, axis, [((i - 1) % n, i) for i in range(n)])]
    ppermute x24, starting transfers between devices: 19.7 us -> 18 us  [swap(): return lax.ppermute(x, AXES, route)]
  transfers between devices with their start and end apart: 25 -> 25, of which waited for: 19 -> 20; matrix products, arithmetic and copies ran while one was open for 0% -> 0% of each run, Pallas kernels for 0% -> 6%
where the time goes in v3:
time: 72 us; the launch traced here: 71.8 us
  waiting for transfers between devices  36.5 us (51%)
  starting transfers between devices  21.1 us (29%)
  Pallas kernels  13.1 us (18%)
  between operations  0.91 us (1%)
    ppermute x24, waiting for transfers between devices, swap(): return lax.ppermute(x, AXES, route)  35 us
    ppermute x24, starting transfers between devices, swap(): return lax.ppermute(x, AXES, route)  18 us
    pallas_call x12, Pallas kernels, run(): pl.pallas_call(kernel, out_shape=[jax.ShapeDtypeStruct(shape, F32) for sh...  9.35 us
    pallas_call x1, Pallas kernels, shards(): pl.pallas_call(first_kernel, out_shape=[jax.ShapeDtypeStruct(shape, F32)...  3.7 us
    ppermute x1, starting transfers between devices, from_behind(): return lax.ppermute(block, axis, [((i - 1) % n, i) for i in range(n)])  3.08 us
    ppermute x1, waiting for transfers between devices, from_behind(): return lax.ppermute(block, axis, [((i - 1) % n, i) for i in range(n)])  1.48 us
  transfers between devices with their start and end apart: 25, of which 20 were waited for; matrix products, arithmetic and copies ran while one was open for 0% of the time, Pallas kernels for 6%

profile of v3, /device:TPU:0, one launch (start us, length us, event | category | flops | bytes accessed | tf_op | source)
XLA Modules:
  0.0 71.8 jit_solution(13709864109944272038)
XLA Ops:
  0.7 3.7 %first_step.1 = (f32[408,128]{1,0:T(8,128)S(1)}, f32[8,112,128]{2,1,0:T(8,128)S(1)}, f32[400,256]{1,0:T(8,128)S(1)}) custom-call(s32[2]{0:T(128)S(1)} %pad_add_fusion.place_ref, s32[2,256]{1,0:T(2,128)} %hid_ref.3, s32[2,256]{1,0:T(2,128)} %refs_8_.1, s32[2,256]{1,0:T(2,128)} %refs_9_.1, s32[2,2,128]{2,1,0:T(2,128)} %refs_10_.1, f32[400,128]{1,0:T(8,128)} %bitcast.36, ...), custom_call_target="tpu_custom_call" | custom-call | tf_op jit(solution)/shard_map/first_step/pallas_call | solution.py:347
  4.4 3.1 %collective-permute-start.2 = (f32[408,128]{1,0:T(8,128)S(1)}, f32[408,128]{1,0:T(8,128)S(1)}, u32[]{:S(2)}, u32[]{:S(2)}) collective-permute-start(f32[408,128]{1,0:T(8,128)S(1)} %get-tuple-element.36), channel_id=1, source_target_pairs={{12,0},{0,4},{4,8},{8,12},{13,1},{1,5},{5,9},{9,13},{14,2},{2,6},{... | collective-permute-start | bytes 626696 | tf_op jit(solution)/shard_map/ppermute | solution.py:327
  7.6 1.5 %collective-permute-done.other_ref = f32[4,112,128]{2,1,0:T(8,128)S(1)} collective-permute-done((f32[4,112,128]{2,1,0:T(8,128)S(1)}, f32[4,112,128]{2,1,0:T(8,128)S(1)}, u32[]{:S(2)}, u32[]{:S(2)}) %collective-permute-start) | collective-permute-done | bytes 229408 | tf_op jit(solution)/shard_map/ppermute | solution.py:294
  9.1 1.6 %collective-permute-start.1 = (f32[224,128]{1,0:T(8,128)S(1)}, f32[224,128]{1,0:T(8,128)S(1)}, u32[]{:S(2)}, u32[]{:S(2)}) collective-permute-start(f32[224,128]{1,0:T(8,128)S(1)} %pad_maximum_fusion), channel_id=1, source_target_pairs={{0,2},{1,3},{2,0},{3,1},{4,6},{5,7},{6,4},{7,5},{8,10},{9,11},{10,... | collective-permute-start | bytes 344072 | tf_op jit(solution)/shard_map/ppermute | solution.py:294
  10.7 1.6 %collective-permute-start.3 = (f32[224,128]{1,0:T(8,128)S(1)}, f32[224,128]{1,0:T(8,128)S(1)}, u32[]{:S(2)}, u32[]{:S(2)}) collective-permute-start(f32[224,128]{1,0:T(8,128)S(1)} %pad_maximum_fusion.1), channel_id=1, source_target_pairs={{0,4},{1,5},{2,6},{3,7},{4,0},{5,1},{6,2},{7,3},{8,12},{9,13},{10,... | collective-permute-start | bytes 344072 | tf_op jit(solution)/shard_map/ppermute | solution.py:294
  13.3 1.5 %collective-permute-done.2.right_ref = f32[408,128]{1,0:T(8,128)S(1)} collective-permute-done((f32[408,128]{1,0:T(8,128)S(1)}, f32[408,128]{1,0:T(8,128)S(1)}, u32[]{:S(2)}, u32[]{:S(2)}) %collective-permute-start.2) | collective-permute-done | bytes 208928 | tf_op jit(solution)/shard_map/ppermute | solution.py:327
  15.2 2.0 %collective-permute-done.3.terms_ref = f32[224,128]{1,0:T(8,128)S(1)} collective-permute-done((f32[224,128]{1,0:T(8,128)S(1)}, f32[224,128]{1,0:T(8,128)S(1)}, u32[]{:S(2)}, u32[]{:S(2)}) %collective-permute-start.3) | collective-permute-done | bytes 114720 | tf_op jit(solution)/shard_map/ppermute | solution.py:294
  17.6 2.9 %collective-permute-done.4.terms_ref = f32[224,128]{1,0:T(8,128)S(1)} collective-permute-done((f32[224,128]{1,0:T(8,128)S(1)}, f32[224,128]{1,0:T(8,128)S(1)}, u32[]{:S(2)}, u32[]{:S(2)}) %collective-permute-start.4) | collective-permute-done | bytes 114720 | tf_op jit(solution)/shard_map/ppermute | solution.py:294
  20.9 1.8 %collective-permute-start.5 = (f32[304,128]{1,0:T(8,128)S(1)}, f32[304,128]{1,0:T(8,128)S(1)}, u32[]{:S(2)}, u32[]{:S(2)}) collective-permute-start(f32[304,128]{1,0:T(8,128)S(1)} %more_terms.8), channel_id=1, source_target_pairs={{0,12},{1,13},{2,14},{3,15},{4,8},{5,9},{6,10},{7,11},{8,4},{9,5},... | collective-permute-start | bytes 466952 | tf_op jit(solution)/shard_map/ppermute | solution.py:294
  23.5 5.4 %collective-permute-done.5 = f32[304,128]{1,0:T(8,128)S(1)} collective-permute-done((f32[304,128]{1,0:T(8,128)S(1)}, f32[304,128]{1,0:T(8,128)S(1)}, u32[]{:S(2)}, u32[]{:S(2)}) %collective-permute-start.5) | collective-permute-done | bytes 155680 | tf_op jit(solution)/shard_map/ppermute | solution.py:294
  28.9 1.0 %collective-permute-start.8 = (f32[304,128]{1,0:T(8,128)S(1)}, f32[304,128]{1,0:T(8,128)S(1)}, u32[]{:S(2)}, u32[]{:S(2)}) collective-permute-start(f32[304,128]{1,0:T(8,128)S(1)} %add.10.refs_0_), channel_id=1, source_target_pairs={{0,6},{1,7},{2,4},{3,5},{4,2},{5,3},{6,0},{7,1},{8,14},{9,15},{10,... | collective-permute-start | bytes 466952 | tf_op jit(solution)/shard_map/ppermute | solution.py:294
  29.9 1.2 %collective-permute-start.7 = (f32[304,128]{1,0:T(8,128)S(1)}, f32[304,128]{1,0:T(8,128)S(1)}, u32[]{:S(2)}, u32[]{:S(2)}) collective-permute-start(f32[304,128]{1,0:T(8,128)S(1)} %add.10.refs_0_), channel_id=1, source_target_pairs={{0,2},{1,3},{2,0},{3,1},{4,6},{5,7},{6,4},{7,5},{8,10},{9,11},{10,... | collective-permute-start | bytes 466952 | tf_op jit(solution)/shard_map/ppermute | solution.py:294
  31.1 1.4 %collective-permute-start.6 = (f32[304,128]{1,0:T(8,128)S(1)}, f32[304,128]{1,0:T(8,128)S(1)}, u32[]{:S(2)}, u32[]{:S(2)}) collective-permute-start(f32[304,128]{1,0:T(8,128)S(1)} %add.10.refs_0_), channel_id=1, source_target_pairs={{0,4},{1,5},{2,6},{3,7},{4,0},{5,1},{6,2},{7,3},{8,12},{9,13},{10,... | collective-permute-start | bytes 466952 | tf_op jit(solution)/shard_map/ppermute | solution.py:294
  32.5 4.1 %collective-permute-done.8.refs_3_ = f32[304,128]{1,0:T(8,128)S(1)} collective-permute-done((f32[304,128]{1,0:T(8,128)S(1)}, f32[304,128]{1,0:T(8,128)S(1)}, u32[]{:S(2)}, u32[]{:S(2)}) %collective-permute-start.8) | collective-permute-done | bytes 155680 | tf_op jit(solution)/shard_map/ppermute | solution.py:294
  36.6 0.8 %collective-permute-done.7.refs_2_ = f32[304,128]{1,0:T(8,128)S(1)} collective-permute-done((f32[304,128]{1,0:T(8,128)S(1)}, f32[304,128]{1,0:T(8,128)S(1)}, u32[]{:S(2)}, u32[]{:S(2)}) %collective-permute-start.7) | collective-permute-done | bytes 155680 | tf_op jit(solution)/shard_map/ppermute | solution.py:294
  38.0 0.8 %collective-permute-done.11.refs_6_ = f32[304,128]{1,0:T(8,128)S(1)} collective-permute-done((f32[304,128]{1,0:T(8,128)S(1)}, f32[304,128]{1,0:T(8,128)S(1)}, u32[]{:S(2)}, u32[]{:S(2)}) %collective-permute-start.11) | collective-permute-done | bytes 155680 | tf_op jit(solution)/shard_map/ppermute | solution.py:294
  39.0 2.3 %next_step.1 = (f32[400,768]{1,0:T(8,128)S(1)}, f32[1,768]{1,0:T(1,128)S(1)}, f32[8,112,128]{2,1,0:T(8,128)S(1)}, f32[400,256]{1,0:T(8,128)S(1)}, f32[400,256]{1,0:T(8,128)S(1)}, /*index=5*/f32[128,256]{1,0:T(8,128)S(1)}) custom-call(s32[2]{0:T(128)S(1)} %pad_add_fusion.place_ref, f32[400,256]{1,0:T(8,128)S(1)} %get-tuple-element.42.heads_ref, ...), custom_call_target="tpu_custom_call" | custom-call | bytes 5742600 | tf_op jit(solution)/shard_map/next_step/pallas_call | solution.py:268
  41.8 1.2 %collective-permute-done.13.other_ref = f32[4,112,128]{2,1,0:T(8,128)S(1)} collective-permute-done((f32[4,112,128]{2,1,0:T(8,128)S(1)}, f32[4,112,128]{2,1,0:T(8,128)S(1)}, u32[]{:S(2)}, u32[]{:S(2)}) %collective-permute-start.13) | collective-permute-done | bytes 229408 | tf_op jit(solution)/shard_map/ppermute | solution.py:294
  43.0 1.3 %collective-permute-start.14 = (f32[224,128]{1,0:T(8,128)S(1)}, f32[224,128]{1,0:T(8,128)S(1)}, u32[]{:S(2)}, u32[]{:S(2)}) collective-permute-start(f32[224,128]{1,0:T(8,128)S(1)} %pad_maximum_fusion.3), channel_id=1, source_target_pairs={{0,2},{1,3},{2,0},{3,1},{4,6},{5,7},{6,4},{7,5},{8,10},{9,11},{10,... | collective-permute-start | bytes 344072 | tf_op jit(solution)/shard_map/ppermute | solution.py:294
  44.8 1.9 %collective-permute-start.16 = (f32[224,128]{1,0:T(8,128)S(1)}, f32[224,128]{1,0:T(8,128)S(1)}, u32[]{:S(2)}, u32[]{:S(2)}) collective-permute-start(f32[224,128]{1,0:T(8,128)S(1)} %pad_maximum_fusion.5), channel_id=1, source_target_pairs={{0,6},{1,7},{2,4},{3,5},{4,2},{5,3},{6,0},{7,1},{8,14},{9,15},{10,... | collective-permute-start | bytes 344072 | tf_op jit(solution)/shard_map/ppermute | solution.py:294
  47.1 1.3 %collective-permute-done.14.terms_ref = f32[224,128]{1,0:T(8,128)S(1)} collective-permute-done((f32[224,128]{1,0:T(8,128)S(1)}, f32[224,128]{1,0:T(8,128)S(1)}, u32[]{:S(2)}, u32[]{:S(2)}) %collective-permute-start.14) | collective-permute-done | bytes 114720 | tf_op jit(solution)/shard_map/ppermute | solution.py:294
  48.8 1.6 %collective-permute-done.15.terms_ref = f32[224,128]{1,0:T(8,128)S(1)} collective-permute-done((f32[224,128]{1,0:T(8,128)S(1)}, f32[224,128]{1,0:T(8,128)S(1)}, u32[]{:S(2)}, u32[]{:S(2)}) %collective-permute-start.15) | collective-permute-done | bytes 114720 | tf_op jit(solution)/shard_map/ppermute | solution.py:294
  50.8 1.3 %collective-permute-done.16.terms_ref = f32[224,128]{1,0:T(8,128)S(1)} collective-permute-done((f32[224,128]{1,0:T(8,128)S(1)}, f32[224,128]{1,0:T(8,128)S(1)}, u32[]{:S(2)}, u32[]{:S(2)}) %collective-permute-start.16) | collective-permute-done | bytes 114720 | tf_op jit(solution)/shard_map/ppermute | solution.py:294
  52.5 0.7 %collective-permute-start.17 = (f32[304,128]{1,0:T(8,128)S(1)}, f32[304,128]{1,0:T(8,128)S(1)}, u32[]{:S(2)}, u32[]{:S(2)}) collective-permute-start(f32[304,128]{1,0:T(8,128)S(1)} %more_terms.11), channel_id=1, source_target_pairs={{0,12},{1,13},{2,14},{3,15},{4,8},{5,9},{6,10},{7,11},{8,4},{9,5},... | collective-permute-start | bytes 466952 | tf_op jit(solution)/shard_map/ppermute | solution.py:294
  53.2 1.2 %last_update.1 = (f32[400,128]{1,0:T(8,128)}, f32[128]{0:T(128)}, f32[400,128]{1,0:T(8,128)}, f32[128]{0:T(128)}) custom-call(f32[400,128]{1,0:T(8,128)S(1)} %get-tuple-element.46.left_ref, f32[1,128]{1,0:T(1,128)S(1)} %get-tuple-element.47.lacc_ref, f32[400,256]{1,0:T(8,128)S(1)} %get-tuple-element.48.carry_ref, s32[2,256]{1,0:T(2,128)S(1)} %copy-done.2, ...), custom_call_target="tpu_custom_call" | custom-call | bytes 1777152 | tf_op jit(solution)/shard_map/last_update/pallas_call | solution.py:268
  54.5 5.2 %collective-permute-done.17 = f32[304,128]{1,0:T(8,128)S(1)} collective-permute-done((f32[304,128]{1,0:T(8,128)S(1)}, f32[304,128]{1,0:T(8,128)S(1)}, u32[]{:S(2)}, u32[]{:S(2)}) %collective-permute-start.17) | collective-permute-done | bytes 155680 | tf_op jit(solution)/shard_map/ppermute | solution.py:294
  59.7 2.6 %collective-permute-start.20 = (f32[304,128]{1,0:T(8,128)S(1)}, f32[304,128]{1,0:T(8,128)S(1)}, u32[]{:S(2)}, u32[]{:S(2)}) collective-permute-start(f32[304,128]{1,0:T(8,128)S(1)} %add.11.refs_0_), channel_id=1, source_target_pairs={{0,6},{1,7},{2,4},{3,5},{4,2},{5,3},{6,0},{7,1},{8,14},{9,15},{10,... | collective-permute-start | bytes 466952 | tf_op jit(solution)/shard_map/ppermute | solution.py:294
  62.2 1.0 %collective-permute-start.19 = (f32[304,128]{1,0:T(8,128)S(1)}, f32[304,128]{1,0:T(8,128)S(1)}, u32[]{:S(2)}, u32[]{:S(2)}) collective-permute-start(f32[304,128]{1,0:T(8,128)S(1)} %add.11.refs_0_), channel_id=1, source_target_pairs={{0,2},{1,3},{2,0},{3,1},{4,6},{5,7},{6,4},{7,5},{8,10},{9,11},{10,... | collective-permute-start | bytes 466952 | tf_op jit(solution)/shard_map/ppermute | solution.py:294
  63.3 3.1 %collective-permute-done.20.refs_3_ = f32[304,128]{1,0:T(8,128)S(1)} collective-permute-done((f32[304,128]{1,0:T(8,128)S(1)}, f32[304,128]{1,0:T(8,128)S(1)}, u32[]{:S(2)}, u32[]{:S(2)}) %collective-permute-start.20) | collective-permute-done | bytes 155680 | tf_op jit(solution)/shard_map/ppermute | solution.py:294
  66.3 1.6 %collective-permute-done.19.refs_2_ = f32[304,128]{1,0:T(8,128)S(1)} collective-permute-done((f32[304,128]{1,0:T(8,128)S(1)}, f32[304,128]{1,0:T(8,128)S(1)}, u32[]{:S(2)}, u32[]{:S(2)}) %collective-permute-start.19) | collective-permute-done | bytes 155680 | tf_op jit(solution)/shard_map/ppermute | solution.py:294
  68.5 0.8 %collective-permute-done.23.refs_6_ = f32[304,128]{1,0:T(8,128)S(1)} collective-permute-done((f32[304,128]{1,0:T(8,128)S(1)}, f32[304,128]{1,0:T(8,128)S(1)}, u32[]{:S(2)}, u32[]{:S(2)}) %collective-permute-start.23) | collective-permute-done | bytes 155680 | tf_op jit(solution)/shard_map/ppermute | solution.py:294
  69.9 1.9 %last_relations.1 = (f32[400,768]{1,0:T(8,128)}, f32[768]{0:T(1024)}) custom-call(s32[2]{0:T(128)S(1)} %pad_add_fusion.place_ref, f32[400,768]{1,0:T(8,128)S(1)} %get-tuple-element.59.rel_ref, f32[1,768]{1,0:T(1,128)S(1)} %get-tuple-element.60.relacc_ref, f32[304,128]{1,0:T(8,128)S(1)} %add.11.refs_0_, f32[304,128]{1,0:T(8,128)S(1)} %collective-permute-done.18.refs_1_, ...), custom_call_target="tpu_custom_call" | custom-call | bytes 3708936 | tf_op jit(solution)/shard_map/last_relations/pallas_call | solution.py:268
  (63 shorter events, 7.5 us)
Async XLA Ops:
  4.4 10.4 %collective-permute-start.2 = (f32[408,128]{1,0:T(8,128)S(1)}, f32[408,128]{1,0:T(8,128)S(1)}, u32[]{:S(2)}, u32[]{:S(2)}) collective-permute-start(f32[408,128]{1,0:T(8,128)S(1)} %get-tuple-element.36), channel_id=1, source_target_pairs={{12,0},{0,4},{4,8},{8,12},{13,1},{1,5},{5,9},{9,13},{14,2},{2,6},{... | collective-permute-start | bytes 626696 | tf_op jit(solution)/shard_map/ppermute | solution.py:327
  7.5 1.6 %collective-permute-start = (f32[4,112,128]{2,1,0:T(8,128)S(1)}, f32[4,112,128]{2,1,0:T(8,128)S(1)}, u32[]{:S(2)}, u32[]{:S(2)}) collective-permute-start(f32[4,112,128]{2,1,0:T(8,128)S(1)} %slice.42), channel_id=1, source_target_pairs={{0,1},{1,0},{2,3},{3,2},{4,5},{5,4},{6,7},{7,6},{8,9},{9,8},{10,11... | collective-permute-start | bytes 688136 | tf_op jit(solution)/shard_map/ppermute | solution.py:294
  9.1 5.7 %collective-permute-start.1 = (f32[224,128]{1,0:T(8,128)S(1)}, f32[224,128]{1,0:T(8,128)S(1)}, u32[]{:S(2)}, u32[]{:S(2)}) collective-permute-start(f32[224,128]{1,0:T(8,128)S(1)} %pad_maximum_fusion), channel_id=1, source_target_pairs={{0,2},{1,3},{2,0},{3,1},{4,6},{5,7},{6,4},{7,5},{8,10},{9,11},{10,... | collective-permute-start | bytes 344072 | tf_op jit(solution)/shard_map/ppermute | solution.py:294
  10.7 12.1 %copy-start.1 = (f32[128,400]{0,1:T(8,128)S(1)}, f32[128,400]{0,1:T(8,128)}, u32[]{:S(2)}) copy-start(f32[128,400]{0,1:T(8,128)} %param.10) | copy-start | bytes 614404
  10.7 12.0 %copy-start.2 = (s32[2,256]{1,0:T(2,128)S(1)}, s32[2,256]{1,0:T(2,128)}, u32[]{:S(2)}) copy-start(s32[2,256]{1,0:T(2,128)} %hid_ref.3) | copy-start | bytes 6148
  10.7 6.5 %collective-permute-start.3 = (f32[224,128]{1,0:T(8,128)S(1)}, f32[224,128]{1,0:T(8,128)S(1)}, u32[]{:S(2)}, u32[]{:S(2)}) collective-permute-start(f32[224,128]{1,0:T(8,128)S(1)} %pad_maximum_fusion.1), channel_id=1, source_target_pairs={{0,4},{1,5},{2,6},{3,7},{4,0},{5,1},{6,2},{7,3},{8,12},{9,13},{10,... | collective-permute-start | bytes 344072 | tf_op jit(solution)/shard_map/ppermute | solution.py:294
  12.4 8.2 %collective-permute-start.4 = (f32[224,128]{1,0:T(8,128)S(1)}, f32[224,128]{1,0:T(8,128)S(1)}, u32[]{:S(2)}, u32[]{:S(2)}) collective-permute-start(f32[224,128]{1,0:T(8,128)S(1)} %pad_maximum_fusion.2), channel_id=1, source_target_pairs={{0,6},{1,7},{2,4},{3,5},{4,2},{5,3},{6,0},{7,1},{8,14},{9,15},{10,... | collective-permute-start | bytes 344072 | tf_op jit(solution)/shard_map/ppermute | solution.py:294
  13.3 24.7 %copy-start.7 = (f32[768]{0:T(1024)S(1)}, f32[768]{0:T(1024)}, u32[]{:S(2)}) copy-start(f32[768]{0:T(1024)} %param.15) | copy-start | bytes 9220
  13.3 25.7 %copy-start = (f32[768,400]{0,1:T(8,128)S(1)}, f32[768,400]{0,1:T(8,128)}, u32[]{:S(2)}) copy-start(f32[768,400]{0,1:T(8,128)} %param.14) | copy-start | bytes 3686404
  13.3 25.7 %copy-start.3 = (s32[2,256]{1,0:T(2,128)S(1)}, s32[2,256]{1,0:T(2,128)}, u32[]{:S(2)}) copy-start(s32[2,256]{1,0:T(2,128)} %refs_8_.1) | copy-start | bytes 6148
  13.3 25.7 %copy-start.4 = (s32[2,256]{1,0:T(2,128)S(1)}, s32[2,256]{1,0:T(2,128)}, u32[]{:S(2)}) copy-start(s32[2,256]{1,0:T(2,128)} %refs_9_.1) | copy-start | bytes 6148
  13.3 25.7 %copy-start.5 = (s32[2,2,128]{2,1,0:T(2,128)S(1)}, s32[2,2,128]{2,1,0:T(2,128)}, u32[]{:S(2)}) copy-start(s32[2,2,128]{2,1,0:T(2,128)} %refs_10_.1) | copy-start | bytes 6148
  20.9 8.0 %collective-permute-start.5 = (f32[304,128]{1,0:T(8,128)S(1)}, f32[304,128]{1,0:T(8,128)S(1)}, u32[]{:S(2)}, u32[]{:S(2)}) collective-permute-start(f32[304,128]{1,0:T(8,128)S(1)} %more_terms.8), channel_id=1, source_target_pairs={{0,12},{1,13},{2,14},{3,15},{4,8},{5,9},{6,10},{7,11},{8,4},{9,5},... | collective-permute-start | bytes 466952 | tf_op jit(solution)/shard_map/ppermute | solution.py:294
  28.9 7.7 %collective-permute-start.8 = (f32[304,128]{1,0:T(8,128)S(1)}, f32[304,128]{1,0:T(8,128)S(1)}, u32[]{:S(2)}, u32[]{:S(2)}) collective-permute-start(f32[304,128]{1,0:T(8,128)S(1)} %add.10.refs_0_), channel_id=1, source_target_pairs={{0,6},{1,7},{2,4},{3,5},{4,2},{5,3},{6,0},{7,1},{8,14},{9,15},{10,... | collective-permute-start | bytes 466952 | tf_op jit(solution)/shard_map/ppermute | solution.py:294
  29.9 7.5 %collective-permute-start.7 = (f32[304,128]{1,0:T(8,128)S(1)}, f32[304,128]{1,0:T(8,128)S(1)}, u32[]{:S(2)}, u32[]{:S(2)}) collective-permute-start(f32[304,128]{1,0:T(8,128)S(1)} %add.10.refs_0_), channel_id=1, source_target_pairs={{0,2},{1,3},{2,0},{3,1},{4,6},{5,7},{6,4},{7,5},{8,10},{9,11},{10,... | collective-permute-start | bytes 466952 | tf_op jit(solution)/shard_map/ppermute | solution.py:294
  31.1 6.3 %collective-permute-start.6 = (f32[304,128]{1,0:T(8,128)S(1)}, f32[304,128]{1,0:T(8,128)S(1)}, u32[]{:S(2)}, u32[]{:S(2)}) collective-permute-start(f32[304,128]{1,0:T(8,128)S(1)} %add.10.refs_0_), channel_id=1, source_target_pairs={{0,4},{1,5},{2,6},{3,7},{4,0},{5,1},{6,2},{7,3},{8,12},{9,13},{10,... | collective-permute-start | bytes 466952 | tf_op jit(solution)/shard_map/ppermute | solution.py:294
  32.5 5.4 %collective-permute-start.9 = (f32[304,128]{1,0:T(8,128)S(1)}, f32[304,128]{1,0:T(8,128)S(1)}, u32[]{:S(2)}, u32[]{:S(2)}) collective-permute-start(f32[304,128]{1,0:T(8,128)S(1)} %add.10.refs_0_), channel_id=1, source_target_pairs={{0,1},{1,0},{2,3},{3,2},{4,5},{5,4},{6,7},{7,6},{8,9},{9,8},{10,11... | collective-permute-start | bytes 466952 | tf_op jit(solution)/shard_map/ppermute | solution.py:294
  36.6 1.4 %collective-permute-start.12 = (f32[304,128]{1,0:T(8,128)S(1)}, f32[304,128]{1,0:T(8,128)S(1)}, u32[]{:S(2)}, u32[]{:S(2)}) collective-permute-start(f32[304,128]{1,0:T(8,128)S(1)} %collective-permute-done.8.refs_3_), channel_id=1, source_target_pairs={{0,1},{1,0},{2,3},{3,2},{4,5},{5,4},{6,7},{7,6},{8,9},{9,8},{10,11... | collective-permute-start | bytes 466952 | tf_op jit(solution)/shard_map/ppermute | solution.py:294
  37.4 1.4 %collective-permute-start.11 = (f32[304,128]{1,0:T(8,128)S(1)}, f32[304,128]{1,0:T(8,128)S(1)}, u32[]{:S(2)}, u32[]{:S(2)}) collective-permute-start(f32[304,128]{1,0:T(8,128)S(1)} %collective-permute-done.7.refs_2_), channel_id=1, source_target_pairs={{0,1},{1,0},{2,3},{3,2},{4,5},{5,4},{6,7},{7,6},{8,9},{9,8},{10,11... | collective-permute-start | bytes 466952 | tf_op jit(solution)/shard_map/ppermute | solution.py:294
  37.4 1.6 %collective-permute-start.10 = (f32[304,128]{1,0:T(8,128)S(1)}, f32[304,128]{1,0:T(8,128)S(1)}, u32[]{:S(2)}, u32[]{:S(2)}) collective-permute-start(f32[304,128]{1,0:T(8,128)S(1)} %collective-permute-done.6.refs_1_), channel_id=1, source_target_pairs={{0,1},{1,0},{2,3},{3,2},{4,5},{5,4},{6,7},{7,6},{8,9},{9,8},{10,11... | collective-permute-start | bytes 466952 | tf_op jit(solution)/shard_map/ppermute | solution.py:294
  41.4 1.6 %collective-permute-start.13 = (f32[4,112,128]{2,1,0:T(8,128)S(1)}, f32[4,112,128]{2,1,0:T(8,128)S(1)}, u32[]{:S(2)}, u32[]{:S(2)}) collective-permute-start(f32[4,112,128]{2,1,0:T(8,128)S(1)} %slice.49), channel_id=1, source_target_pairs={{0,1},{1,0},{2,3},{3,2},{4,5},{5,4},{6,7},{7,6},{8,9},{9,8},{10,11... | collective-permute-start | bytes 688136 | tf_op jit(solution)/shard_map/ppermute | solution.py:294
  43.0 5.4 %collective-permute-start.14 = (f32[224,128]{1,0:T(8,128)S(1)}, f32[224,128]{1,0:T(8,128)S(1)}, u32[]{:S(2)}, u32[]{:S(2)}) collective-permute-start(f32[224,128]{1,0:T(8,128)S(1)} %pad_maximum_fusion.3), channel_id=1, source_target_pairs={{0,2},{1,3},{2,0},{3,1},{4,6},{5,7},{6,4},{7,5},{8,10},{9,11},{10,... | collective-permute-start | bytes 344072 | tf_op jit(solution)/shard_map/ppermute | solution.py:294
  44.3 6.1 %collective-permute-start.15 = (f32[224,128]{1,0:T(8,128)S(1)}, f32[224,128]{1,0:T(8,128)S(1)}, u32[]{:S(2)}, u32[]{:S(2)}) collective-permute-start(f32[224,128]{1,0:T(8,128)S(1)} %pad_maximum_fusion.4), channel_id=1, source_target_pairs={{0,4},{1,5},{2,6},{3,7},{4,0},{5,1},{6,2},{7,3},{8,12},{9,13},{10,... | collective-permute-start | bytes 344072 | tf_op jit(solution)/shard_map/ppermute | solution.py:294
  44.8 7.3 %collective-permute-start.16 = (f32[224,128]{1,0:T(8,128)S(1)}, f32[224,128]{1,0:T(8,128)S(1)}, u32[]{:S(2)}, u32[]{:S(2)}) collective-permute-start(f32[224,128]{1,0:T(8,128)S(1)} %pad_maximum_fusion.5), channel_id=1, source_target_pairs={{0,6},{1,7},{2,4},{3,5},{4,2},{5,3},{6,0},{7,1},{8,14},{9,15},{10,... | collective-permute-start | bytes 344072 | tf_op jit(solution)/shard_map/ppermute | solution.py:294
  52.5 7.2 %collective-permute-start.17 = (f32[304,128]{1,0:T(8,128)S(1)}, f32[304,128]{1,0:T(8,128)S(1)}, u32[]{:S(2)}, u32[]{:S(2)}) collective-permute-start(f32[304,128]{1,0:T(8,128)S(1)} %more_terms.11), channel_id=1, source_target_pairs={{0,12},{1,13},{2,14},{3,15},{4,8},{5,9},{6,10},{7,11},{8,4},{9,5},... | collective-permute-start | bytes 466952 | tf_op jit(solution)/shard_map/ppermute | solution.py:294
  59.7 6.7 %collective-permute-start.20 = (f32[304,128]{1,0:T(8,128)S(1)}, f32[304,128]{1,0:T(8,128)S(1)}, u32[]{:S(2)}, u32[]{:S(2)}) collective-permute-start(f32[304,128]{1,0:T(8,128)S(1)} %add.11.refs_0_), channel_id=1, source_target_pairs={{0,6},{1,7},{2,4},{3,5},{4,2},{5,3},{6,0},{7,1},{8,14},{9,15},{10,... | collective-permute-start | bytes 466952 | tf_op jit(solution)/shard_map/ppermute | solution.py:294
  62.2 5.7 %collective-permute-start.19 = (f32[304,128]{1,0:T(8,128)S(1)}, f32[304,128]{1,0:T(8,128)S(1)}, u32[]{:S(2)}, u32[]{:S(2)}) collective-permute-start(f32[304,128]{1,0:T(8,128)S(1)} %add.11.refs_0_), channel_id=1, source_target_pairs={{0,2},{1,3},{2,0},{3,1},{4,6},{5,7},{6,4},{7,5},{8,10},{9,11},{10,... | collective-permute-start | bytes 466952 | tf_op jit(solution)/shard_map/ppermute | solution.py:294
  63.3 5.2 %collective-permute-start.18 = (f32[304,128]{1,0:T(8,128)S(1)}, f32[304,128]{1,0:T(8,128)S(1)}, u32[]{:S(2)}, u32[]{:S(2)}) collective-permute-start(f32[304,128]{1,0:T(8,128)S(1)} %add.11.refs_0_), channel_id=1, source_target_pairs={{0,4},{1,5},{2,6},{3,7},{4,0},{5,1},{6,2},{7,3},{8,12},{9,13},{10,... | collective-permute-start | bytes 466952 | tf_op jit(solution)/shard_map/ppermute | solution.py:294
  63.3 5.2 %collective-permute-start.21 = (f32[304,128]{1,0:T(8,128)S(1)}, f32[304,128]{1,0:T(8,128)S(1)}, u32[]{:S(2)}, u32[]{:S(2)}) collective-permute-start(f32[304,128]{1,0:T(8,128)S(1)} %add.11.refs_0_), channel_id=1, source_target_pairs={{0,1},{1,0},{2,3},{3,2},{4,5},{5,4},{6,7},{7,6},{8,9},{9,8},{10,11... | collective-permute-start | bytes 466952 | tf_op jit(solution)/shard_map/ppermute | solution.py:294
  66.3 2.2 %collective-permute-start.24 = (f32[304,128]{1,0:T(8,128)S(1)}, f32[304,128]{1,0:T(8,128)S(1)}, u32[]{:S(2)}, u32[]{:S(2)}) collective-permute-start(f32[304,128]{1,0:T(8,128)S(1)} %collective-permute-done.20.refs_3_), channel_id=1, source_target_pairs={{0,1},{1,0},{2,3},{3,2},{4,5},{5,4},{6,7},{7,6},{8,9},{9,8},{10,11... | collective-permute-start | bytes 466952 | tf_op jit(solution)/shard_map/ppermute | solution.py:294
  68.0 1.4 %collective-permute-start.23 = (f32[304,128]{1,0:T(8,128)S(1)}, f32[304,128]{1,0:T(8,128)S(1)}, u32[]{:S(2)}, u32[]{:S(2)}) collective-permute-start(f32[304,128]{1,0:T(8,128)S(1)} %collective-permute-done.19.refs_2_), channel_id=1, source_target_pairs={{0,1},{1,0},{2,3},{3,2},{4,5},{5,4},{6,7},{7,6},{8,9},{9,8},{10,11... | collective-permute-start | bytes 466952 | tf_op jit(solution)/shard_map/ppermute | solution.py:294
  68.5 1.4 %collective-permute-start.22 = (f32[304,128]{1,0:T(8,128)S(1)}, f32[304,128]{1,0:T(8,128)S(1)}, u32[]{:S(2)}, u32[]{:S(2)}) collective-permute-start(f32[304,128]{1,0:T(8,128)S(1)} %collective-permute-done.18.refs_1_), channel_id=1, source_target_pairs={{0,1},{1,0},{2,3},{3,2},{4,5},{5,4},{6,7},{7,6},{8,9},{9,8},{10,11... | collective-permute-start | bytes 466952 | tf_op jit(solution)/shard_map/ppermute | solution.py:294
  (1 other events, 12.0 us)

commit v4 on v3

--- a/solution.py
+++ b/solution.py
@@ -53,28 +53,45 @@
     return weights - grads * (RATE / jnp.sqrt(accum)), accum
 
 
-def score(right, rel_rows, heads, tail_ids, negative):
+def prepare(right, tail_ids, negative):
     rows = right.shape[1]
     count, negs = negative.shape
-    query = heads * rel_rows
-    scores = times(nn, right.T, query)
+    named = []
+    for c in range(count):
+        hits = lax.broadcasted_iota(jnp.int32, (rows, negs), 0) == negative[c : c + 1]
+        share = jnp.sum(hits.astype(F32), axis=1, keepdims=True) * (1.0 / negs)
+        named.append(jnp.broadcast_to(share, (rows, tail_ids.shape[1] // count)))
+    return jnp.concatenate(named, axis=1), selector(tail_ids, rows)
+
+
+def split_times(dot, a_both, b):
+    rows = a_both.shape[0] // 2
+    b_high, b_low = halves(b)
+    both = dot(a_both, b_high)
+    return both[:rows] + (both[rows:] + dot(a_both[:rows], b_low))
+
+
+def stack(x):
+    return jnp.concatenate(halves(x), axis=0)
+
+
+def score(right_turned, query, named, tail_sel):
+    scores = split_times(nn, right_turned, query)
     tiny = jnp.exp(-jnp.abs(scores))
     inverse = 1.0 / (1.0 + tiny)
     up = scores >= 0
     sig = jnp.where(up, 1.0, tiny) * inverse
     sig_minus = jnp.where(up, tiny, 1.0) * inverse
-    named = []
-    for c in range(count):
-        hits = lax.broadcasted_iota(jnp.int32, (rows, negs), 0) == negative[c : c + 1]
-        share = jnp.sum(hits.astype(F32), axis=1, keepdims=True) * (1.0 / negs)
-        named.append(jnp.broadcast_to(share, (rows, query.shape[1] // count)))
-    weight = jnp.concatenate(named, axis=1) * sig - selector(tail_ids, rows) * sig_minus
-    return query, weight
+    return named * sig - tail_sel * sig_minus
 
 
 def cut(width):
     main = width // (8 * PIECES) * 8
     return main, width // PIECES - main
+
+
+def piece_rows(width, kinds):
+    return -(-(width // PIECES) * kinds // LANES // 8) * 8
 
 
 def put_terms(place_ref, terms, kinds, out_ref):
@@ -183,44 +200,88 @@
         copy.wait()
     right = right_ref[...]
     rel_rows = times_selector(nn, rel_ref[...], kind_sel)
-    query, weight = score(right, rel_rows, heads, tid_ref[0:1], nid_ref[0])
+    query = heads * rel_rows
+    weight = score(stack(right.T), query, *prepare(right, tid_ref[0:1], nid_ref[0]))
     grad_query = times(nn, right, weight)
     put_terms(place_ref, grad_query * heads, kid_ref[0:1], terms_out)
     put_packed(right_out, *adagrad(right, racc_ref[...], times(nt, query, weight)))
     carry_out[...] = grad_query * rel_rows
 
 
-def left_kernel(step, left_ref, lacc_ref, carry_ref, hid_ref, left_out, lacc_out, heads_out):
-    rows = left_ref.shape[1]
-    grad = times_selector(nt, carry_ref[...], selector(hid_ref[step : step + 1], rows).astype(BF16))
+def ready_kernel(
+    step, left_ref, lacc_ref, carry_ref, right_ref, rel_ref, relacc_ref, hid_ref, tid_ref, kid_ref, nid_ref,
+    left_out, lacc_out, heads_out, turned_out, right_out, named_out, tail_out, kind_out, rows_out, state_out,
+):
+    width, rows = left_ref.shape
+    grad = times_selector(nt, carry_ref[...], selector(hid_ref[step - 1 : step], rows).astype(BF16))
     left, lacc_out[...] = adagrad(left_ref[...], lacc_ref[...], grad)
     left_out[...] = left
-    heads_out[...] = times_selector(nn, left, selector(hid_ref[step + 1 : step + 2], rows).astype(BF16))
-
-
-def next_kernel(step, place_ref, heads_ref, right_ref, rel_ref, relacc_ref, *refs):
-    piece_refs, (tid_ref, kid_ref, nid_ref) = refs[:PIECES], refs[PIECES : PIECES + 3]
-    rel_out, relacc_out, terms_out, carry_out, query_out, weight_out, all_ref, split_ref = refs[PIECES + 3 :]
-    width = heads_ref.shape[0]
-    order_pieces(place_ref, piece_refs, all_ref)
-    relacc_out[...], rate = next_accum(relacc_ref, all_ref, width)
-    blocks = rel_ref.shape[1] // LANES
-    for j in range(blocks):
-        lanes = slice(LANES * j, LANES * (j + 1))
-        rel = rel_ref[:, lanes] - take_rel_grad(all_ref, j, width, blocks) * rate[:, lanes]
-        rel_out[:, lanes] = rel
-        split_ref[:width, lanes], split_ref[width:, lanes] = halves(rel)
+    heads_out[...] = times_selector(nn, left, selector(hid_ref[step : step + 1], rows).astype(BF16))
+    right = right_ref[:width]
+    turned_out[...] = stack(right.T)
+    right_out[...] = stack(right)
+    named_out[...], tail_out[...] = prepare(right, tid_ref[step : step + 1], nid_ref[step])
     kind_sel = selector(kid_ref[step : step + 1], rel_ref.shape[1]).astype(BF16)
+    kind_out[...] = kind_sel
+    state = jnp.broadcast_to(relacc_ref[...], (8, rel_ref.shape[1]))
+    rel_rows = times_selector(nn, jnp.concatenate([rel_ref[...], state], axis=0), kind_sel)
+    rows_out[...] = rel_rows[:width]
+    state_out[...] = rel_rows[width : width + 1]
+
+
+def gather_pieces(piece_refs, kind_sel, width):
+    main, rest = cut(width)
+    blocks = kind_sel.shape[0] // LANES
+    mains = [jnp.concatenate([ref[main * j : main * (j + 1)] for j in range(blocks)], axis=1) for ref in piece_refs]
+    first = main * blocks
+    rests = [
+        jnp.concatenate([ref[first + rest * j : first + rest * (j + 1)] for j in range(blocks)], axis=1)
+        for ref in piece_refs
+    ]
+    return times_selector(nn, jnp.concatenate(mains + rests, axis=0), kind_sel)
+
+
+def gather_kernel(width, *refs):
+    refs[-1][...] = gather_pieces(refs[:-2], refs[-2][...], width)
+
+
+def next_kernel(step, place_ref, heads_ref, turned_ref, right_ref, named_ref, tail_ref, kind_ref, rows_ref, *refs):
+    state_ref, mine_ref, piece_refs, kid_ref = refs[0], refs[1], refs[2 : 2 + PIECES // 2], refs[2 + PIECES // 2]
+    terms_out, carry_out, query_out, weight_out, main_ref, rest_ref = refs[3 + PIECES // 2 :]
     heads = heads_ref[...]
-    both = nn(split_ref[...], kind_sel)
-    rel_rows = both[:width] + both[width:]
-    right = right_ref[:width]
-    query, weight = score(right, rel_rows, heads, tid_ref[step : step + 1], nid_ref[step])
-    grad_query = times(nn, right, weight)
+    width = heads.shape[0]
+    square, core = place_ref[0], place_ref[1]
+    half = PIECES // 2
+    main, rest = cut(width)
+    theirs = gather_pieces(piece_refs, kind_ref[...], width)
+    for first, columns in ((core * half, mine_ref[...]), ((1 - core) * half, theirs)):
+        for i in range(half):
+            at = first + jnp.bitwise_xor(square, i)
+            last = main * half + rest * i
+            main_ref[at] = columns[main * i : main * (i + 1)]
+            rest_ref[at, :rest] = columns[last : last + rest]
+    grad = jnp.concatenate([main_ref[c] for c in range(PIECES)] + [rest_ref[c, :rest] for c in range(PIECES)], axis=0)
+    state = state_ref[...] + jnp.sum(grad * grad, axis=0, keepdims=True) * (1.0 / width)
+    rel_rows = rows_ref[...] - grad * (RATE / jnp.sqrt(state))
+    query = heads * rel_rows
+    weight = score(turned_ref[...], query, named_ref[...], tail_ref[...])
+    grad_query = split_times(nn, right_ref[...], weight)
     put_terms(place_ref, grad_query * heads, kid_ref[step : step + 1], terms_out)
     carry_out[...] = grad_query * rel_rows
     query_out[...] = query
     weight_out[...] = weight
+
+
+def relations_kernel(place_ref, rel_ref, relacc_ref, *refs):
+    piece_refs, (rel_out, relacc_out, all_ref) = refs[:PIECES], refs[PIECES:]
+    width = rel_ref.shape[0]
+    order_pieces(place_ref, piece_refs, all_ref)
+    accum, rate = next_accum(relacc_ref, all_ref, width)
+    relacc_out[...] = accum[0] if len(relacc_out.shape) == 1 else accum
+    blocks = rel_ref.shape[1] // LANES
+    for j in range(blocks):
+        lanes = slice(LANES * j, LANES * (j + 1))
+        rel_out[:, lanes] = rel_ref[:, lanes] - take_rel_grad(all_ref, j, width, blocks) * rate[:, lanes]
 
 
 def right_kernel(right_ref, query_ref, weight_ref, right_out):
@@ -243,18 +304,6 @@
     racc_out[...] = acc[0]
 
 
-def last_kernel(place_ref, rel_ref, relacc_ref, *refs):
-    piece_refs, (rel_out, relacc_out, all_ref) = refs[:PIECES], refs[PIECES:]
-    width = rel_ref.shape[0]
-    order_pieces(place_ref, piece_refs, all_ref)
-    accum, rate = next_accum(relacc_ref, all_ref, width)
-    relacc_out[...] = accum[0]
-    blocks = rel_ref.shape[1] // LANES
-    for j in range(blocks):
-        lanes = slice(LANES * j, LANES * (j + 1))
-        rel_out[:, lanes] = rel_ref[:, lanes] - take_rel_grad(all_ref, j, width, blocks) * rate[:, lanes]
-
-
 HBM = pl.BlockSpec(memory_space=pltpu.HBM)
 VMEM = pl.BlockSpec(memory_space=pltpu.VMEM)
 SMEM = pl.BlockSpec(memory_space=pltpu.SMEM)
@@ -263,11 +312,11 @@
 
 def call(kernel, outs, scratch=(), smem=0, hbm_outs=(), name=None, flops=0):
     def run(*given):
-        moved = sum(math.prod(x.shape) for x in given) + sum(math.prod(shape) for shape in outs)
+        moved = sum(math.prod(x.shape) for x in given) + sum(math.prod(getattr(shape, "shape", shape)) for shape in outs)
         in_specs = [SMEM if i < smem else VMEM for i in range(len(given))]
         return pl.pallas_call(
             kernel,
-            out_shape=[jax.ShapeDtypeStruct(shape, F32) for shape in outs],
+            out_shape=[jax.ShapeDtypeStruct(shape, F32) if isinstance(shape, tuple) else shape for shape in outs],
             in_specs=in_specs,
             out_specs=[HBM if i in hbm_outs else VMEM for i in range(len(outs))],
             scratch_shapes=list(scratch),
@@ -298,16 +347,21 @@
     return jnp.bitwise_and(jnp.bitwise_xor(i, i >> 1), 1)
 
 
-def sum_pieces(terms, sizes, width, kinds, beside=(), aside=()):
+def sum_pieces(terms, sizes, width, kinds, beside=None, work=lambda _: ()):
     half = PIECES // 2
-    piece = (-(-(width // PIECES) * kinds // LANES // 8) * 8, LANES)
-    other = swap(terms[half:], sizes, sub=1)
+    piece = (piece_rows(width, kinds), LANES)
+    sent = terms[half:]
+    if beside is not None:
+        sent, beside = lax.optimization_barrier((sent, beside))
+        beside = from_behind(beside, "blk")
+    other = swap(sent, sizes, sub=1)
     got = [
         swap(jnp.concatenate([terms[i], other[i]], axis=0), sizes, blk=i & 1, shard=i >> 1) for i in range(1, half)
     ]
-    got[1], beside = lax.optimization_barrier((got[1], beside))
+    if beside is not None:
+        got[1], beside = lax.optimization_barrier((got[1], beside))
     total = call(functools.partial(chip_kernel, width, kinds), [piece], name="chip_terms")(terms, other)[0]
-    for more in (got[1], got[0], got[2]):
+    for more in (got[1], got[2], got[0]):
         total = call(functools.partial(more_kernel, width, kinds), [piece], name="more_terms")(total, more)[0]
     reach = 4
     while reach <= sizes[0]:
@@ -317,7 +371,7 @@
     while reach <= sizes[1]:
         total = total + swap(total, sizes, shard=reach - 1)
         reach *= 2
-    total, aside = lax.optimization_barrier((total, aside))
+    total, aside = lax.optimization_barrier((total, work(beside)))
     mine = [total] + [swap(total, sizes, blk=i & 1, shard=i >> 1) for i in range(1, half)]
     return mine + [swap(x, sizes, sub=1) for x in mine], beside, aside
 
@@ -353,33 +407,53 @@
         compiler_params=PARAMS,
         name="first_step",
     )(place, *[pltpu.with_memory_space_constraint(x, pltpu.HBM) for x in given])
-    all_pieces = pltpu.VMEM((PIECES, -(-(width // PIECES) * kinds // LANES // 8) * 8, LANES), F32)
+    all_pieces = pltpu.VMEM((PIECES, piece_rows(width, kinds), LANES), F32)
+    half = PIECES // 2
+    main, rest = cut(width)
+
+    def short(*shape):
+        return jax.ShapeDtypeStruct(shape, BF16)
+
+    def relations(rel, relacc, summed, shape, name):
+        return call(relations_kernel, [(width, kinds), shape], [all_pieces], smem=1, name=name)(
+            place, rel, relacc, *summed
+        )
+
+    summed = None
     for step in range(1, steps):
         if step > 1:
-            right = call(right_kernel, [(width + 8, rows)])(right, query, weight)
-        right = from_behind(right, "blk")
-        left, lacc, heads = call(functools.partial(left_kernel, step - 1), [table, state, each], name="left_update")(
-            left, lacc, carry, head_ids
+            right = call(right_kernel, [(width + 8, rows)])(right, query, weight)[0]
+
+        def ready(right, step=step, rel=rel, relacc=relacc, summed=summed):
+            if summed is not None:
+                rel, relacc = relations(rel, relacc, summed, (1, kinds), "relations")
+            outs = [table, state, each, short(2 * rows, width), short(2 * width, rows), (rows, edges), (rows, edges)]
+            outs += [short(kinds, edges), each, (1, edges)]
+            return rel, relacc, *call(functools.partial(ready_kernel, step), outs, name="ready")(
+                left, lacc, carry, right, rel, relacc, head_ids, tail_ids, rel_ids, neg_ids
+            )
+
+        summed, right, (rel, relacc, left, lacc, heads, turned, both, named, tail_sel, kind_sel, rel_rows, rel_state) = (
+            sum_pieces(terms, sizes, width, kinds, right, ready)
         )
-        summed, right, (left, lacc, heads) = sum_pieces(terms, sizes, width, kinds, right, (left, lacc, heads))
-        rel, relacc, terms, carry, query, weight = call(
+        mine = call(functools.partial(gather_kernel, width), [(half * (main + rest), edges)], name="gather")(
+            *summed[:half], kind_sel
+        )[0]
+        terms, carry, query, weight = call(
             functools.partial(next_kernel, step),
-            [(width, kinds), (1, kinds), cut_terms, each, each, (rows, edges)],
-            [all_pieces, pltpu.VMEM((2 * width, kinds), BF16)],
+            [cut_terms, each, each, (rows, edges)],
+            [pltpu.VMEM((PIECES, main, edges), F32), pltpu.VMEM((PIECES, 8, edges), F32)],
             smem=1,
             name="next_step",
-        )(place, heads, right, rel, relacc, *summed, tail_ids, rel_ids, neg_ids)
-    updated = call(
-        functools.partial(update_kernel, steps - 1), [table, (rows,), table, (rows,)], name="last_update"
-    )(left, lacc, carry, head_ids, right, query, weight)
-    summed, _, (left, lacc, right, racc) = sum_pieces(terms, sizes, width, kinds, aside=updated)
-    rel, relacc = call(
-        last_kernel,
-        [(width, kinds), (kinds,)],
-        [all_pieces],
-        smem=1,
-        name="last_relations",
-    )(place, rel, relacc, *summed)
+        )(place, heads, turned, both, named, tail_sel, kind_sel, rel_rows, rel_state, mine, *summed[half:], rel_ids)
+
+    def update(_):
+        return *relations(rel, relacc, summed, (1, kinds), "relations"), *call(
+            functools.partial(update_kernel, steps - 1), [table, (rows,), table, (rows,)], name="last_update"
+        )(left, lacc, carry, head_ids, right, query, weight)
+
+    last, _, (rel, relacc, left, lacc, right, racc) = sum_pieces(terms, sizes, width, kinds, work=update)
+    rel, relacc = relations(rel, relacc, last, (kinds,), "last_relations")
     return (left.T, lacc, right.T, racc, rel.T, relacc)
 
 

time: 72 us -> 71.1 us (0.987)
  waiting for transfers between devices: 36.5 us -> 35.3 us
  Pallas kernels: 13.1 us -> 14.3 us
  starting transfers between devices: 21.1 us -> 20.1 us
    ppermute x24, waiting for transfers between devices: 35 us -> 33.7 us  [swap(): return lax.ppermute(x, AXES, route)]
    pallas_call x12 -> x14, Pallas kernels: 9.35 us -> 10.6 us  [run(): pl.pallas_call(kernel, out_shape=[jax.ShapeDtypeStruct(shape, F32) if isi...]
    ppermute x24, starting transfers between devices: 18 us -> 17 us  [swap(): return lax.ppermute(x, AXES, route)]
  transfers between devices with their start and end apart: 25 -> 25, of which waited for: 20 -> 19; matrix products, arithmetic and copies ran while one was open for 0% -> 0% of each run, Pallas kernels for 6% -> 8%
where the time goes in v4:
time: 71.1 us; the launch traced here: 70.9 us
  waiting for transfers between devices  35.3 us (50%)
  starting transfers between devices  20.1 us (28%)
  Pallas kernels  14.3 us (20%)
  between operations  0.97 us (1%)
    ppermute x24, waiting for transfers between devices, swap(): return lax.ppermute(x, AXES, route)  33.7 us
    ppermute x24, starting transfers between devices, swap(): return lax.ppermute(x, AXES, route)  17 us
    pallas_call x14, Pallas kernels, run(): pl.pallas_call(kernel, out_shape=[jax.ShapeDtypeStruct(shape, F32) if isi...  10.6 us
    pallas_call x1, Pallas kernels, shards(): pl.pallas_call(first_kernel, out_shape=[jax.ShapeDtypeStruct(shape, F32)...  3.7 us
    ppermute x1, starting transfers between devices, from_behind(): return lax.ppermute(block, axis, [((i - 1) % n, i) for i in range(n)])  3.07 us
    ppermute x1, waiting for transfers between devices, from_behind(): return lax.ppermute(block, axis, [((i - 1) % n, i) for i in range(n)])  1.57 us
  transfers between devices with their start and end apart: 25, of which 19 were waited for; matrix products, arithmetic and copies ran while one was open for 0% of the time, Pallas kernels for 8%

profile of v4, /device:TPU:0, one launch (start us, length us, event | category | flops | bytes accessed | tf_op | source)
XLA Modules:
  0.0 70.9 jit_solution(10207425976764862465)
XLA Ops:
  0.7 3.7 %first_step.1 = (f32[408,128]{1,0:T(8,128)S(1)}, f32[8,112,128]{2,1,0:T(8,128)S(1)}, f32[400,256]{1,0:T(8,128)S(1)}) custom-call(s32[2]{0:T(128)S(1)} %pad_add_fusion.place_ref, s32[2,256]{1,0:T(2,128)} %hid_ref.3, s32[2,256]{1,0:T(2,128)} %tid_ref.1, s32[2,256]{1,0:T(2,128)} %refs_6_.1, s32[2,2,128]{2,1,0:T(2,128)} %nid_ref.1, f32[400,128]{1,0:T(8,128)} %bitcast.37, ...), custom_call_target="tpu_custom_call" | custom-call | tf_op jit(solution)/shard_map/first_step/pallas_call | solution.py:401
  4.5 3.1 %collective-permute-start.2 = (f32[408,128]{1,0:T(8,128)S(1)}, f32[408,128]{1,0:T(8,128)S(1)}, u32[]{:S(2)}, u32[]{:S(2)}) collective-permute-start(f32[408,128]{1,0:T(8,128)S(1)} %get-tuple-element.58), channel_id=1, source_target_pairs={{12,0},{0,4},{4,8},{8,12},{13,1},{1,5},{5,9},{9,13},{14,2},{2,6},{... | collective-permute-start | bytes 626696 | tf_op jit(solution)/shard_map/ppermute | solution.py:381
  7.5 1.5 %collective-permute-done.other_ref = f32[4,112,128]{2,1,0:T(8,128)S(1)} collective-permute-done((f32[4,112,128]{2,1,0:T(8,128)S(1)}, f32[4,112,128]{2,1,0:T(8,128)S(1)}, u32[]{:S(2)}, u32[]{:S(2)}) %collective-permute-start) | collective-permute-done | bytes 229408 | tf_op jit(solution)/shard_map/ppermute | solution.py:343
  9.0 1.6 %collective-permute-start.1 = (f32[224,128]{1,0:T(8,128)S(1)}, f32[224,128]{1,0:T(8,128)S(1)}, u32[]{:S(2)}, u32[]{:S(2)}) collective-permute-start(f32[224,128]{1,0:T(8,128)S(1)} %pad_maximum_fusion), channel_id=1, source_target_pairs={{0,2},{1,3},{2,0},{3,1},{4,6},{5,7},{6,4},{7,5},{8,10},{9,11},{10,... | collective-permute-start | bytes 344072 | tf_op jit(solution)/shard_map/ppermute | solution.py:343
  10.7 1.6 %collective-permute-start.3 = (f32[224,128]{1,0:T(8,128)S(1)}, f32[224,128]{1,0:T(8,128)S(1)}, u32[]{:S(2)}, u32[]{:S(2)}) collective-permute-start(f32[224,128]{1,0:T(8,128)S(1)} %pad_maximum_fusion.1), channel_id=1, source_target_pairs={{0,6},{1,7},{2,4},{3,5},{4,2},{5,3},{6,0},{7,1},{8,14},{9,15},{10,... | collective-permute-start | bytes 344072 | tf_op jit(solution)/shard_map/ppermute | solution.py:343
  13.2 1.6 %collective-permute-done.2.right_ref = f32[408,128]{1,0:T(8,128)S(1)} collective-permute-done((f32[408,128]{1,0:T(8,128)S(1)}, f32[408,128]{1,0:T(8,128)S(1)}, u32[]{:S(2)}, u32[]{:S(2)}) %collective-permute-start.2) | collective-permute-done | bytes 208928 | tf_op jit(solution)/shard_map/ppermute | solution.py:381
  15.2 3.0 %collective-permute-done.3.terms_ref = f32[224,128]{1,0:T(8,128)S(1)} collective-permute-done((f32[224,128]{1,0:T(8,128)S(1)}, f32[224,128]{1,0:T(8,128)S(1)}, u32[]{:S(2)}, u32[]{:S(2)}) %collective-permute-start.3) | collective-permute-done | bytes 114720 | tf_op jit(solution)/shard_map/ppermute | solution.py:343
  18.6 1.0 %collective-permute-done.4.terms_ref = f32[224,128]{1,0:T(8,128)S(1)} collective-permute-done((f32[224,128]{1,0:T(8,128)S(1)}, f32[224,128]{1,0:T(8,128)S(1)}, u32[]{:S(2)}, u32[]{:S(2)}) %collective-permute-start.4) | collective-permute-done | bytes 114720 | tf_op jit(solution)/shard_map/ppermute | solution.py:343
  20.0 1.8 %collective-permute-start.5 = (f32[304,128]{1,0:T(8,128)S(1)}, f32[304,128]{1,0:T(8,128)S(1)}, u32[]{:S(2)}, u32[]{:S(2)}) collective-permute-start(f32[304,128]{1,0:T(8,128)S(1)} %more_terms.8), channel_id=1, source_target_pairs={{0,12},{1,13},{2,14},{3,15},{4,8},{5,9},{6,10},{7,11},{8,4},{9,5},... | collective-permute-start | bytes 466952 | tf_op jit(solution)/shard_map/ppermute | solution.py:343
  21.9 1.1 %ready.1 = (f32[400,128]{1,0:T(8,128)S(1)}, f32[1,128]{1,0:T(1,128)S(1)}, f32[400,256]{1,0:T(8,128)S(1)}, bf16[256,400]{1,0:T(8,128)(2,1)S(1)}, bf16[800,128]{1,...) custom-call(f32[400,128]{1,0:T(8,128)S(1)} %bitcast.38, ...), custom_call_target="tpu_custom_call" | custom-call | bytes 4957184 | tf_op jit(solution)/shard_map/ready/pallas_call | solution.py:317
  23.0 4.9 %collective-permute-done.5 = f32[304,128]{1,0:T(8,128)S(1)} collective-permute-done((f32[304,128]{1,0:T(8,128)S(1)}, f32[304,128]{1,0:T(8,128)S(1)}, u32[]{:S(2)}, u32[]{:S(2)}) %collective-permute-start.5) | collective-permute-done | bytes 155680 | tf_op jit(solution)/shard_map/ppermute | solution.py:343
  28.0 2.0 %collective-permute-start.8 = (f32[304,128]{1,0:T(8,128)S(1)}, f32[304,128]{1,0:T(8,128)S(1)}, u32[]{:S(2)}, u32[]{:S(2)}) collective-permute-start(f32[304,128]{1,0:T(8,128)S(1)} %add.10.refs_0_), channel_id=1, source_target_pairs={{0,6},{1,7},{2,4},{3,5},{4,2},{5,3},{6,0},{7,1},{8,14},{9,15},{10,... | collective-permute-start | bytes 466952 | tf_op jit(solution)/shard_map/ppermute | solution.py:343
  30.5 1.0 %collective-permute-start.6 = (f32[304,128]{1,0:T(8,128)S(1)}, f32[304,128]{1,0:T(8,128)S(1)}, u32[]{:S(2)}, u32[]{:S(2)}) collective-permute-start(f32[304,128]{1,0:T(8,128)S(1)} %add.10.refs_0_), channel_id=1, source_target_pairs={{0,4},{1,5},{2,6},{3,7},{4,0},{5,1},{6,2},{7,3},{8,12},{9,13},{10,... | collective-permute-start | bytes 466952 | tf_op jit(solution)/shard_map/ppermute | solution.py:343
  31.5 4.2 %collective-permute-done.8.refs_3_ = f32[304,128]{1,0:T(8,128)S(1)} collective-permute-done((f32[304,128]{1,0:T(8,128)S(1)}, f32[304,128]{1,0:T(8,128)S(1)}, u32[]{:S(2)}, u32[]{:S(2)}) %collective-permute-start.8) | collective-permute-done | bytes 155680 | tf_op jit(solution)/shard_map/ppermute | solution.py:343
  35.7 0.8 %collective-permute-done.7.refs_2_ = f32[304,128]{1,0:T(8,128)S(1)} collective-permute-done((f32[304,128]{1,0:T(8,128)S(1)}, f32[304,128]{1,0:T(8,128)S(1)}, u32[]{:S(2)}, u32[]{:S(2)}) %collective-permute-start.7) | collective-permute-done | bytes 155680 | tf_op jit(solution)/shard_map/ppermute | solution.py:343
  36.5 0.9 %collective-permute-done.6.refs_1_ = f32[304,128]{1,0:T(8,128)S(1)} collective-permute-done((f32[304,128]{1,0:T(8,128)S(1)}, f32[304,128]{1,0:T(8,128)S(1)}, u32[]{:S(2)}, u32[]{:S(2)}) %collective-permute-start.6) | collective-permute-done | bytes 155680 | tf_op jit(solution)/shard_map/ppermute | solution.py:343
  37.9 0.9 %collective-permute-done.10.refs_3_.refs_5_ = f32[304,128]{1,0:T(8,128)S(1)} collective-permute-done((f32[304,128]{1,0:T(8,128)S(1)}, f32[304,128]{1,0:T(8,128)S(1)}, u32[]{:S(2)}, u32[]{:S(2)}) %collective-permute-start.10) | collective-permute-done | bytes 155680 | tf_op jit(solution)/shard_map/ppermute | solution.py:343
  38.8 1.9 %next_step.1 = (f32[8,112,128]{2,1,0:T(8,128)S(1)}, f32[400,256]{1,0:T(8,128)S(1)}, f32[400,256]{1,0:T(8,128)S(1)}, f32[128,256]{1,0:T(8,128)S(1)}) custom-call(s32[2]{0:T(128)S(1)} %pad_add_fusion.place_ref, f32[400,256]{1,0:T(8,128)S(1)} %get-tuple-element.72.heads_ref, bf16[256,400]{1,0:T(8,128)(2,1)S(1)} %get-tuple-element.73.turned_ref, ...), custom_call_target="tpu_custom_call" | custom-call | bytes 4926472 | tf_op jit(solution)/shard_map/next_step/pallas_call | solution.py:317
  40.9 1.3 %collective-permute-done.13.other_ref = f32[4,112,128]{2,1,0:T(8,128)S(1)} collective-permute-done((f32[4,112,128]{2,1,0:T(8,128)S(1)}, f32[4,112,128]{2,1,0:T(8,128)S(1)}, u32[]{:S(2)}, u32[]{:S(2)}) %collective-permute-start.13) | collective-permute-done | bytes 229408 | tf_op jit(solution)/shard_map/ppermute | solution.py:343
  42.3 0.9 %collective-permute-start.14 = (f32[224,128]{1,0:T(8,128)S(1)}, f32[224,128]{1,0:T(8,128)S(1)}, u32[]{:S(2)}, u32[]{:S(2)}) collective-permute-start(f32[224,128]{1,0:T(8,128)S(1)} %pad_maximum_fusion.3), channel_id=1, source_target_pairs={{0,2},{1,3},{2,0},{3,1},{4,6},{5,7},{6,4},{7,5},{8,10},{9,11},{10,... | collective-permute-start | bytes 344072 | tf_op jit(solution)/shard_map/ppermute | solution.py:343
  43.2 1.2 %collective-permute-start.15 = (f32[224,128]{1,0:T(8,128)S(1)}, f32[224,128]{1,0:T(8,128)S(1)}, u32[]{:S(2)}, u32[]{:S(2)}) collective-permute-start(f32[224,128]{1,0:T(8,128)S(1)} %pad_maximum_fusion.4), channel_id=1, source_target_pairs={{0,6},{1,7},{2,4},{3,5},{4,2},{5,3},{6,0},{7,1},{8,14},{9,15},{10,... | collective-permute-start | bytes 344072 | tf_op jit(solution)/shard_map/ppermute | solution.py:343
  44.4 1.6 %collective-permute-start.16 = (f32[224,128]{1,0:T(8,128)S(1)}, f32[224,128]{1,0:T(8,128)S(1)}, u32[]{:S(2)}, u32[]{:S(2)}) collective-permute-start(f32[224,128]{1,0:T(8,128)S(1)} %pad_maximum_fusion.5), channel_id=1, source_target_pairs={{0,4},{1,5},{2,6},{3,7},{4,0},{5,1},{6,2},{7,3},{8,12},{9,13},{10,... | collective-permute-start | bytes 344072 | tf_op jit(solution)/shard_map/ppermute | solution.py:343
  46.4 3.4 %collective-permute-done.14.terms_ref = f32[224,128]{1,0:T(8,128)S(1)} collective-permute-done((f32[224,128]{1,0:T(8,128)S(1)}, f32[224,128]{1,0:T(8,128)S(1)}, u32[]{:S(2)}, u32[]{:S(2)}) %collective-permute-start.14) | collective-permute-done | bytes 114720 | tf_op jit(solution)/shard_map/ppermute | solution.py:343
  52.2 1.2 %last_update.1 = (f32[400,128]{1,0:T(8,128)}, f32[128]{0:T(128)}, f32[400,128]{1,0:T(8,128)}, f32[128]{0:T(128)}) custom-call(f32[400,128]{1,0:T(8,128)S(1)} %get-tuple-element.86.left_ref, f32[1,128]{1,0:T(1,128)S(1)} %get-tuple-element.87.lacc_ref, f32[400,256]{1,0:T(8,128)S(1)} %get-tuple-element.88.carry_ref, s32[2,256]{1,0:T(2,128)S(1)} %copy-done.3, ...), custom_call_target="tpu_custom_call" | custom-call | bytes 1777152 | tf_op jit(solution)/shard_map/last_update/pallas_call | solution.py:317
  53.4 0.9 %relations.1 = (f32[400,768]{1,0:T(8,128)S(1)}, f32[1,768]{1,0:T(1,128)S(1)}) custom-call(s32[2]{0:T(128)S(1)} %pad_add_fusion.place_ref, f32[400,768]{1,0:T(8,128)S(1)} %bitcast.36, f32[1,768]{1,0:T(1,128)S(1)} %broadcast_in_dim.10.relacc_ref, f32[304,128]{1,0:T(8,128)S(1)} %add.10.refs_0_, f32[304,128]{1,0:T(8,128)S(1)} %collective-permute-done.6.refs_1_, ...), custom_call_target="tpu_custom_call" | custom-call | bytes 3708936 | tf_op jit(solution)/shard_map/relations/pallas_call | solution.py:317
  54.4 4.5 %collective-permute-done.17 = f32[304,128]{1,0:T(8,128)S(1)} collective-permute-done((f32[304,128]{1,0:T(8,128)S(1)}, f32[304,128]{1,0:T(8,128)S(1)}, u32[]{:S(2)}, u32[]{:S(2)}) %collective-permute-start.17) | collective-permute-done | bytes 155680 | tf_op jit(solution)/shard_map/ppermute | solution.py:343
  58.9 2.5 %collective-permute-start.20 = (f32[304,128]{1,0:T(8,128)S(1)}, f32[304,128]{1,0:T(8,128)S(1)}, u32[]{:S(2)}, u32[]{:S(2)}) collective-permute-start(f32[304,128]{1,0:T(8,128)S(1)} %add.11.refs_0_), channel_id=1, source_target_pairs={{0,6},{1,7},{2,4},{3,5},{4,2},{5,3},{6,0},{7,1},{8,14},{9,15},{10,... | collective-permute-start | bytes 466952 | tf_op jit(solution)/shard_map/ppermute | solution.py:343
  61.4 1.0 %collective-permute-start.19 = (f32[304,128]{1,0:T(8,128)S(1)}, f32[304,128]{1,0:T(8,128)S(1)}, u32[]{:S(2)}, u32[]{:S(2)}) collective-permute-start(f32[304,128]{1,0:T(8,128)S(1)} %add.11.refs_0_), channel_id=1, source_target_pairs={{0,2},{1,3},{2,0},{3,1},{4,6},{5,7},{6,4},{7,5},{8,10},{9,11},{10,... | collective-permute-start | bytes 466952 | tf_op jit(solution)/shard_map/ppermute | solution.py:343
  62.4 3.0 %collective-permute-done.20.refs_3_ = f32[304,128]{1,0:T(8,128)S(1)} collective-permute-done((f32[304,128]{1,0:T(8,128)S(1)}, f32[304,128]{1,0:T(8,128)S(1)}, u32[]{:S(2)}, u32[]{:S(2)}) %collective-permute-start.20) | collective-permute-done | bytes 155680 | tf_op jit(solution)/shard_map/ppermute | solution.py:343
  65.5 1.6 %collective-permute-done.19.refs_2_ = f32[304,128]{1,0:T(8,128)S(1)} collective-permute-done((f32[304,128]{1,0:T(8,128)S(1)}, f32[304,128]{1,0:T(8,128)S(1)}, u32[]{:S(2)}, u32[]{:S(2)}) %collective-permute-start.19) | collective-permute-done | bytes 155680 | tf_op jit(solution)/shard_map/ppermute | solution.py:343
  67.6 0.9 %collective-permute-done.23.refs_6_ = f32[304,128]{1,0:T(8,128)S(1)} collective-permute-done((f32[304,128]{1,0:T(8,128)S(1)}, f32[304,128]{1,0:T(8,128)S(1)}, u32[]{:S(2)}, u32[]{:S(2)}) %collective-permute-start.23) | collective-permute-done | bytes 155680 | tf_op jit(solution)/shard_map/ppermute | solution.py:343
  69.0 2.0 %last_relations.1 = (f32[400,768]{1,0:T(8,128)}, f32[768]{0:T(1024)}) custom-call(s32[2]{0:T(128)S(1)} %pad_add_fusion.place_ref, f32[400,768]{1,0:T(8,128)S(1)} %get-tuple-element.99.rel_ref, f32[1,768]{1,0:T(1,128)S(1)} %get-tuple-element.100.relacc_ref, f32[304,128]{1,0:T(8,128)S(1)} %add.11.refs_0_, f32[304,128]{1,0:T(8,128)S(1)} %collective-permute-done.18.refs_1_, ...), custom_call_target="tpu_custom_call" | custom-call | bytes 3708936 | tf_op jit(solution)/shard_map/last_relations/pallas_call | solution.py:317
  (65 shorter events, 7.5 us)
Async XLA Ops:
  4.5 10.4 %collective-permute-start.2 = (f32[408,128]{1,0:T(8,128)S(1)}, f32[408,128]{1,0:T(8,128)S(1)}, u32[]{:S(2)}, u32[]{:S(2)}) collective-permute-start(f32[408,128]{1,0:T(8,128)S(1)} %get-tuple-element.58), channel_id=1, source_target_pairs={{12,0},{0,4},{4,8},{8,12},{13,1},{1,5},{5,9},{9,13},{14,2},{2,6},{... | collective-permute-start | bytes 626696 | tf_op jit(solution)/shard_map/ppermute | solution.py:381
  7.5 1.5 %collective-permute-start = (f32[4,112,128]{2,1,0:T(8,128)S(1)}, f32[4,112,128]{2,1,0:T(8,128)S(1)}, u32[]{:S(2)}, u32[]{:S(2)}) collective-permute-start(f32[4,112,128]{2,1,0:T(8,128)S(1)} %slice.42), channel_id=1, source_target_pairs={{0,1},{1,0},{2,3},{3,2},{4,5},{5,4},{6,7},{7,6},{8,9},{9,8},{10,11... | collective-permute-start | bytes 688136 | tf_op jit(solution)/shard_map/ppermute | solution.py:343
  9.0 5.8 %collective-permute-start.1 = (f32[224,128]{1,0:T(8,128)S(1)}, f32[224,128]{1,0:T(8,128)S(1)}, u32[]{:S(2)}, u32[]{:S(2)}) collective-permute-start(f32[224,128]{1,0:T(8,128)S(1)} %pad_maximum_fusion), channel_id=1, source_target_pairs={{0,2},{1,3},{2,0},{3,1},{4,6},{5,7},{6,4},{7,5},{8,10},{9,11},{10,... | collective-permute-start | bytes 344072 | tf_op jit(solution)/shard_map/ppermute | solution.py:343
  10.6 11.2 %copy-start.7 = (f32[768]{0:T(1024)S(1)}, f32[768]{0:T(1024)}, u32[]{:S(2)}) copy-start(f32[768]{0:T(1024)} %param.15) | copy-start | bytes 9220
  10.6 11.2 %copy-start = (f32[768,400]{0,1:T(8,128)S(1)}, f32[768,400]{0,1:T(8,128)}, u32[]{:S(2)}) copy-start(f32[768,400]{0,1:T(8,128)} %param.14) | copy-start | bytes 3686404
  10.6 11.2 %copy-start.1 = (f32[128,400]{0,1:T(8,128)S(1)}, f32[128,400]{0,1:T(8,128)}, u32[]{:S(2)}) copy-start(f32[128,400]{0,1:T(8,128)} %param.10) | copy-start | bytes 614404
  10.7 11.2 %copy-start.2 = (s32[2,256]{1,0:T(2,128)S(1)}, s32[2,256]{1,0:T(2,128)}, u32[]{:S(2)}) copy-start(s32[2,256]{1,0:T(2,128)} %refs_6_.1) | copy-start | bytes 6148
  10.7 11.2 %copy-start.3 = (s32[2,256]{1,0:T(2,128)S(1)}, s32[2,256]{1,0:T(2,128)}, u32[]{:S(2)}) copy-start(s32[2,256]{1,0:T(2,128)} %hid_ref.3) | copy-start | bytes 6148
  10.7 11.2 %copy-start.4 = (s32[2,256]{1,0:T(2,128)S(1)}, s32[2,256]{1,0:T(2,128)}, u32[]{:S(2)}) copy-start(s32[2,256]{1,0:T(2,128)} %tid_ref.1) | copy-start | bytes 6148
  10.7 11.2 %copy-start.5 = (s32[2,2,128]{2,1,0:T(2,128)S(1)}, s32[2,2,128]{2,1,0:T(2,128)}, u32[]{:S(2)}) copy-start(s32[2,2,128]{2,1,0:T(2,128)} %nid_ref.1) | copy-start | bytes 6148
  10.7 7.5 %collective-permute-start.3 = (f32[224,128]{1,0:T(8,128)S(1)}, f32[224,128]{1,0:T(8,128)S(1)}, u32[]{:S(2)}, u32[]{:S(2)}) collective-permute-start(f32[224,128]{1,0:T(8,128)S(1)} %pad_maximum_fusion.1), channel_id=1, source_target_pairs={{0,6},{1,7},{2,4},{3,5},{4,2},{5,3},{6,0},{7,1},{8,14},{9,15},{10,... | collective-permute-start | bytes 344072 | tf_op jit(solution)/shard_map/ppermute | solution.py:343
  12.3 7.3 %collective-permute-start.4 = (f32[224,128]{1,0:T(8,128)S(1)}, f32[224,128]{1,0:T(8,128)S(1)}, u32[]{:S(2)}, u32[]{:S(2)}) collective-permute-start(f32[224,128]{1,0:T(8,128)S(1)} %pad_maximum_fusion.2), channel_id=1, source_target_pairs={{0,4},{1,5},{2,6},{3,7},{4,0},{5,1},{6,2},{7,3},{8,12},{9,13},{10,... | collective-permute-start | bytes 344072 | tf_op jit(solution)/shard_map/ppermute | solution.py:343
  20.0 7.9 %collective-permute-start.5 = (f32[304,128]{1,0:T(8,128)S(1)}, f32[304,128]{1,0:T(8,128)S(1)}, u32[]{:S(2)}, u32[]{:S(2)}) collective-permute-start(f32[304,128]{1,0:T(8,128)S(1)} %more_terms.8), channel_id=1, source_target_pairs={{0,12},{1,13},{2,14},{3,15},{4,8},{5,9},{6,10},{7,11},{8,4},{9,5},... | collective-permute-start | bytes 466952 | tf_op jit(solution)/shard_map/ppermute | solution.py:343
  28.0 7.7 %collective-permute-start.8 = (f32[304,128]{1,0:T(8,128)S(1)}, f32[304,128]{1,0:T(8,128)S(1)}, u32[]{:S(2)}, u32[]{:S(2)}) collective-permute-start(f32[304,128]{1,0:T(8,128)S(1)} %add.10.refs_0_), channel_id=1, source_target_pairs={{0,6},{1,7},{2,4},{3,5},{4,2},{5,3},{6,0},{7,1},{8,14},{9,15},{10,... | collective-permute-start | bytes 466952 | tf_op jit(solution)/shard_map/ppermute | solution.py:343
  29.9 6.5 %collective-permute-start.7 = (f32[304,128]{1,0:T(8,128)S(1)}, f32[304,128]{1,0:T(8,128)S(1)}, u32[]{:S(2)}, u32[]{:S(2)}) collective-permute-start(f32[304,128]{1,0:T(8,128)S(1)} %add.10.refs_0_), channel_id=1, source_target_pairs={{0,2},{1,3},{2,0},{3,1},{4,6},{5,7},{6,4},{7,5},{8,10},{9,11},{10,... | collective-permute-start | bytes 466952 | tf_op jit(solution)/shard_map/ppermute | solution.py:343
  30.5 6.9 %collective-permute-start.6 = (f32[304,128]{1,0:T(8,128)S(1)}, f32[304,128]{1,0:T(8,128)S(1)}, u32[]{:S(2)}, u32[]{:S(2)}) collective-permute-start(f32[304,128]{1,0:T(8,128)S(1)} %add.10.refs_0_), channel_id=1, source_target_pairs={{0,4},{1,5},{2,6},{3,7},{4,0},{5,1},{6,2},{7,3},{8,12},{9,13},{10,... | collective-permute-start | bytes 466952 | tf_op jit(solution)/shard_map/ppermute | solution.py:343
  31.5 6.2 %collective-permute-start.9 = (f32[304,128]{1,0:T(8,128)S(1)}, f32[304,128]{1,0:T(8,128)S(1)}, u32[]{:S(2)}, u32[]{:S(2)}) collective-permute-start(f32[304,128]{1,0:T(8,128)S(1)} %add.10.refs_0_), channel_id=1, source_target_pairs={{0,1},{1,0},{2,3},{3,2},{4,5},{5,4},{6,7},{7,6},{8,9},{9,8},{10,11... | collective-permute-start | bytes 466952 | tf_op jit(solution)/shard_map/ppermute | solution.py:343
  35.7 2.0 %collective-permute-start.12 = (f32[304,128]{1,0:T(8,128)S(1)}, f32[304,128]{1,0:T(8,128)S(1)}, u32[]{:S(2)}, u32[]{:S(2)}) collective-permute-start(f32[304,128]{1,0:T(8,128)S(1)} %collective-permute-done.8.refs_3_), channel_id=1, source_target_pairs={{0,1},{1,0},{2,3},{3,2},{4,5},{5,4},{6,7},{7,6},{8,9},{9,8},{10,11... | collective-permute-start | bytes 466952 | tf_op jit(solution)/shard_map/ppermute | solution.py:343
  36.5 1.4 %collective-permute-start.11 = (f32[304,128]{1,0:T(8,128)S(1)}, f32[304,128]{1,0:T(8,128)S(1)}, u32[]{:S(2)}, u32[]{:S(2)}) collective-permute-start(f32[304,128]{1,0:T(8,128)S(1)} %collective-permute-done.7.refs_2_), channel_id=1, source_target_pairs={{0,1},{1,0},{2,3},{3,2},{4,5},{5,4},{6,7},{7,6},{8,9},{9,8},{10,11... | collective-permute-start | bytes 466952 | tf_op jit(solution)/shard_map/ppermute | solution.py:343
  37.4 1.4 %collective-permute-start.10 = (f32[304,128]{1,0:T(8,128)S(1)}, f32[304,128]{1,0:T(8,128)S(1)}, u32[]{:S(2)}, u32[]{:S(2)}) collective-permute-start(f32[304,128]{1,0:T(8,128)S(1)} %collective-permute-done.6.refs_1_), channel_id=1, source_target_pairs={{0,1},{1,0},{2,3},{3,2},{4,5},{5,4},{6,7},{7,6},{8,9},{9,8},{10,11... | collective-permute-start | bytes 466952 | tf_op jit(solution)/shard_map/ppermute | solution.py:343
  40.7 1.6 %collective-permute-start.13 = (f32[4,112,128]{2,1,0:T(8,128)S(1)}, f32[4,112,128]{2,1,0:T(8,128)S(1)}, u32[]{:S(2)}, u32[]{:S(2)}) collective-permute-start(f32[4,112,128]{2,1,0:T(8,128)S(1)} %slice.49), channel_id=1, source_target_pairs={{0,1},{1,0},{2,3},{3,2},{4,5},{5,4},{6,7},{7,6},{8,9},{9,8},{10,11... | collective-permute-start | bytes 688136 | tf_op jit(solution)/shard_map/ppermute | solution.py:343
  42.3 7.5 %collective-permute-start.14 = (f32[224,128]{1,0:T(8,128)S(1)}, f32[224,128]{1,0:T(8,128)S(1)}, u32[]{:S(2)}, u32[]{:S(2)}) collective-permute-start(f32[224,128]{1,0:T(8,128)S(1)} %pad_maximum_fusion.3), channel_id=1, source_target_pairs={{0,2},{1,3},{2,0},{3,1},{4,6},{5,7},{6,4},{7,5},{8,10},{9,11},{10,... | collective-permute-start | bytes 344072 | tf_op jit(solution)/shard_map/ppermute | solution.py:343
  43.2 7.0 %collective-permute-start.15 = (f32[224,128]{1,0:T(8,128)S(1)}, f32[224,128]{1,0:T(8,128)S(1)}, u32[]{:S(2)}, u32[]{:S(2)}) collective-permute-start(f32[224,128]{1,0:T(8,128)S(1)} %pad_maximum_fusion.4), channel_id=1, source_target_pairs={{0,6},{1,7},{2,4},{3,5},{4,2},{5,3},{6,0},{7,1},{8,14},{9,15},{10,... | collective-permute-start | bytes 344072 | tf_op jit(solution)/shard_map/ppermute | solution.py:343
  44.4 6.9 %collective-permute-start.16 = (f32[224,128]{1,0:T(8,128)S(1)}, f32[224,128]{1,0:T(8,128)S(1)}, u32[]{:S(2)}, u32[]{:S(2)}) collective-permute-start(f32[224,128]{1,0:T(8,128)S(1)} %pad_maximum_fusion.5), channel_id=1, source_target_pairs={{0,4},{1,5},{2,6},{3,7},{4,0},{5,1},{6,2},{7,3},{8,12},{9,13},{10,... | collective-permute-start | bytes 344072 | tf_op jit(solution)/shard_map/ppermute | solution.py:343
  51.7 7.2 %collective-permute-start.17 = (f32[304,128]{1,0:T(8,128)S(1)}, f32[304,128]{1,0:T(8,128)S(1)}, u32[]{:S(2)}, u32[]{:S(2)}) collective-permute-start(f32[304,128]{1,0:T(8,128)S(1)} %more_terms.11), channel_id=1, source_target_pairs={{0,12},{1,13},{2,14},{3,15},{4,8},{5,9},{6,10},{7,11},{8,4},{9,5},... | collective-permute-start | bytes 466952 | tf_op jit(solution)/shard_map/ppermute | solution.py:343
  58.9 6.6 %collective-permute-start.20 = (f32[304,128]{1,0:T(8,128)S(1)}, f32[304,128]{1,0:T(8,128)S(1)}, u32[]{:S(2)}, u32[]{:S(2)}) collective-permute-start(f32[304,128]{1,0:T(8,128)S(1)} %add.11.refs_0_), channel_id=1, source_target_pairs={{0,6},{1,7},{2,4},{3,5},{4,2},{5,3},{6,0},{7,1},{8,14},{9,15},{10,... | collective-permute-start | bytes 466952 | tf_op jit(solution)/shard_map/ppermute | solution.py:343
  61.4 5.7 %collective-permute-start.19 = (f32[304,128]{1,0:T(8,128)S(1)}, f32[304,128]{1,0:T(8,128)S(1)}, u32[]{:S(2)}, u32[]{:S(2)}) collective-permute-start(f32[304,128]{1,0:T(8,128)S(1)} %add.11.refs_0_), channel_id=1, source_target_pairs={{0,2},{1,3},{2,0},{3,1},{4,6},{5,7},{6,4},{7,5},{8,10},{9,11},{10,... | collective-permute-start | bytes 466952 | tf_op jit(solution)/shard_map/ppermute | solution.py:343
  62.4 5.2 %collective-permute-start.18 = (f32[304,128]{1,0:T(8,128)S(1)}, f32[304,128]{1,0:T(8,128)S(1)}, u32[]{:S(2)}, u32[]{:S(2)}) collective-permute-start(f32[304,128]{1,0:T(8,128)S(1)} %add.11.refs_0_), channel_id=1, source_target_pairs={{0,4},{1,5},{2,6},{3,7},{4,0},{5,1},{6,2},{7,3},{8,12},{9,13},{10,... | collective-permute-start | bytes 466952 | tf_op jit(solution)/shard_map/ppermute | solution.py:343
  62.4 5.2 %collective-permute-start.21 = (f32[304,128]{1,0:T(8,128)S(1)}, f32[304,128]{1,0:T(8,128)S(1)}, u32[]{:S(2)}, u32[]{:S(2)}) collective-permute-start(f32[304,128]{1,0:T(8,128)S(1)} %add.11.refs_0_), channel_id=1, source_target_pairs={{0,1},{1,0},{2,3},{3,2},{4,5},{5,4},{6,7},{7,6},{8,9},{9,8},{10,11... | collective-permute-start | bytes 466952 | tf_op jit(solution)/shard_map/ppermute | solution.py:343
  65.5 2.1 %collective-permute-start.24 = (f32[304,128]{1,0:T(8,128)S(1)}, f32[304,128]{1,0:T(8,128)S(1)}, u32[]{:S(2)}, u32[]{:S(2)}) collective-permute-start(f32[304,128]{1,0:T(8,128)S(1)} %collective-permute-done.20.refs_3_), channel_id=1, source_target_pairs={{0,1},{1,0},{2,3},{3,2},{4,5},{5,4},{6,7},{7,6},{8,9},{9,8},{10,11... | collective-permute-start | bytes 466952 | tf_op jit(solution)/shard_map/ppermute | solution.py:343
  67.1 1.4 %collective-permute-start.23 = (f32[304,128]{1,0:T(8,128)S(1)}, f32[304,128]{1,0:T(8,128)S(1)}, u32[]{:S(2)}, u32[]{:S(2)}) collective-permute-start(f32[304,128]{1,0:T(8,128)S(1)} %collective-permute-done.19.refs_2_), channel_id=1, source_target_pairs={{0,1},{1,0},{2,3},{3,2},{4,5},{5,4},{6,7},{7,6},{8,9},{9,8},{10,11... | collective-permute-start | bytes 466952 | tf_op jit(solution)/shard_map/ppermute | solution.py:343
  67.6 1.4 %collective-permute-start.22 = (f32[304,128]{1,0:T(8,128)S(1)}, f32[304,128]{1,0:T(8,128)S(1)}, u32[]{:S(2)}, u32[]{:S(2)}) collective-permute-start(f32[304,128]{1,0:T(8,128)S(1)} %collective-permute-done.18.refs_1_), channel_id=1, source_target_pairs={{0,1},{1,0},{2,3},{3,2},{4,5},{5,4},{6,7},{7,6},{8,9},{9,8},{10,11... | collective-permute-start | bytes 466952 | tf_op jit(solution)/shard_map/ppermute | solution.py:343
  (1 other events, 11.2 us)

commit v5 on v4

--- a/solution.py
+++ b/solution.py
@@ -94,31 +94,46 @@
     return -(-(width // PIECES) * kinds // LANES // 8) * 8
 
 
+def term_rows(width, edges):
+    return edges // LANES * cut(width)[0] + 8
+
+
 def put_terms(place_ref, terms, kinds, out_ref):
     square, core = place_ref[0], place_ref[1]
     width, edges = terms.shape
     half = PIECES // 2
     main, rest = cut(width)
-    below = jnp.zeros((8 - rest - 1, LANES), F32)
+    tiles = [slice(LANES * j, LANES * (j + 1)) for j in range(edges // LANES)]
+    ids = [kinds[:, lanes].astype(F32) for lanes in tiles]
+    ids.append(jnp.zeros((8 - len(tiles) * (rest + 1), LANES), F32))
     for c in range(PIECES):
         at = jnp.bitwise_xor(c // half, core) * half + jnp.bitwise_xor(c % half, square)
         last = main * PIECES + rest * c
-        for j in range(edges // LANES):
-            lanes = slice(LANES * j, LANES * (j + 1))
-            top = (main + 8) * j
-            out_ref[at, top : top + main] = terms[main * c : main * (c + 1), lanes]
-            out_ref[at, top + main : top + main + 8] = jnp.concatenate(
-                [terms[last : last + rest, lanes], kinds[:, lanes].astype(F32), below], axis=0
-            )
-
-
-def sum_terms(width, kinds, blocks_of_edges):
+        for j, lanes in enumerate(tiles):
+            out_ref[at, main * j : main * (j + 1)] = terms[main * c : main * (c + 1), lanes]
+        out_ref[at, main * len(tiles) :] = jnp.concatenate(
+            [terms[last : last + rest, lanes] for lanes in tiles] + ids, axis=0
+        )
+
+
+def turn(x, by):
+    return [x[by:], x[:by]] if by else [x]
+
+
+def sum_terms(width, kinds, parts):
     main, rest = cut(width)
     total = None
-    for i in range(0, len(blocks_of_edges), 2):
-        pair = jnp.concatenate(blocks_of_edges[i : i + 2], axis=1)
-        both = jnp.concatenate(halves(pair), axis=0)
-        grad = nt(both, selector(pair[main + rest : main + rest + 1].astype(jnp.int32), kinds).astype(BF16))
+    for part in parts:
+        tiles = part.shape[0] // main
+        below = part[main * tiles :]
+        each = [
+            jnp.concatenate([part[main * j : main * (j + 1)]] + turn(below, rest * j), axis=0)
+            for j in range(tiles)
+        ]
+        first = rest * tiles
+        ids = jnp.concatenate([below[first + j : first + j + 1] for j in range(tiles)], axis=1)
+        both = stack(jnp.concatenate(each, axis=1))
+        grad = nt(both, selector(ids.astype(jnp.int32), kinds).astype(BF16))
         grad = grad[: main + 8] + grad[main + 8 :]
         total = grad if total is None else total + grad
     return total
@@ -139,15 +154,12 @@
 
 
 def chip_kernel(width, kinds, own_ref, other_ref, out_ref):
-    rows = cut(width)[0] + 8
-    tiles = [ref[0, rows * j : rows * (j + 1)] for ref in (own_ref, other_ref) for j in range(ref.shape[1] // rows)]
-    put_piece(sum_terms(width, kinds, tiles), width, out_ref)
+    put_piece(sum_terms(width, kinds, [own_ref[0], other_ref[0]]), width, out_ref)
 
 
 def more_kernel(width, kinds, total_ref, terms_ref, out_ref):
-    rows = cut(width)[0] + 8
-    tiles = [terms_ref[rows * j : rows * (j + 1)] for j in range(terms_ref.shape[0] // rows)]
-    put_piece(sum_terms(width, kinds, tiles), width, out_ref, total_ref)
+    rows = terms_ref.shape[0] // 2
+    put_piece(sum_terms(width, kinds, [terms_ref[:rows], terms_ref[rows:]]), width, out_ref, total_ref)
 
 
 def order_pieces(place_ref, piece_refs, all_ref):
@@ -396,7 +408,7 @@
     rel, relacc = relations.T, rel_accum[None]
     edges = head_ids.shape[1]
     table, state, each = (width, rows), (1, rows), (width, edges)
-    cut_terms = (PIECES, edges // LANES * (cut(width)[0] + 8), LANES)
+    cut_terms = (PIECES, term_rows(width, edges), LANES)
     given = (head_ids, tail_ids, rel_ids, neg_ids, left, tail_table.T, tail_accum[None], rel)
     right, terms, carry = pl.pallas_call(
         first_kernel,

time: 71.1 us -> 70.4 us (level)
  waiting for transfers between devices: 35.3 us -> 34.5 us
    ppermute x24, waiting for transfers between devices: 33.7 us -> 32.9 us  [swap(): return lax.ppermute(x, AXES, route)]
  transfers between devices with their start and end apart: 25 -> 25, of which waited for: 19 -> 20; matrix products, arithmetic and copies ran while one was open for 0% -> 0% of each run, Pallas kernels for 8% -> 8%
where the time goes in v5:
time: 70.4 us; the launch traced here: 70.2 us
  waiting for transfers between devices  34.5 us (49%)
  starting transfers between devices  20.2 us (29%)
  Pallas kernels  14.3 us (20%)
  between operations  0.94 us (1%)
    ppermute x24, waiting for transfers between devices, swap(): return lax.ppermute(x, AXES, route)  32.9 us
    ppermute x24, starting transfers between devices, swap(): return lax.ppermute(x, AXES, route)  17.1 us
    pallas_call x14, Pallas kernels, run(): pl.pallas_call(kernel, out_shape=[jax.ShapeDtypeStruct(shape, F32) if isi...  10.6 us
    pallas_call x1, Pallas kernels, shards(): pl.pallas_call(first_kernel, out_shape=[jax.ShapeDtypeStruct(shape, F32)...  3.7 us
    ppermute x1, starting transfers between devices, from_behind(): return lax.ppermute(block, axis, [((i - 1) % n, i) for i in range(n)])  3.07 us
    ppermute x1, waiting for transfers between devices, from_behind(): return lax.ppermute(block, axis, [((i - 1) % n, i) for i in range(n)])  1.62 us
  transfers between devices with their start and end apart: 25, of which 20 were waited for; matrix products, arithmetic and copies ran while one was open for 0% of the time, Pallas kernels for 8%

profile of v5, /device:TPU:0, one launch (start us, length us, event | category | flops | bytes accessed | tf_op | source)
XLA Modules:
  0.0 70.2 jit_solution(1475915032542094489)
XLA Ops:
  0.7 3.7 %first_step.1 = (f32[408,128]{1,0:T(8,128)S(1)}, f32[8,104,128]{2,1,0:T(8,128)S(1)}, f32[400,256]{1,0:T(8,128)S(1)}) custom-call(s32[2]{0:T(128)S(1)} %pad_add_fusion.place_ref, s32[2,256]{1,0:T(2,128)} %hid_ref.3, s32[2,256]{1,0:T(2,128)} %tid_ref.1, s32[2,256]{1,0:T(2,128)} %refs_6_.1, s32[2,2,128]{2,1,0:T(2,128)} %nid_ref.1, f32[400,128]{1,0:T(8,128)} %bitcast.37, ...), custom_call_target="tpu_custom_call" | custom-call | tf_op jit(solution)/shard_map/first_step/pallas_call | solution.py:413
  4.4 3.1 %collective-permute-start.2 = (f32[408,128]{1,0:T(8,128)S(1)}, f32[408,128]{1,0:T(8,128)S(1)}, u32[]{:S(2)}, u32[]{:S(2)}) collective-permute-start(f32[408,128]{1,0:T(8,128)S(1)} %get-tuple-element.58), channel_id=1, source_target_pairs={{12,0},{0,4},{4,8},{8,12},{13,1},{1,5},{5,9},{9,13},{14,2},{2,6},{... | collective-permute-start | bytes 626696 | tf_op jit(solution)/shard_map/ppermute | solution.py:393
  7.5 1.4 %collective-permute-done.other_ref = f32[4,104,128]{2,1,0:T(8,128)S(1)} collective-permute-done((f32[4,104,128]{2,1,0:T(8,128)S(1)}, f32[4,104,128]{2,1,0:T(8,128)S(1)}, u32[]{:S(2)}, u32[]{:S(2)}) %collective-permute-start) | collective-permute-done | bytes 213024 | tf_op jit(solution)/shard_map/ppermute | solution.py:355
  9.0 1.6 %collective-permute-start.1 = (f32[208,128]{1,0:T(8,128)S(1)}, f32[208,128]{1,0:T(8,128)S(1)}, u32[]{:S(2)}, u32[]{:S(2)}) collective-permute-start(f32[208,128]{1,0:T(8,128)S(1)} %pad_maximum_fusion), channel_id=1, source_target_pairs={{0,2},{1,3},{2,0},{3,1},{4,6},{5,7},{6,4},{7,5},{8,10},{9,11},{10,... | collective-permute-start | bytes 319496 | tf_op jit(solution)/shard_map/ppermute | solution.py:355
  10.7 1.6 %collective-permute-start.3 = (f32[208,128]{1,0:T(8,128)S(1)}, f32[208,128]{1,0:T(8,128)S(1)}, u32[]{:S(2)}, u32[]{:S(2)}) collective-permute-start(f32[208,128]{1,0:T(8,128)S(1)} %pad_maximum_fusion.1), channel_id=1, source_target_pairs={{0,6},{1,7},{2,4},{3,5},{4,2},{5,3},{6,0},{7,1},{8,14},{9,15},{10,... | collective-permute-start | bytes 319496 | tf_op jit(solution)/shard_map/ppermute | solution.py:355
  13.2 1.6 %collective-permute-done.2.right_ref = f32[408,128]{1,0:T(8,128)S(1)} collective-permute-done((f32[408,128]{1,0:T(8,128)S(1)}, f32[408,128]{1,0:T(8,128)S(1)}, u32[]{:S(2)}, u32[]{:S(2)}) %collective-permute-start.2) | collective-permute-done | bytes 208928 | tf_op jit(solution)/shard_map/ppermute | solution.py:393
  15.2 2.8 %collective-permute-done.3.terms_ref = f32[208,128]{1,0:T(8,128)S(1)} collective-permute-done((f32[208,128]{1,0:T(8,128)S(1)}, f32[208,128]{1,0:T(8,128)S(1)}, u32[]{:S(2)}, u32[]{:S(2)}) %collective-permute-start.3) | collective-permute-done | bytes 106528 | tf_op jit(solution)/shard_map/ppermute | solution.py:355
  18.4 0.9 %collective-permute-done.4.terms_ref = f32[208,128]{1,0:T(8,128)S(1)} collective-permute-done((f32[208,128]{1,0:T(8,128)S(1)}, f32[208,128]{1,0:T(8,128)S(1)}, u32[]{:S(2)}, u32[]{:S(2)}) %collective-permute-start.4) | collective-permute-done | bytes 106528 | tf_op jit(solution)/shard_map/ppermute | solution.py:355
  19.7 1.8 %collective-permute-start.5 = (f32[304,128]{1,0:T(8,128)S(1)}, f32[304,128]{1,0:T(8,128)S(1)}, u32[]{:S(2)}, u32[]{:S(2)}) collective-permute-start(f32[304,128]{1,0:T(8,128)S(1)} %more_terms.8), channel_id=1, source_target_pairs={{0,12},{1,13},{2,14},{3,15},{4,8},{5,9},{6,10},{7,11},{8,4},{9,5},... | collective-permute-start | bytes 466952 | tf_op jit(solution)/shard_map/ppermute | solution.py:355
  21.6 1.1 %ready.1 = (f32[400,128]{1,0:T(8,128)S(1)}, f32[1,128]{1,0:T(1,128)S(1)}, f32[400,256]{1,0:T(8,128)S(1)}, bf16[256,400]{1,0:T(8,128)(2,1)S(1)}, bf16[800,128]{1,...) custom-call(f32[400,128]{1,0:T(8,128)S(1)} %bitcast.38, ...), custom_call_target="tpu_custom_call" | custom-call | bytes 4957184 | tf_op jit(solution)/shard_map/ready/pallas_call | solution.py:329
  22.7 4.9 %collective-permute-done.5 = f32[304,128]{1,0:T(8,128)S(1)} collective-permute-done((f32[304,128]{1,0:T(8,128)S(1)}, f32[304,128]{1,0:T(8,128)S(1)}, u32[]{:S(2)}, u32[]{:S(2)}) %collective-permute-start.5) | collective-permute-done | bytes 155680 | tf_op jit(solution)/shard_map/ppermute | solution.py:355
  27.6 2.0 %collective-permute-start.8 = (f32[304,128]{1,0:T(8,128)S(1)}, f32[304,128]{1,0:T(8,128)S(1)}, u32[]{:S(2)}, u32[]{:S(2)}) collective-permute-start(f32[304,128]{1,0:T(8,128)S(1)} %add.10.refs_0_), channel_id=1, source_target_pairs={{0,6},{1,7},{2,4},{3,5},{4,2},{5,3},{6,0},{7,1},{8,14},{9,15},{10,... | collective-permute-start | bytes 466952 | tf_op jit(solution)/shard_map/ppermute | solution.py:355
  30.1 1.1 %collective-permute-start.6 = (f32[304,128]{1,0:T(8,128)S(1)}, f32[304,128]{1,0:T(8,128)S(1)}, u32[]{:S(2)}, u32[]{:S(2)}) collective-permute-start(f32[304,128]{1,0:T(8,128)S(1)} %add.10.refs_0_), channel_id=1, source_target_pairs={{0,4},{1,5},{2,6},{3,7},{4,0},{5,1},{6,2},{7,3},{8,12},{9,13},{10,... | collective-permute-start | bytes 466952 | tf_op jit(solution)/shard_map/ppermute | solution.py:355
  31.2 4.2 %collective-permute-done.8.refs_3_ = f32[304,128]{1,0:T(8,128)S(1)} collective-permute-done((f32[304,128]{1,0:T(8,128)S(1)}, f32[304,128]{1,0:T(8,128)S(1)}, u32[]{:S(2)}, u32[]{:S(2)}) %collective-permute-start.8) | collective-permute-done | bytes 155680 | tf_op jit(solution)/shard_map/ppermute | solution.py:355
  35.4 0.8 %collective-permute-done.7.refs_2_ = f32[304,128]{1,0:T(8,128)S(1)} collective-permute-done((f32[304,128]{1,0:T(8,128)S(1)}, f32[304,128]{1,0:T(8,128)S(1)}, u32[]{:S(2)}, u32[]{:S(2)}) %collective-permute-start.7) | collective-permute-done | bytes 155680 | tf_op jit(solution)/shard_map/ppermute | solution.py:355
  36.1 0.9 %collective-permute-done.6.refs_1_ = f32[304,128]{1,0:T(8,128)S(1)} collective-permute-done((f32[304,128]{1,0:T(8,128)S(1)}, f32[304,128]{1,0:T(8,128)S(1)}, u32[]{:S(2)}, u32[]{:S(2)}) %collective-permute-start.6) | collective-permute-done | bytes 155680 | tf_op jit(solution)/shard_map/ppermute | solution.py:355
  37.5 0.9 %collective-permute-done.10.refs_3_.refs_5_ = f32[304,128]{1,0:T(8,128)S(1)} collective-permute-done((f32[304,128]{1,0:T(8,128)S(1)}, f32[304,128]{1,0:T(8,128)S(1)}, u32[]{:S(2)}, u32[]{:S(2)}) %collective-permute-start.10) | collective-permute-done | bytes 155680 | tf_op jit(solution)/shard_map/ppermute | solution.py:355
  38.4 1.9 %next_step.1 = (f32[8,104,128]{2,1,0:T(8,128)S(1)}, f32[400,256]{1,0:T(8,128)S(1)}, f32[400,256]{1,0:T(8,128)S(1)}, f32[128,256]{1,0:T(8,128)S(1)}) custom-call(s32[2]{0:T(128)S(1)} %pad_add_fusion.place_ref, f32[400,256]{1,0:T(8,128)S(1)} %get-tuple-element.72.heads_ref, bf16[256,400]{1,0:T(8,128)(2,1)S(1)} %get-tuple-element.73.turned_ref, ...), custom_call_target="tpu_custom_call" | custom-call | bytes 4893704 | tf_op jit(solution)/shard_map/next_step/pallas_call | solution.py:329
  40.6 1.3 %collective-permute-done.13.other_ref = f32[4,104,128]{2,1,0:T(8,128)S(1)} collective-permute-done((f32[4,104,128]{2,1,0:T(8,128)S(1)}, f32[4,104,128]{2,1,0:T(8,128)S(1)}, u32[]{:S(2)}, u32[]{:S(2)}) %collective-permute-start.13) | collective-permute-done | bytes 213024 | tf_op jit(solution)/shard_map/ppermute | solution.py:355
  41.9 0.9 %collective-permute-start.14 = (f32[208,128]{1,0:T(8,128)S(1)}, f32[208,128]{1,0:T(8,128)S(1)}, u32[]{:S(2)}, u32[]{:S(2)}) collective-permute-start(f32[208,128]{1,0:T(8,128)S(1)} %pad_maximum_fusion.3), channel_id=1, source_target_pairs={{0,2},{1,3},{2,0},{3,1},{4,6},{5,7},{6,4},{7,5},{8,10},{9,11},{10,... | collective-permute-start | bytes 319496 | tf_op jit(solution)/shard_map/ppermute | solution.py:355
  42.8 1.2 %collective-permute-start.15 = (f32[208,128]{1,0:T(8,128)S(1)}, f32[208,128]{1,0:T(8,128)S(1)}, u32[]{:S(2)}, u32[]{:S(2)}) collective-permute-start(f32[208,128]{1,0:T(8,128)S(1)} %pad_maximum_fusion.4), channel_id=1, source_target_pairs={{0,6},{1,7},{2,4},{3,5},{4,2},{5,3},{6,0},{7,1},{8,14},{9,15},{10,... | collective-permute-start | bytes 319496 | tf_op jit(solution)/shard_map/ppermute | solution.py:355
  44.0 1.6 %collective-permute-start.16 = (f32[208,128]{1,0:T(8,128)S(1)}, f32[208,128]{1,0:T(8,128)S(1)}, u32[]{:S(2)}, u32[]{:S(2)}) collective-permute-start(f32[208,128]{1,0:T(8,128)S(1)} %pad_maximum_fusion.5), channel_id=1, source_target_pairs={{0,4},{1,5},{2,6},{3,7},{4,0},{5,1},{6,2},{7,3},{8,12},{9,13},{10,... | collective-permute-start | bytes 319496 | tf_op jit(solution)/shard_map/ppermute | solution.py:355
  46.0 2.9 %collective-permute-done.14.terms_ref = f32[208,128]{1,0:T(8,128)S(1)} collective-permute-done((f32[208,128]{1,0:T(8,128)S(1)}, f32[208,128]{1,0:T(8,128)S(1)}, u32[]{:S(2)}, u32[]{:S(2)}) %collective-permute-start.14) | collective-permute-done | bytes 106528 | tf_op jit(solution)/shard_map/ppermute | solution.py:355
  51.5 1.2 %last_update.1 = (f32[400,128]{1,0:T(8,128)}, f32[128]{0:T(128)}, f32[400,128]{1,0:T(8,128)}, f32[128]{0:T(128)}) custom-call(f32[400,128]{1,0:T(8,128)S(1)} %get-tuple-element.86.left_ref, f32[1,128]{1,0:T(1,128)S(1)} %get-tuple-element.87.lacc_ref, f32[400,256]{1,0:T(8,128)S(1)} %get-tuple-element.88.carry_ref, s32[2,256]{1,0:T(2,128)S(1)} %copy-done.3, ...), custom_call_target="tpu_custom_call" | custom-call | bytes 1777152 | tf_op jit(solution)/shard_map/last_update/pallas_call | solution.py:329
  52.7 0.9 %relations.1 = (f32[400,768]{1,0:T(8,128)S(1)}, f32[1,768]{1,0:T(1,128)S(1)}) custom-call(s32[2]{0:T(128)S(1)} %pad_add_fusion.place_ref, f32[400,768]{1,0:T(8,128)S(1)} %bitcast.36, f32[1,768]{1,0:T(1,128)S(1)} %broadcast_in_dim.10.relacc_ref, f32[304,128]{1,0:T(8,128)S(1)} %add.10.refs_0_, f32[304,128]{1,0:T(8,128)S(1)} %collective-permute-done.6.refs_1_, ...), custom_call_target="tpu_custom_call" | custom-call | bytes 3708936 | tf_op jit(solution)/shard_map/relations/pallas_call | solution.py:329
  53.6 4.5 %collective-permute-done.17 = f32[304,128]{1,0:T(8,128)S(1)} collective-permute-done((f32[304,128]{1,0:T(8,128)S(1)}, f32[304,128]{1,0:T(8,128)S(1)}, u32[]{:S(2)}, u32[]{:S(2)}) %collective-permute-start.17) | collective-permute-done | bytes 155680 | tf_op jit(solution)/shard_map/ppermute | solution.py:355
  58.1 2.5 %collective-permute-start.20 = (f32[304,128]{1,0:T(8,128)S(1)}, f32[304,128]{1,0:T(8,128)S(1)}, u32[]{:S(2)}, u32[]{:S(2)}) collective-permute-start(f32[304,128]{1,0:T(8,128)S(1)} %add.11.refs_0_), channel_id=1, source_target_pairs={{0,6},{1,7},{2,4},{3,5},{4,2},{5,3},{6,0},{7,1},{8,14},{9,15},{10,... | collective-permute-start | bytes 466952 | tf_op jit(solution)/shard_map/ppermute | solution.py:355
  60.6 1.0 %collective-permute-start.19 = (f32[304,128]{1,0:T(8,128)S(1)}, f32[304,128]{1,0:T(8,128)S(1)}, u32[]{:S(2)}, u32[]{:S(2)}) collective-permute-start(f32[304,128]{1,0:T(8,128)S(1)} %add.11.refs_0_), channel_id=1, source_target_pairs={{0,2},{1,3},{2,0},{3,1},{4,6},{5,7},{6,4},{7,5},{8,10},{9,11},{10,... | collective-permute-start | bytes 466952 | tf_op jit(solution)/shard_map/ppermute | solution.py:355
  61.7 3.0 %collective-permute-done.20.refs_3_ = f32[304,128]{1,0:T(8,128)S(1)} collective-permute-done((f32[304,128]{1,0:T(8,128)S(1)}, f32[304,128]{1,0:T(8,128)S(1)}, u32[]{:S(2)}, u32[]{:S(2)}) %collective-permute-start.20) | collective-permute-done | bytes 155680 | tf_op jit(solution)/shard_map/ppermute | solution.py:355
  64.7 1.6 %collective-permute-done.19.refs_2_ = f32[304,128]{1,0:T(8,128)S(1)} collective-permute-done((f32[304,128]{1,0:T(8,128)S(1)}, f32[304,128]{1,0:T(8,128)S(1)}, u32[]{:S(2)}, u32[]{:S(2)}) %collective-permute-start.19) | collective-permute-done | bytes 155680 | tf_op jit(solution)/shard_map/ppermute | solution.py:355
  66.9 0.9 %collective-permute-done.23.refs_6_ = f32[304,128]{1,0:T(8,128)S(1)} collective-permute-done((f32[304,128]{1,0:T(8,128)S(1)}, f32[304,128]{1,0:T(8,128)S(1)}, u32[]{:S(2)}, u32[]{:S(2)}) %collective-permute-start.23) | collective-permute-done | bytes 155680 | tf_op jit(solution)/shard_map/ppermute | solution.py:355
  68.2 2.0 %last_relations.1 = (f32[400,768]{1,0:T(8,128)}, f32[768]{0:T(1024)}) custom-call(s32[2]{0:T(128)S(1)} %pad_add_fusion.place_ref, f32[400,768]{1,0:T(8,128)S(1)} %get-tuple-element.99.rel_ref, f32[1,768]{1,0:T(1,128)S(1)} %get-tuple-element.100.relacc_ref, f32[304,128]{1,0:T(8,128)S(1)} %add.11.refs_0_, f32[304,128]{1,0:T(8,128)S(1)} %collective-permute-done.18.refs_1_, ...), custom_call_target="tpu_custom_call" | custom-call | bytes 3708936 | tf_op jit(solution)/shard_map/last_relations/pallas_call | solution.py:329
  (65 shorter events, 7.7 us)
Async XLA Ops:
  4.4 10.4 %collective-permute-start.2 = (f32[408,128]{1,0:T(8,128)S(1)}, f32[408,128]{1,0:T(8,128)S(1)}, u32[]{:S(2)}, u32[]{:S(2)}) collective-permute-start(f32[408,128]{1,0:T(8,128)S(1)} %get-tuple-element.58), channel_id=1, source_target_pairs={{12,0},{0,4},{4,8},{8,12},{13,1},{1,5},{5,9},{9,13},{14,2},{2,6},{... | collective-permute-start | bytes 626696 | tf_op jit(solution)/shard_map/ppermute | solution.py:393
  7.5 1.5 %collective-permute-start = (f32[4,104,128]{2,1,0:T(8,128)S(1)}, f32[4,104,128]{2,1,0:T(8,128)S(1)}, u32[]{:S(2)}, u32[]{:S(2)}) collective-permute-start(f32[4,104,128]{2,1,0:T(8,128)S(1)} %slice.42), channel_id=1, source_target_pairs={{0,1},{1,0},{2,3},{3,2},{4,5},{5,4},{6,7},{7,6},{8,9},{9,8},{10,11... | collective-permute-start | bytes 638984 | tf_op jit(solution)/shard_map/ppermute | solution.py:355
  9.0 5.8 %collective-permute-start.1 = (f32[208,128]{1,0:T(8,128)S(1)}, f32[208,128]{1,0:T(8,128)S(1)}, u32[]{:S(2)}, u32[]{:S(2)}) collective-permute-start(f32[208,128]{1,0:T(8,128)S(1)} %pad_maximum_fusion), channel_id=1, source_target_pairs={{0,2},{1,3},{2,0},{3,1},{4,6},{5,7},{6,4},{7,5},{8,10},{9,11},{10,... | collective-permute-start | bytes 319496 | tf_op jit(solution)/shard_map/ppermute | solution.py:355
  10.6 11.0 %copy-start = (f32[768,400]{0,1:T(8,128)S(1)}, f32[768,400]{0,1:T(8,128)}, u32[]{:S(2)}) copy-start(f32[768,400]{0,1:T(8,128)} %param.14) | copy-start | bytes 3686404
  10.6 11.0 %copy-start.1 = (f32[128,400]{0,1:T(8,128)S(1)}, f32[128,400]{0,1:T(8,128)}, u32[]{:S(2)}) copy-start(f32[128,400]{0,1:T(8,128)} %param.10) | copy-start | bytes 614404
  10.6 11.0 %copy-start.2 = (s32[2,256]{1,0:T(2,128)S(1)}, s32[2,256]{1,0:T(2,128)}, u32[]{:S(2)}) copy-start(s32[2,256]{1,0:T(2,128)} %refs_6_.1) | copy-start | bytes 6148
  10.6 11.0 %copy-start.3 = (s32[2,256]{1,0:T(2,128)S(1)}, s32[2,256]{1,0:T(2,128)}, u32[]{:S(2)}) copy-start(s32[2,256]{1,0:T(2,128)} %hid_ref.3) | copy-start | bytes 6148
  10.6 11.0 %copy-start.4 = (s32[2,256]{1,0:T(2,128)S(1)}, s32[2,256]{1,0:T(2,128)}, u32[]{:S(2)}) copy-start(s32[2,256]{1,0:T(2,128)} %tid_ref.1) | copy-start | bytes 6148
  10.6 11.0 %copy-start.5 = (s32[2,2,128]{2,1,0:T(2,128)S(1)}, s32[2,2,128]{2,1,0:T(2,128)}, u32[]{:S(2)}) copy-start(s32[2,2,128]{2,1,0:T(2,128)} %nid_ref.1) | copy-start | bytes 6148
  10.6 11.0 %copy-start.6 = (f32[128]{0:T(128)S(1)}, f32[128]{0:T(128)}, u32[]{:S(2)}) copy-start(f32[128]{0:T(128)} %param.11) | copy-start | bytes 1540
  10.7 7.4 %collective-permute-start.3 = (f32[208,128]{1,0:T(8,128)S(1)}, f32[208,128]{1,0:T(8,128)S(1)}, u32[]{:S(2)}, u32[]{:S(2)}) collective-permute-start(f32[208,128]{1,0:T(8,128)S(1)} %pad_maximum_fusion.1), channel_id=1, source_target_pairs={{0,6},{1,7},{2,4},{3,5},{4,2},{5,3},{6,0},{7,1},{8,14},{9,15},{10,... | collective-permute-start | bytes 319496 | tf_op jit(solution)/shard_map/ppermute | solution.py:355
  12.3 7.0 %collective-permute-start.4 = (f32[208,128]{1,0:T(8,128)S(1)}, f32[208,128]{1,0:T(8,128)S(1)}, u32[]{:S(2)}, u32[]{:S(2)}) collective-permute-start(f32[208,128]{1,0:T(8,128)S(1)} %pad_maximum_fusion.2), channel_id=1, source_target_pairs={{0,4},{1,5},{2,6},{3,7},{4,0},{5,1},{6,2},{7,3},{8,12},{9,13},{10,... | collective-permute-start | bytes 319496 | tf_op jit(solution)/shard_map/ppermute | solution.py:355
  19.7 7.9 %collective-permute-start.5 = (f32[304,128]{1,0:T(8,128)S(1)}, f32[304,128]{1,0:T(8,128)S(1)}, u32[]{:S(2)}, u32[]{:S(2)}) collective-permute-start(f32[304,128]{1,0:T(8,128)S(1)} %more_terms.8), channel_id=1, source_target_pairs={{0,12},{1,13},{2,14},{3,15},{4,8},{5,9},{6,10},{7,11},{8,4},{9,5},... | collective-permute-start | bytes 466952 | tf_op jit(solution)/shard_map/ppermute | solution.py:355
  27.6 7.7 %collective-permute-start.8 = (f32[304,128]{1,0:T(8,128)S(1)}, f32[304,128]{1,0:T(8,128)S(1)}, u32[]{:S(2)}, u32[]{:S(2)}) collective-permute-start(f32[304,128]{1,0:T(8,128)S(1)} %add.10.refs_0_), channel_id=1, source_target_pairs={{0,6},{1,7},{2,4},{3,5},{4,2},{5,3},{6,0},{7,1},{8,14},{9,15},{10,... | collective-permute-start | bytes 466952 | tf_op jit(solution)/shard_map/ppermute | solution.py:355
  29.6 6.6 %collective-permute-start.7 = (f32[304,128]{1,0:T(8,128)S(1)}, f32[304,128]{1,0:T(8,128)S(1)}, u32[]{:S(2)}, u32[]{:S(2)}) collective-permute-start(f32[304,128]{1,0:T(8,128)S(1)} %add.10.refs_0_), channel_id=1, source_target_pairs={{0,2},{1,3},{2,0},{3,1},{4,6},{5,7},{6,4},{7,5},{8,10},{9,11},{10,... | collective-permute-start | bytes 466952 | tf_op jit(solution)/shard_map/ppermute | solution.py:355
  30.1 6.9 %collective-permute-start.6 = (f32[304,128]{1,0:T(8,128)S(1)}, f32[304,128]{1,0:T(8,128)S(1)}, u32[]{:S(2)}, u32[]{:S(2)}) collective-permute-start(f32[304,128]{1,0:T(8,128)S(1)} %add.10.refs_0_), channel_id=1, source_target_pairs={{0,4},{1,5},{2,6},{3,7},{4,0},{5,1},{6,2},{7,3},{8,12},{9,13},{10,... | collective-permute-start | bytes 466952 | tf_op jit(solution)/shard_map/ppermute | solution.py:355
  31.2 6.2 %collective-permute-start.9 = (f32[304,128]{1,0:T(8,128)S(1)}, f32[304,128]{1,0:T(8,128)S(1)}, u32[]{:S(2)}, u32[]{:S(2)}) collective-permute-start(f32[304,128]{1,0:T(8,128)S(1)} %add.10.refs_0_), channel_id=1, source_target_pairs={{0,1},{1,0},{2,3},{3,2},{4,5},{5,4},{6,7},{7,6},{8,9},{9,8},{10,11... | collective-permute-start | bytes 466952 | tf_op jit(solution)/shard_map/ppermute | solution.py:355
  35.4 2.0 %collective-permute-start.12 = (f32[304,128]{1,0:T(8,128)S(1)}, f32[304,128]{1,0:T(8,128)S(1)}, u32[]{:S(2)}, u32[]{:S(2)}) collective-permute-start(f32[304,128]{1,0:T(8,128)S(1)} %collective-permute-done.8.refs_3_), channel_id=1, source_target_pairs={{0,1},{1,0},{2,3},{3,2},{4,5},{5,4},{6,7},{7,6},{8,9},{9,8},{10,11... | collective-permute-start | bytes 466952 | tf_op jit(solution)/shard_map/ppermute | solution.py:355
  36.1 1.4 %collective-permute-start.11 = (f32[304,128]{1,0:T(8,128)S(1)}, f32[304,128]{1,0:T(8,128)S(1)}, u32[]{:S(2)}, u32[]{:S(2)}) collective-permute-start(f32[304,128]{1,0:T(8,128)S(1)} %collective-permute-done.7.refs_2_), channel_id=1, source_target_pairs={{0,1},{1,0},{2,3},{3,2},{4,5},{5,4},{6,7},{7,6},{8,9},{9,8},{10,11... | collective-permute-start | bytes 466952 | tf_op jit(solution)/shard_map/ppermute | solution.py:355
  37.0 1.4 %collective-permute-start.10 = (f32[304,128]{1,0:T(8,128)S(1)}, f32[304,128]{1,0:T(8,128)S(1)}, u32[]{:S(2)}, u32[]{:S(2)}) collective-permute-start(f32[304,128]{1,0:T(8,128)S(1)} %collective-permute-done.6.refs_1_), channel_id=1, source_target_pairs={{0,1},{1,0},{2,3},{3,2},{4,5},{5,4},{6,7},{7,6},{8,9},{9,8},{10,11... | collective-permute-start | bytes 466952 | tf_op jit(solution)/shard_map/ppermute | solution.py:355
  40.3 1.5 %collective-permute-start.13 = (f32[4,104,128]{2,1,0:T(8,128)S(1)}, f32[4,104,128]{2,1,0:T(8,128)S(1)}, u32[]{:S(2)}, u32[]{:S(2)}) collective-permute-start(f32[4,104,128]{2,1,0:T(8,128)S(1)} %slice.49), channel_id=1, source_target_pairs={{0,1},{1,0},{2,3},{3,2},{4,5},{5,4},{6,7},{7,6},{8,9},{9,8},{10,11... | collective-permute-start | bytes 638984 | tf_op jit(solution)/shard_map/ppermute | solution.py:355
  41.9 7.0 %collective-permute-start.14 = (f32[208,128]{1,0:T(8,128)S(1)}, f32[208,128]{1,0:T(8,128)S(1)}, u32[]{:S(2)}, u32[]{:S(2)}) collective-permute-start(f32[208,128]{1,0:T(8,128)S(1)} %pad_maximum_fusion.3), channel_id=1, source_target_pairs={{0,2},{1,3},{2,0},{3,1},{4,6},{5,7},{6,4},{7,5},{8,10},{9,11},{10,... | collective-permute-start | bytes 319496 | tf_op jit(solution)/shard_map/ppermute | solution.py:355
  42.8 6.8 %collective-permute-start.15 = (f32[208,128]{1,0:T(8,128)S(1)}, f32[208,128]{1,0:T(8,128)S(1)}, u32[]{:S(2)}, u32[]{:S(2)}) collective-permute-start(f32[208,128]{1,0:T(8,128)S(1)} %pad_maximum_fusion.4), channel_id=1, source_target_pairs={{0,6},{1,7},{2,4},{3,5},{4,2},{5,3},{6,0},{7,1},{8,14},{9,15},{10,... | collective-permute-start | bytes 319496 | tf_op jit(solution)/shard_map/ppermute | solution.py:355
  44.0 6.6 %collective-permute-start.16 = (f32[208,128]{1,0:T(8,128)S(1)}, f32[208,128]{1,0:T(8,128)S(1)}, u32[]{:S(2)}, u32[]{:S(2)}) collective-permute-start(f32[208,128]{1,0:T(8,128)S(1)} %pad_maximum_fusion.5), channel_id=1, source_target_pairs={{0,4},{1,5},{2,6},{3,7},{4,0},{5,1},{6,2},{7,3},{8,12},{9,13},{10,... | collective-permute-start | bytes 319496 | tf_op jit(solution)/shard_map/ppermute | solution.py:355
  51.0 7.2 %collective-permute-start.17 = (f32[304,128]{1,0:T(8,128)S(1)}, f32[304,128]{1,0:T(8,128)S(1)}, u32[]{:S(2)}, u32[]{:S(2)}) collective-permute-start(f32[304,128]{1,0:T(8,128)S(1)} %more_terms.11), channel_id=1, source_target_pairs={{0,12},{1,13},{2,14},{3,15},{4,8},{5,9},{6,10},{7,11},{8,4},{9,5},... | collective-permute-start | bytes 466952 | tf_op jit(solution)/shard_map/ppermute | solution.py:355
  58.1 6.6 %collective-permute-start.20 = (f32[304,128]{1,0:T(8,128)S(1)}, f32[304,128]{1,0:T(8,128)S(1)}, u32[]{:S(2)}, u32[]{:S(2)}) collective-permute-start(f32[304,128]{1,0:T(8,128)S(1)} %add.11.refs_0_), channel_id=1, source_target_pairs={{0,6},{1,7},{2,4},{3,5},{4,2},{5,3},{6,0},{7,1},{8,14},{9,15},{10,... | collective-permute-start | bytes 466952 | tf_op jit(solution)/shard_map/ppermute | solution.py:355
  60.6 5.7 %collective-permute-start.19 = (f32[304,128]{1,0:T(8,128)S(1)}, f32[304,128]{1,0:T(8,128)S(1)}, u32[]{:S(2)}, u32[]{:S(2)}) collective-permute-start(f32[304,128]{1,0:T(8,128)S(1)} %add.11.refs_0_), channel_id=1, source_target_pairs={{0,2},{1,3},{2,0},{3,1},{4,6},{5,7},{6,4},{7,5},{8,10},{9,11},{10,... | collective-permute-start | bytes 466952 | tf_op jit(solution)/shard_map/ppermute | solution.py:355
  61.6 5.2 %collective-permute-start.18 = (f32[304,128]{1,0:T(8,128)S(1)}, f32[304,128]{1,0:T(8,128)S(1)}, u32[]{:S(2)}, u32[]{:S(2)}) collective-permute-start(f32[304,128]{1,0:T(8,128)S(1)} %add.11.refs_0_), channel_id=1, source_target_pairs={{0,4},{1,5},{2,6},{3,7},{4,0},{5,1},{6,2},{7,3},{8,12},{9,13},{10,... | collective-permute-start | bytes 466952 | tf_op jit(solution)/shard_map/ppermute | solution.py:355
  61.7 5.2 %collective-permute-start.21 = (f32[304,128]{1,0:T(8,128)S(1)}, f32[304,128]{1,0:T(8,128)S(1)}, u32[]{:S(2)}, u32[]{:S(2)}) collective-permute-start(f32[304,128]{1,0:T(8,128)S(1)} %add.11.refs_0_), channel_id=1, source_target_pairs={{0,1},{1,0},{2,3},{3,2},{4,5},{5,4},{6,7},{7,6},{8,9},{9,8},{10,11... | collective-permute-start | bytes 466952 | tf_op jit(solution)/shard_map/ppermute | solution.py:355
  64.7 2.1 %collective-permute-start.24 = (f32[304,128]{1,0:T(8,128)S(1)}, f32[304,128]{1,0:T(8,128)S(1)}, u32[]{:S(2)}, u32[]{:S(2)}) collective-permute-start(f32[304,128]{1,0:T(8,128)S(1)} %collective-permute-done.20.refs_3_), channel_id=1, source_target_pairs={{0,1},{1,0},{2,3},{3,2},{4,5},{5,4},{6,7},{7,6},{8,9},{9,8},{10,11... | collective-permute-start | bytes 466952 | tf_op jit(solution)/shard_map/ppermute | solution.py:355
  66.4 1.4 %collective-permute-start.23 = (f32[304,128]{1,0:T(8,128)S(1)}, f32[304,128]{1,0:T(8,128)S(1)}, u32[]{:S(2)}, u32[]{:S(2)}) collective-permute-start(f32[304,128]{1,0:T(8,128)S(1)} %collective-permute-done.19.refs_2_), channel_id=1, source_target_pairs={{0,1},{1,0},{2,3},{3,2},{4,5},{5,4},{6,7},{7,6},{8,9},{9,8},{10,11... | collective-permute-start | bytes 466952 | tf_op jit(solution)/shard_map/ppermute | solution.py:355
  66.9 1.4 %collective-permute-start.22 = (f32[304,128]{1,0:T(8,128)S(1)}, f32[304,128]{1,0:T(8,128)S(1)}, u32[]{:S(2)}, u32[]{:S(2)}) collective-permute-start(f32[304,128]{1,0:T(8,128)S(1)} %collective-permute-done.18.refs_1_), channel_id=1, source_target_pairs={{0,1},{1,0},{2,3},{3,2},{4,5},{5,4},{6,7},{7,6},{8,9},{9,8},{10,11... | collective-permute-start | bytes 466952 | tf_op jit(solution)/shard_map/ppermute | solution.py:355
  (1 other events, 11.0 us)

commit v6 on v5

--- a/solution.py
+++ b/solution.py
@@ -29,10 +29,14 @@
     return lax.dot_general(a, b, (((1,), (1,)), ((), ())), preferred_element_type=F32)
 
 
+def stack(x):
+    high = x.astype(BF16).astype(F32)
+    return jnp.concatenate([high, x - high], axis=0).astype(BF16)
+
+
 def times_selector(dot, x, selector):
-    high, low = halves(x)
     rows = x.shape[0]
-    both = dot(jnp.concatenate([high, low], axis=0), selector)
+    both = dot(stack(x), selector)
     return both[:rows] + both[rows:]
 
 
@@ -69,10 +73,6 @@
     b_high, b_low = halves(b)
     both = dot(a_both, b_high)
     return both[:rows] + (both[rows:] + dot(a_both[:rows], b_low))
-
-
-def stack(x):
-    return jnp.concatenate(halves(x), axis=0)
 
 
 def score(right_turned, query, named, tail_sel):

time: 70.4 us -> 70.3 us (level)
  no operation moved by 1% of the time
where the time goes in v6:
time: 70.3 us; the launch traced here: 70.2 us
  waiting for transfers between devices  34.5 us (49%)
  starting transfers between devices  20.2 us (29%)
  Pallas kernels  14.3 us (20%)
  between operations  0.94 us (1%)
    ppermute x24, waiting for transfers between devices, swap(): return lax.ppermute(x, AXES, route)  32.9 us
    ppermute x24, starting transfers between devices, swap(): return lax.ppermute(x, AXES, route)  17.1 us
    pallas_call x14, Pallas kernels, run(): pl.pallas_call(kernel, out_shape=[jax.ShapeDtypeStruct(shape, F32) if isi...  10.6 us
    pallas_call x1, Pallas kernels, shards(): pl.pallas_call(first_kernel, out_shape=[jax.ShapeDtypeStruct(shape, F32)...  3.7 us
    ppermute x1, starting transfers between devices, from_behind(): return lax.ppermute(block, axis, [((i - 1) % n, i) for i in range(n)])  3.07 us
    ppermute x1, waiting for transfers between devices, from_behind(): return lax.ppermute(block, axis, [((i - 1) % n, i) for i in range(n)])  1.63 us
  transfers between devices with their start and end apart: 25, of which 20 were waited for; matrix products, arithmetic and copies ran while one was open for 0% of the time, Pallas kernels for 8%

profile of v6, /device:TPU:0, one launch (start us, length us, event | category | flops | bytes accessed | tf_op | source)
XLA Modules:
  0.0 70.2 jit_solution(15785289916185868451)
XLA Ops:
  0.7 3.7 %first_step.1 = (f32[408,128]{1,0:T(8,128)S(1)}, f32[8,104,128]{2,1,0:T(8,128)S(1)}, f32[400,256]{1,0:T(8,128)S(1)}) custom-call(s32[2]{0:T(128)S(1)} %pad_add_fusion.place_ref, s32[2,256]{1,0:T(2,128)} %hid_ref.3, s32[2,256]{1,0:T(2,128)} %tid_ref.1, s32[2,256]{1,0:T(2,128)} %refs_6_.1, s32[2,2,128]{2,1,0:T(2,128)} %nid_ref.1, f32[400,128]{1,0:T(8,128)} %bitcast.37, ...), custom_call_target="tpu_custom_call" | custom-call | tf_op jit(solution)/shard_map/first_step/pallas_call | solution.py:413
  4.4 3.1 %collective-permute-start.2 = (f32[408,128]{1,0:T(8,128)S(1)}, f32[408,128]{1,0:T(8,128)S(1)}, u32[]{:S(2)}, u32[]{:S(2)}) collective-permute-start(f32[408,128]{1,0:T(8,128)S(1)} %get-tuple-element.58), channel_id=1, source_target_pairs={{12,0},{0,4},{4,8},{8,12},{13,1},{1,5},{5,9},{9,13},{14,2},{2,6},{... | collective-permute-start | bytes 626696 | tf_op jit(solution)/shard_map/ppermute | solution.py:393
  7.5 1.4 %collective-permute-done.other_ref = f32[4,104,128]{2,1,0:T(8,128)S(1)} collective-permute-done((f32[4,104,128]{2,1,0:T(8,128)S(1)}, f32[4,104,128]{2,1,0:T(8,128)S(1)}, u32[]{:S(2)}, u32[]{:S(2)}) %collective-permute-start) | collective-permute-done | bytes 213024 | tf_op jit(solution)/shard_map/ppermute | solution.py:355
  9.0 1.6 %collective-permute-start.1 = (f32[208,128]{1,0:T(8,128)S(1)}, f32[208,128]{1,0:T(8,128)S(1)}, u32[]{:S(2)}, u32[]{:S(2)}) collective-permute-start(f32[208,128]{1,0:T(8,128)S(1)} %pad_maximum_fusion), channel_id=1, source_target_pairs={{0,2},{1,3},{2,0},{3,1},{4,6},{5,7},{6,4},{7,5},{8,10},{9,11},{10,... | collective-permute-start | bytes 319496 | tf_op jit(solution)/shard_map/ppermute | solution.py:355
  10.7 1.6 %collective-permute-start.3 = (f32[208,128]{1,0:T(8,128)S(1)}, f32[208,128]{1,0:T(8,128)S(1)}, u32[]{:S(2)}, u32[]{:S(2)}) collective-permute-start(f32[208,128]{1,0:T(8,128)S(1)} %pad_maximum_fusion.1), channel_id=1, source_target_pairs={{0,6},{1,7},{2,4},{3,5},{4,2},{5,3},{6,0},{7,1},{8,14},{9,15},{10,... | collective-permute-start | bytes 319496 | tf_op jit(solution)/shard_map/ppermute | solution.py:355
  13.2 1.6 %collective-permute-done.2.right_ref = f32[408,128]{1,0:T(8,128)S(1)} collective-permute-done((f32[408,128]{1,0:T(8,128)S(1)}, f32[408,128]{1,0:T(8,128)S(1)}, u32[]{:S(2)}, u32[]{:S(2)}) %collective-permute-start.2) | collective-permute-done | bytes 208928 | tf_op jit(solution)/shard_map/ppermute | solution.py:393
  15.2 2.8 %collective-permute-done.3.terms_ref = f32[208,128]{1,0:T(8,128)S(1)} collective-permute-done((f32[208,128]{1,0:T(8,128)S(1)}, f32[208,128]{1,0:T(8,128)S(1)}, u32[]{:S(2)}, u32[]{:S(2)}) %collective-permute-start.3) | collective-permute-done | bytes 106528 | tf_op jit(solution)/shard_map/ppermute | solution.py:355
  18.4 0.9 %collective-permute-done.4.terms_ref = f32[208,128]{1,0:T(8,128)S(1)} collective-permute-done((f32[208,128]{1,0:T(8,128)S(1)}, f32[208,128]{1,0:T(8,128)S(1)}, u32[]{:S(2)}, u32[]{:S(2)}) %collective-permute-start.4) | collective-permute-done | bytes 106528 | tf_op jit(solution)/shard_map/ppermute | solution.py:355
  19.7 1.8 %collective-permute-start.5 = (f32[304,128]{1,0:T(8,128)S(1)}, f32[304,128]{1,0:T(8,128)S(1)}, u32[]{:S(2)}, u32[]{:S(2)}) collective-permute-start(f32[304,128]{1,0:T(8,128)S(1)} %more_terms.8), channel_id=1, source_target_pairs={{0,12},{1,13},{2,14},{3,15},{4,8},{5,9},{6,10},{7,11},{8,4},{9,5},... | collective-permute-start | bytes 466952 | tf_op jit(solution)/shard_map/ppermute | solution.py:355
  21.6 1.1 %ready.1 = (f32[400,128]{1,0:T(8,128)S(1)}, f32[1,128]{1,0:T(1,128)S(1)}, f32[400,256]{1,0:T(8,128)S(1)}, bf16[256,400]{1,0:T(8,128)(2,1)S(1)}, bf16[800,128]{1,...) custom-call(f32[400,128]{1,0:T(8,128)S(1)} %bitcast.38, ...), custom_call_target="tpu_custom_call" | custom-call | bytes 4957184 | tf_op jit(solution)/shard_map/ready/pallas_call | solution.py:329
  22.7 4.9 %collective-permute-done.5 = f32[304,128]{1,0:T(8,128)S(1)} collective-permute-done((f32[304,128]{1,0:T(8,128)S(1)}, f32[304,128]{1,0:T(8,128)S(1)}, u32[]{:S(2)}, u32[]{:S(2)}) %collective-permute-start.5) | collective-permute-done | bytes 155680 | tf_op jit(solution)/shard_map/ppermute | solution.py:355
  27.6 2.0 %collective-permute-start.8 = (f32[304,128]{1,0:T(8,128)S(1)}, f32[304,128]{1,0:T(8,128)S(1)}, u32[]{:S(2)}, u32[]{:S(2)}) collective-permute-start(f32[304,128]{1,0:T(8,128)S(1)} %add.10.refs_0_), channel_id=1, source_target_pairs={{0,6},{1,7},{2,4},{3,5},{4,2},{5,3},{6,0},{7,1},{8,14},{9,15},{10,... | collective-permute-start | bytes 466952 | tf_op jit(solution)/shard_map/ppermute | solution.py:355
  30.1 1.1 %collective-permute-start.6 = (f32[304,128]{1,0:T(8,128)S(1)}, f32[304,128]{1,0:T(8,128)S(1)}, u32[]{:S(2)}, u32[]{:S(2)}) collective-permute-start(f32[304,128]{1,0:T(8,128)S(1)} %add.10.refs_0_), channel_id=1, source_target_pairs={{0,4},{1,5},{2,6},{3,7},{4,0},{5,1},{6,2},{7,3},{8,12},{9,13},{10,... | collective-permute-start | bytes 466952 | tf_op jit(solution)/shard_map/ppermute | solution.py:355
  31.2 4.2 %collective-permute-done.8.refs_3_ = f32[304,128]{1,0:T(8,128)S(1)} collective-permute-done((f32[304,128]{1,0:T(8,128)S(1)}, f32[304,128]{1,0:T(8,128)S(1)}, u32[]{:S(2)}, u32[]{:S(2)}) %collective-permute-start.8) | collective-permute-done | bytes 155680 | tf_op jit(solution)/shard_map/ppermute | solution.py:355
  35.4 0.8 %collective-permute-done.7.refs_2_ = f32[304,128]{1,0:T(8,128)S(1)} collective-permute-done((f32[304,128]{1,0:T(8,128)S(1)}, f32[304,128]{1,0:T(8,128)S(1)}, u32[]{:S(2)}, u32[]{:S(2)}) %collective-permute-start.7) | collective-permute-done | bytes 155680 | tf_op jit(solution)/shard_map/ppermute | solution.py:355
  36.1 0.9 %collective-permute-done.6.refs_1_ = f32[304,128]{1,0:T(8,128)S(1)} collective-permute-done((f32[304,128]{1,0:T(8,128)S(1)}, f32[304,128]{1,0:T(8,128)S(1)}, u32[]{:S(2)}, u32[]{:S(2)}) %collective-permute-start.6) | collective-permute-done | bytes 155680 | tf_op jit(solution)/shard_map/ppermute | solution.py:355
  37.5 0.9 %collective-permute-done.10.refs_3_.refs_5_ = f32[304,128]{1,0:T(8,128)S(1)} collective-permute-done((f32[304,128]{1,0:T(8,128)S(1)}, f32[304,128]{1,0:T(8,128)S(1)}, u32[]{:S(2)}, u32[]{:S(2)}) %collective-permute-start.10) | collective-permute-done | bytes 155680 | tf_op jit(solution)/shard_map/ppermute | solution.py:355
  38.4 1.9 %next_step.1 = (f32[8,104,128]{2,1,0:T(8,128)S(1)}, f32[400,256]{1,0:T(8,128)S(1)}, f32[400,256]{1,0:T(8,128)S(1)}, f32[128,256]{1,0:T(8,128)S(1)}) custom-call(s32[2]{0:T(128)S(1)} %pad_add_fusion.place_ref, f32[400,256]{1,0:T(8,128)S(1)} %get-tuple-element.72.heads_ref, bf16[256,400]{1,0:T(8,128)(2,1)S(1)} %get-tuple-element.73.turned_ref, ...), custom_call_target="tpu_custom_call" | custom-call | bytes 4893704 | tf_op jit(solution)/shard_map/next_step/pallas_call | solution.py:329
  40.6 1.3 %collective-permute-done.13.other_ref = f32[4,104,128]{2,1,0:T(8,128)S(1)} collective-permute-done((f32[4,104,128]{2,1,0:T(8,128)S(1)}, f32[4,104,128]{2,1,0:T(8,128)S(1)}, u32[]{:S(2)}, u32[]{:S(2)}) %collective-permute-start.13) | collective-permute-done | bytes 213024 | tf_op jit(solution)/shard_map/ppermute | solution.py:355
  41.9 0.9 %collective-permute-start.14 = (f32[208,128]{1,0:T(8,128)S(1)}, f32[208,128]{1,0:T(8,128)S(1)}, u32[]{:S(2)}, u32[]{:S(2)}) collective-permute-start(f32[208,128]{1,0:T(8,128)S(1)} %pad_maximum_fusion.3), channel_id=1, source_target_pairs={{0,2},{1,3},{2,0},{3,1},{4,6},{5,7},{6,4},{7,5},{8,10},{9,11},{10,... | collective-permute-start | bytes 319496 | tf_op jit(solution)/shard_map/ppermute | solution.py:355
  42.8 1.2 %collective-permute-start.15 = (f32[208,128]{1,0:T(8,128)S(1)}, f32[208,128]{1,0:T(8,128)S(1)}, u32[]{:S(2)}, u32[]{:S(2)}) collective-permute-start(f32[208,128]{1,0:T(8,128)S(1)} %pad_maximum_fusion.4), channel_id=1, source_target_pairs={{0,6},{1,7},{2,4},{3,5},{4,2},{5,3},{6,0},{7,1},{8,14},{9,15},{10,... | collective-permute-start | bytes 319496 | tf_op jit(solution)/shard_map/ppermute | solution.py:355
  44.0 1.6 %collective-permute-start.16 = (f32[208,128]{1,0:T(8,128)S(1)}, f32[208,128]{1,0:T(8,128)S(1)}, u32[]{:S(2)}, u32[]{:S(2)}) collective-permute-start(f32[208,128]{1,0:T(8,128)S(1)} %pad_maximum_fusion.5), channel_id=1, source_target_pairs={{0,4},{1,5},{2,6},{3,7},{4,0},{5,1},{6,2},{7,3},{8,12},{9,13},{10,... | collective-permute-start | bytes 319496 | tf_op jit(solution)/shard_map/ppermute | solution.py:355
  46.0 2.9 %collective-permute-done.14.terms_ref = f32[208,128]{1,0:T(8,128)S(1)} collective-permute-done((f32[208,128]{1,0:T(8,128)S(1)}, f32[208,128]{1,0:T(8,128)S(1)}, u32[]{:S(2)}, u32[]{:S(2)}) %collective-permute-start.14) | collective-permute-done | bytes 106528 | tf_op jit(solution)/shard_map/ppermute | solution.py:355
  51.5 1.2 %last_update.1 = (f32[400,128]{1,0:T(8,128)}, f32[128]{0:T(128)}, f32[400,128]{1,0:T(8,128)}, f32[128]{0:T(128)}) custom-call(f32[400,128]{1,0:T(8,128)S(1)} %get-tuple-element.86.left_ref, f32[1,128]{1,0:T(1,128)S(1)} %get-tuple-element.87.lacc_ref, f32[400,256]{1,0:T(8,128)S(1)} %get-tuple-element.88.carry_ref, s32[2,256]{1,0:T(2,128)S(1)} %copy-done.3, ...), custom_call_target="tpu_custom_call" | custom-call | bytes 1777152 | tf_op jit(solution)/shard_map/last_update/pallas_call | solution.py:329
  52.7 0.9 %relations.1 = (f32[400,768]{1,0:T(8,128)S(1)}, f32[1,768]{1,0:T(1,128)S(1)}) custom-call(s32[2]{0:T(128)S(1)} %pad_add_fusion.place_ref, f32[400,768]{1,0:T(8,128)S(1)} %bitcast.36, f32[1,768]{1,0:T(1,128)S(1)} %broadcast_in_dim.10.relacc_ref, f32[304,128]{1,0:T(8,128)S(1)} %add.10.refs_0_, f32[304,128]{1,0:T(8,128)S(1)} %collective-permute-done.6.refs_1_, ...), custom_call_target="tpu_custom_call" | custom-call | bytes 3708936 | tf_op jit(solution)/shard_map/relations/pallas_call | solution.py:329
  53.6 4.5 %collective-permute-done.17 = f32[304,128]{1,0:T(8,128)S(1)} collective-permute-done((f32[304,128]{1,0:T(8,128)S(1)}, f32[304,128]{1,0:T(8,128)S(1)}, u32[]{:S(2)}, u32[]{:S(2)}) %collective-permute-start.17) | collective-permute-done | bytes 155680 | tf_op jit(solution)/shard_map/ppermute | solution.py:355
  58.1 2.5 %collective-permute-start.20 = (f32[304,128]{1,0:T(8,128)S(1)}, f32[304,128]{1,0:T(8,128)S(1)}, u32[]{:S(2)}, u32[]{:S(2)}) collective-permute-start(f32[304,128]{1,0:T(8,128)S(1)} %add.11.refs_0_), channel_id=1, source_target_pairs={{0,6},{1,7},{2,4},{3,5},{4,2},{5,3},{6,0},{7,1},{8,14},{9,15},{10,... | collective-permute-start | bytes 466952 | tf_op jit(solution)/shard_map/ppermute | solution.py:355
  60.6 1.0 %collective-permute-start.19 = (f32[304,128]{1,0:T(8,128)S(1)}, f32[304,128]{1,0:T(8,128)S(1)}, u32[]{:S(2)}, u32[]{:S(2)}) collective-permute-start(f32[304,128]{1,0:T(8,128)S(1)} %add.11.refs_0_), channel_id=1, source_target_pairs={{0,2},{1,3},{2,0},{3,1},{4,6},{5,7},{6,4},{7,5},{8,10},{9,11},{10,... | collective-permute-start | bytes 466952 | tf_op jit(solution)/shard_map/ppermute | solution.py:355
  61.7 3.0 %collective-permute-done.20.refs_3_ = f32[304,128]{1,0:T(8,128)S(1)} collective-permute-done((f32[304,128]{1,0:T(8,128)S(1)}, f32[304,128]{1,0:T(8,128)S(1)}, u32[]{:S(2)}, u32[]{:S(2)}) %collective-permute-start.20) | collective-permute-done | bytes 155680 | tf_op jit(solution)/shard_map/ppermute | solution.py:355
  64.7 1.6 %collective-permute-done.19.refs_2_ = f32[304,128]{1,0:T(8,128)S(1)} collective-permute-done((f32[304,128]{1,0:T(8,128)S(1)}, f32[304,128]{1,0:T(8,128)S(1)}, u32[]{:S(2)}, u32[]{:S(2)}) %collective-permute-start.19) | collective-permute-done | bytes 155680 | tf_op jit(solution)/shard_map/ppermute | solution.py:355
  66.9 0.9 %collective-permute-done.23.refs_6_ = f32[304,128]{1,0:T(8,128)S(1)} collective-permute-done((f32[304,128]{1,0:T(8,128)S(1)}, f32[304,128]{1,0:T(8,128)S(1)}, u32[]{:S(2)}, u32[]{:S(2)}) %collective-permute-start.23) | collective-permute-done | bytes 155680 | tf_op jit(solution)/shard_map/ppermute | solution.py:355
  68.2 2.0 %last_relations.1 = (f32[400,768]{1,0:T(8,128)}, f32[768]{0:T(1024)}) custom-call(s32[2]{0:T(128)S(1)} %pad_add_fusion.place_ref, f32[400,768]{1,0:T(8,128)S(1)} %get-tuple-element.99.rel_ref, f32[1,768]{1,0:T(1,128)S(1)} %get-tuple-element.100.relacc_ref, f32[304,128]{1,0:T(8,128)S(1)} %add.11.refs_0_, f32[304,128]{1,0:T(8,128)S(1)} %collective-permute-done.18.refs_1_, ...), custom_call_target="tpu_custom_call" | custom-call | bytes 3708936 | tf_op jit(solution)/shard_map/last_relations/pallas_call | solution.py:329
  (65 shorter events, 7.7 us)
Async XLA Ops:
  4.4 10.4 %collective-permute-start.2 = (f32[408,128]{1,0:T(8,128)S(1)}, f32[408,128]{1,0:T(8,128)S(1)}, u32[]{:S(2)}, u32[]{:S(2)}) collective-permute-start(f32[408,128]{1,0:T(8,128)S(1)} %get-tuple-element.58), channel_id=1, source_target_pairs={{12,0},{0,4},{4,8},{8,12},{13,1},{1,5},{5,9},{9,13},{14,2},{2,6},{... | collective-permute-start | bytes 626696 | tf_op jit(solution)/shard_map/ppermute | solution.py:393
  7.5 1.5 %collective-permute-start = (f32[4,104,128]{2,1,0:T(8,128)S(1)}, f32[4,104,128]{2,1,0:T(8,128)S(1)}, u32[]{:S(2)}, u32[]{:S(2)}) collective-permute-start(f32[4,104,128]{2,1,0:T(8,128)S(1)} %slice.42), channel_id=1, source_target_pairs={{0,1},{1,0},{2,3},{3,2},{4,5},{5,4},{6,7},{7,6},{8,9},{9,8},{10,11... | collective-permute-start | bytes 638984 | tf_op jit(solution)/shard_map/ppermute | solution.py:355
  9.0 5.8 %collective-permute-start.1 = (f32[208,128]{1,0:T(8,128)S(1)}, f32[208,128]{1,0:T(8,128)S(1)}, u32[]{:S(2)}, u32[]{:S(2)}) collective-permute-start(f32[208,128]{1,0:T(8,128)S(1)} %pad_maximum_fusion), channel_id=1, source_target_pairs={{0,2},{1,3},{2,0},{3,1},{4,6},{5,7},{6,4},{7,5},{8,10},{9,11},{10,... | collective-permute-start | bytes 319496 | tf_op jit(solution)/shard_map/ppermute | solution.py:355
  10.6 10.9 %copy-start = (f32[768,400]{0,1:T(8,128)S(1)}, f32[768,400]{0,1:T(8,128)}, u32[]{:S(2)}) copy-start(f32[768,400]{0,1:T(8,128)} %param.14) | copy-start | bytes 3686404
  10.6 10.9 %copy-start.1 = (f32[128,400]{0,1:T(8,128)S(1)}, f32[128,400]{0,1:T(8,128)}, u32[]{:S(2)}) copy-start(f32[128,400]{0,1:T(8,128)} %param.10) | copy-start | bytes 614404
  10.6 11.0 %copy-start.2 = (s32[2,256]{1,0:T(2,128)S(1)}, s32[2,256]{1,0:T(2,128)}, u32[]{:S(2)}) copy-start(s32[2,256]{1,0:T(2,128)} %refs_6_.1) | copy-start | bytes 6148
  10.6 11.0 %copy-start.3 = (s32[2,256]{1,0:T(2,128)S(1)}, s32[2,256]{1,0:T(2,128)}, u32[]{:S(2)}) copy-start(s32[2,256]{1,0:T(2,128)} %hid_ref.3) | copy-start | bytes 6148
  10.6 11.0 %copy-start.4 = (s32[2,256]{1,0:T(2,128)S(1)}, s32[2,256]{1,0:T(2,128)}, u32[]{:S(2)}) copy-start(s32[2,256]{1,0:T(2,128)} %tid_ref.1) | copy-start | bytes 6148
  10.6 11.0 %copy-start.5 = (s32[2,2,128]{2,1,0:T(2,128)S(1)}, s32[2,2,128]{2,1,0:T(2,128)}, u32[]{:S(2)}) copy-start(s32[2,2,128]{2,1,0:T(2,128)} %nid_ref.1) | copy-start | bytes 6148
  10.6 11.0 %copy-start.6 = (f32[128]{0:T(128)S(1)}, f32[128]{0:T(128)}, u32[]{:S(2)}) copy-start(f32[128]{0:T(128)} %param.11) | copy-start | bytes 1540
  10.7 7.4 %collective-permute-start.3 = (f32[208,128]{1,0:T(8,128)S(1)}, f32[208,128]{1,0:T(8,128)S(1)}, u32[]{:S(2)}, u32[]{:S(2)}) collective-permute-start(f32[208,128]{1,0:T(8,128)S(1)} %pad_maximum_fusion.1), channel_id=1, source_target_pairs={{0,6},{1,7},{2,4},{3,5},{4,2},{5,3},{6,0},{7,1},{8,14},{9,15},{10,... | collective-permute-start | bytes 319496 | tf_op jit(solution)/shard_map/ppermute | solution.py:355
  12.3 7.0 %collective-permute-start.4 = (f32[208,128]{1,0:T(8,128)S(1)}, f32[208,128]{1,0:T(8,128)S(1)}, u32[]{:S(2)}, u32[]{:S(2)}) collective-permute-start(f32[208,128]{1,0:T(8,128)S(1)} %pad_maximum_fusion.2), channel_id=1, source_target_pairs={{0,4},{1,5},{2,6},{3,7},{4,0},{5,1},{6,2},{7,3},{8,12},{9,13},{10,... | collective-permute-start | bytes 319496 | tf_op jit(solution)/shard_map/ppermute | solution.py:355
  19.7 7.9 %collective-permute-start.5 = (f32[304,128]{1,0:T(8,128)S(1)}, f32[304,128]{1,0:T(8,128)S(1)}, u32[]{:S(2)}, u32[]{:S(2)}) collective-permute-start(f32[304,128]{1,0:T(8,128)S(1)} %more_terms.8), channel_id=1, source_target_pairs={{0,12},{1,13},{2,14},{3,15},{4,8},{5,9},{6,10},{7,11},{8,4},{9,5},... | collective-permute-start | bytes 466952 | tf_op jit(solution)/shard_map/ppermute | solution.py:355
  27.6 7.7 %collective-permute-start.8 = (f32[304,128]{1,0:T(8,128)S(1)}, f32[304,128]{1,0:T(8,128)S(1)}, u32[]{:S(2)}, u32[]{:S(2)}) collective-permute-start(f32[304,128]{1,0:T(8,128)S(1)} %add.10.refs_0_), channel_id=1, source_target_pairs={{0,6},{1,7},{2,4},{3,5},{4,2},{5,3},{6,0},{7,1},{8,14},{9,15},{10,... | collective-permute-start | bytes 466952 | tf_op jit(solution)/shard_map/ppermute | solution.py:355
  29.6 6.6 %collective-permute-start.7 = (f32[304,128]{1,0:T(8,128)S(1)}, f32[304,128]{1,0:T(8,128)S(1)}, u32[]{:S(2)}, u32[]{:S(2)}) collective-permute-start(f32[304,128]{1,0:T(8,128)S(1)} %add.10.refs_0_), channel_id=1, source_target_pairs={{0,2},{1,3},{2,0},{3,1},{4,6},{5,7},{6,4},{7,5},{8,10},{9,11},{10,... | collective-permute-start | bytes 466952 | tf_op jit(solution)/shard_map/ppermute | solution.py:355
  30.1 6.9 %collective-permute-start.6 = (f32[304,128]{1,0:T(8,128)S(1)}, f32[304,128]{1,0:T(8,128)S(1)}, u32[]{:S(2)}, u32[]{:S(2)}) collective-permute-start(f32[304,128]{1,0:T(8,128)S(1)} %add.10.refs_0_), channel_id=1, source_target_pairs={{0,4},{1,5},{2,6},{3,7},{4,0},{5,1},{6,2},{7,3},{8,12},{9,13},{10,... | collective-permute-start | bytes 466952 | tf_op jit(solution)/shard_map/ppermute | solution.py:355
  31.2 6.2 %collective-permute-start.9 = (f32[304,128]{1,0:T(8,128)S(1)}, f32[304,128]{1,0:T(8,128)S(1)}, u32[]{:S(2)}, u32[]{:S(2)}) collective-permute-start(f32[304,128]{1,0:T(8,128)S(1)} %add.10.refs_0_), channel_id=1, source_target_pairs={{0,1},{1,0},{2,3},{3,2},{4,5},{5,4},{6,7},{7,6},{8,9},{9,8},{10,11... | collective-permute-start | bytes 466952 | tf_op jit(solution)/shard_map/ppermute | solution.py:355
  35.4 2.0 %collective-permute-start.12 = (f32[304,128]{1,0:T(8,128)S(1)}, f32[304,128]{1,0:T(8,128)S(1)}, u32[]{:S(2)}, u32[]{:S(2)}) collective-permute-start(f32[304,128]{1,0:T(8,128)S(1)} %collective-permute-done.8.refs_3_), channel_id=1, source_target_pairs={{0,1},{1,0},{2,3},{3,2},{4,5},{5,4},{6,7},{7,6},{8,9},{9,8},{10,11... | collective-permute-start | bytes 466952 | tf_op jit(solution)/shard_map/ppermute | solution.py:355
  36.1 1.4 %collective-permute-start.11 = (f32[304,128]{1,0:T(8,128)S(1)}, f32[304,128]{1,0:T(8,128)S(1)}, u32[]{:S(2)}, u32[]{:S(2)}) collective-permute-start(f32[304,128]{1,0:T(8,128)S(1)} %collective-permute-done.7.refs_2_), channel_id=1, source_target_pairs={{0,1},{1,0},{2,3},{3,2},{4,5},{5,4},{6,7},{7,6},{8,9},{9,8},{10,11... | collective-permute-start | bytes 466952 | tf_op jit(solution)/shard_map/ppermute | solution.py:355
  37.0 1.4 %collective-permute-start.10 = (f32[304,128]{1,0:T(8,128)S(1)}, f32[304,128]{1,0:T(8,128)S(1)}, u32[]{:S(2)}, u32[]{:S(2)}) collective-permute-start(f32[304,128]{1,0:T(8,128)S(1)} %collective-permute-done.6.refs_1_), channel_id=1, source_target_pairs={{0,1},{1,0},{2,3},{3,2},{4,5},{5,4},{6,7},{7,6},{8,9},{9,8},{10,11... | collective-permute-start | bytes 466952 | tf_op jit(solution)/shard_map/ppermute | solution.py:355
  40.3 1.5 %collective-permute-start.13 = (f32[4,104,128]{2,1,0:T(8,128)S(1)}, f32[4,104,128]{2,1,0:T(8,128)S(1)}, u32[]{:S(2)}, u32[]{:S(2)}) collective-permute-start(f32[4,104,128]{2,1,0:T(8,128)S(1)} %slice.49), channel_id=1, source_target_pairs={{0,1},{1,0},{2,3},{3,2},{4,5},{5,4},{6,7},{7,6},{8,9},{9,8},{10,11... | collective-permute-start | bytes 638984 | tf_op jit(solution)/shard_map/ppermute | solution.py:355
  41.9 7.0 %collective-permute-start.14 = (f32[208,128]{1,0:T(8,128)S(1)}, f32[208,128]{1,0:T(8,128)S(1)}, u32[]{:S(2)}, u32[]{:S(2)}) collective-permute-start(f32[208,128]{1,0:T(8,128)S(1)} %pad_maximum_fusion.3), channel_id=1, source_target_pairs={{0,2},{1,3},{2,0},{3,1},{4,6},{5,7},{6,4},{7,5},{8,10},{9,11},{10,... | collective-permute-start | bytes 319496 | tf_op jit(solution)/shard_map/ppermute | solution.py:355
  42.8 6.9 %collective-permute-start.15 = (f32[208,128]{1,0:T(8,128)S(1)}, f32[208,128]{1,0:T(8,128)S(1)}, u32[]{:S(2)}, u32[]{:S(2)}) collective-permute-start(f32[208,128]{1,0:T(8,128)S(1)} %pad_maximum_fusion.4), channel_id=1, source_target_pairs={{0,6},{1,7},{2,4},{3,5},{4,2},{5,3},{6,0},{7,1},{8,14},{9,15},{10,... | collective-permute-start | bytes 319496 | tf_op jit(solution)/shard_map/ppermute | solution.py:355
  44.0 6.6 %collective-permute-start.16 = (f32[208,128]{1,0:T(8,128)S(1)}, f32[208,128]{1,0:T(8,128)S(1)}, u32[]{:S(2)}, u32[]{:S(2)}) collective-permute-start(f32[208,128]{1,0:T(8,128)S(1)} %pad_maximum_fusion.5), channel_id=1, source_target_pairs={{0,4},{1,5},{2,6},{3,7},{4,0},{5,1},{6,2},{7,3},{8,12},{9,13},{10,... | collective-permute-start | bytes 319496 | tf_op jit(solution)/shard_map/ppermute | solution.py:355
  51.0 7.1 %collective-permute-start.17 = (f32[304,128]{1,0:T(8,128)S(1)}, f32[304,128]{1,0:T(8,128)S(1)}, u32[]{:S(2)}, u32[]{:S(2)}) collective-permute-start(f32[304,128]{1,0:T(8,128)S(1)} %more_terms.11), channel_id=1, source_target_pairs={{0,12},{1,13},{2,14},{3,15},{4,8},{5,9},{6,10},{7,11},{8,4},{9,5},... | collective-permute-start | bytes 466952 | tf_op jit(solution)/shard_map/ppermute | solution.py:355
  58.1 6.6 %collective-permute-start.20 = (f32[304,128]{1,0:T(8,128)S(1)}, f32[304,128]{1,0:T(8,128)S(1)}, u32[]{:S(2)}, u32[]{:S(2)}) collective-permute-start(f32[304,128]{1,0:T(8,128)S(1)} %add.11.refs_0_), channel_id=1, source_target_pairs={{0,6},{1,7},{2,4},{3,5},{4,2},{5,3},{6,0},{7,1},{8,14},{9,15},{10,... | collective-permute-start | bytes 466952 | tf_op jit(solution)/shard_map/ppermute | solution.py:355
  60.6 5.7 %collective-permute-start.19 = (f32[304,128]{1,0:T(8,128)S(1)}, f32[304,128]{1,0:T(8,128)S(1)}, u32[]{:S(2)}, u32[]{:S(2)}) collective-permute-start(f32[304,128]{1,0:T(8,128)S(1)} %add.11.refs_0_), channel_id=1, source_target_pairs={{0,2},{1,3},{2,0},{3,1},{4,6},{5,7},{6,4},{7,5},{8,10},{9,11},{10,... | collective-permute-start | bytes 466952 | tf_op jit(solution)/shard_map/ppermute | solution.py:355
  61.6 5.2 %collective-permute-start.18 = (f32[304,128]{1,0:T(8,128)S(1)}, f32[304,128]{1,0:T(8,128)S(1)}, u32[]{:S(2)}, u32[]{:S(2)}) collective-permute-start(f32[304,128]{1,0:T(8,128)S(1)} %add.11.refs_0_), channel_id=1, source_target_pairs={{0,4},{1,5},{2,6},{3,7},{4,0},{5,1},{6,2},{7,3},{8,12},{9,13},{10,... | collective-permute-start | bytes 466952 | tf_op jit(solution)/shard_map/ppermute | solution.py:355
  61.7 5.2 %collective-permute-start.21 = (f32[304,128]{1,0:T(8,128)S(1)}, f32[304,128]{1,0:T(8,128)S(1)}, u32[]{:S(2)}, u32[]{:S(2)}) collective-permute-start(f32[304,128]{1,0:T(8,128)S(1)} %add.11.refs_0_), channel_id=1, source_target_pairs={{0,1},{1,0},{2,3},{3,2},{4,5},{5,4},{6,7},{7,6},{8,9},{9,8},{10,11... | collective-permute-start | bytes 466952 | tf_op jit(solution)/shard_map/ppermute | solution.py:355
  64.7 2.1 %collective-permute-start.24 = (f32[304,128]{1,0:T(8,128)S(1)}, f32[304,128]{1,0:T(8,128)S(1)}, u32[]{:S(2)}, u32[]{:S(2)}) collective-permute-start(f32[304,128]{1,0:T(8,128)S(1)} %collective-permute-done.20.refs_3_), channel_id=1, source_target_pairs={{0,1},{1,0},{2,3},{3,2},{4,5},{5,4},{6,7},{7,6},{8,9},{9,8},{10,11... | collective-permute-start | bytes 466952 | tf_op jit(solution)/shard_map/ppermute | solution.py:355
  66.4 1.4 %collective-permute-start.23 = (f32[304,128]{1,0:T(8,128)S(1)}, f32[304,128]{1,0:T(8,128)S(1)}, u32[]{:S(2)}, u32[]{:S(2)}) collective-permute-start(f32[304,128]{1,0:T(8,128)S(1)} %collective-permute-done.19.refs_2_), channel_id=1, source_target_pairs={{0,1},{1,0},{2,3},{3,2},{4,5},{5,4},{6,7},{7,6},{8,9},{9,8},{10,11... | collective-permute-start | bytes 466952 | tf_op jit(solution)/shard_map/ppermute | solution.py:355
  66.8 1.4 %collective-permute-start.22 = (f32[304,128]{1,0:T(8,128)S(1)}, f32[304,128]{1,0:T(8,128)S(1)}, u32[]{:S(2)}, u32[]{:S(2)}) collective-permute-start(f32[304,128]{1,0:T(8,128)S(1)} %collective-permute-done.18.refs_1_), channel_id=1, source_target_pairs={{0,1},{1,0},{2,3},{3,2},{4,5},{5,4},{6,7},{7,6},{8,9},{9,8},{10,11... | collective-permute-start | bytes 466952 | tf_op jit(solution)/shard_map/ppermute | solution.py:355
  (1 other events, 10.9 us)

commit v7 on v6

--- a/solution.py
+++ b/solution.py
@@ -85,6 +85,14 @@
     return named * sig - tail_sel * sig_minus
 
 
+def gray(i):
+    return jnp.bitwise_and(jnp.bitwise_xor(i, i >> 1), 1)
+
+
+def place():
+    return gray(lax.axis_index("shard")) * 2 + gray(lax.axis_index("blk")), lax.axis_index("sub")
+
+
 def cut(width):
     main = width // (8 * PIECES) * 8
     return main, width // PIECES - main
@@ -98,8 +106,8 @@
     return edges // LANES * cut(width)[0] + 8
 
 
-def put_terms(place_ref, terms, kinds, out_ref):
-    square, core = place_ref[0], place_ref[1]
+def put_terms(terms, kinds, out_ref):
+    square, core = place()
     width, edges = terms.shape
     half = PIECES // 2
     main, rest = cut(width)
@@ -162,8 +170,8 @@
     put_piece(sum_terms(width, kinds, [terms_ref[:rows], terms_ref[rows:]]), width, out_ref, total_ref)
 
 
-def order_pieces(place_ref, piece_refs, all_ref):
-    square, core = place_ref[0], place_ref[1]
+def order_pieces(piece_refs, all_ref):
+    square, core = place()
     half = PIECES // 2
     for i in range(half):
         piece = jnp.bitwise_xor(square, i)
@@ -197,7 +205,7 @@
     out_ref[width:] = jnp.broadcast_to(acc, (8, acc.shape[1]))
 
 
-def first_kernel(place_ref, *refs):
+def first_kernel(*refs):
     given, (right_out, terms_out, carry_out), held, sems = refs[:8], refs[8:11], refs[11:19], refs[19]
     copies = [pltpu.make_async_copy(a, b, sems.at[i]) for i, (a, b) in enumerate(zip(given, held))]
     for copy in copies:
@@ -215,7 +223,7 @@
     query = heads * rel_rows
     weight = score(stack(right.T), query, *prepare(right, tid_ref[0:1], nid_ref[0]))
     grad_query = times(nn, right, weight)
-    put_terms(place_ref, grad_query * heads, kid_ref[0:1], terms_out)
+    put_terms(grad_query * heads, kid_ref[0:1], terms_out)
     put_packed(right_out, *adagrad(right, racc_ref[...], times(nt, query, weight)))
     carry_out[...] = grad_query * rel_rows
 
@@ -257,12 +265,12 @@
     refs[-1][...] = gather_pieces(refs[:-2], refs[-2][...], width)
 
 
-def next_kernel(step, place_ref, heads_ref, turned_ref, right_ref, named_ref, tail_ref, kind_ref, rows_ref, *refs):
+def next_kernel(step, heads_ref, turned_ref, right_ref, named_ref, tail_ref, kind_ref, rows_ref, *refs):
     state_ref, mine_ref, piece_refs, kid_ref = refs[0], refs[1], refs[2 : 2 + PIECES // 2], refs[2 + PIECES // 2]
     terms_out, carry_out, query_out, weight_out, main_ref, rest_ref = refs[3 + PIECES // 2 :]
     heads = heads_ref[...]
     width = heads.shape[0]
-    square, core = place_ref[0], place_ref[1]
+    square, core = place()
     half = PIECES // 2
     main, rest = cut(width)
     theirs = gather_pieces(piece_refs, kind_ref[...], width)
@@ -278,16 +286,16 @@
     query = heads * rel_rows
     weight = score(turned_ref[...], query, named_ref[...], tail_ref[...])
     grad_query = split_times(nn, right_ref[...], weight)
-    put_terms(place_ref, grad_query * heads, kid_ref[step : step + 1], terms_out)
+    put_terms(grad_query * heads, kid_ref[step : step + 1], terms_out)
     carry_out[...] = grad_query * rel_rows
     query_out[...] = query
     weight_out[...] = weight
 
 
-def relations_kernel(place_ref, rel_ref, relacc_ref, *refs):
+def relations_kernel(rel_ref, relacc_ref, *refs):
     piece_refs, (rel_out, relacc_out, all_ref) = refs[:PIECES], refs[PIECES:]
     width = rel_ref.shape[0]
-    order_pieces(place_ref, piece_refs, all_ref)
+    order_pieces(piece_refs, all_ref)
     accum, rate = next_accum(relacc_ref, all_ref, width)
     relacc_out[...] = accum[0] if len(relacc_out.shape) == 1 else accum
     blocks = rel_ref.shape[1] // LANES
@@ -318,18 +326,16 @@
 
 HBM = pl.BlockSpec(memory_space=pltpu.HBM)
 VMEM = pl.BlockSpec(memory_space=pltpu.VMEM)
-SMEM = pl.BlockSpec(memory_space=pltpu.SMEM)
 PARAMS = pltpu.CompilerParams(vmem_limit_bytes=40 * 1024 * 1024)
 
 
-def call(kernel, outs, scratch=(), smem=0, hbm_outs=(), name=None, flops=0):
+def call(kernel, outs, scratch=(), hbm_outs=(), name=None, flops=0):
     def run(*given):
         moved = sum(math.prod(x.shape) for x in given) + sum(math.prod(getattr(shape, "shape", shape)) for shape in outs)
-        in_specs = [SMEM if i < smem else VMEM for i in range(len(given))]
         return pl.pallas_call(
             kernel,
             out_shape=[jax.ShapeDtypeStruct(shape, F32) if isinstance(shape, tuple) else shape for shape in outs],
-            in_specs=in_specs,
+            in_specs=[VMEM] * len(given),
             out_specs=[HBM if i in hbm_outs else VMEM for i in range(len(outs))],
             scratch_shapes=list(scratch),
             compiler_params=PARAMS,
@@ -353,10 +359,6 @@
         for u in range(n_sub)
     ]
     return lax.ppermute(x, AXES, route)
-
-
-def gray(i):
-    return jnp.bitwise_and(jnp.bitwise_xor(i, i >> 1), 1)
 
 
 def sum_pieces(terms, sizes, width, kinds, beside=None, work=lambda _: ()):
@@ -400,9 +402,6 @@
     steps = head_ids.shape[0]
     rows, width = head_table.shape
     kinds = relations.shape[0]
-    core = lax.axis_index("sub")
-    square = gray(lax.axis_index("shard")) * 2 + gray(lax.axis_index("blk"))
-    place = jnp.stack([square, core]).astype(jnp.int32)
 
     left, lacc = head_table.T, head_accum[None]
     rel, relacc = relations.T, rel_accum[None]
@@ -413,12 +412,12 @@
     right, terms, carry = pl.pallas_call(
         first_kernel,
         out_shape=[jax.ShapeDtypeStruct(shape, F32) for shape in [(width + 8, rows), cut_terms, each]],
-        in_specs=[SMEM] + [HBM] * len(given),
+        in_specs=[HBM] * len(given),
         out_specs=[VMEM] * 3,
         scratch_shapes=[pltpu.VMEM(x.shape, x.dtype) for x in given] + [pltpu.SemaphoreType.DMA((len(given),))],
         compiler_params=PARAMS,
         name="first_step",
-    )(place, *[pltpu.with_memory_space_constraint(x, pltpu.HBM) for x in given])
+    )(*[pltpu.with_memory_space_constraint(x, pltpu.HBM) for x in given])
     all_pieces = pltpu.VMEM((PIECES, piece_rows(width, kinds), LANES), F32)
     half = PIECES // 2
     main, rest = cut(width)
@@ -427,9 +426,7 @@
         return jax.ShapeDtypeStruct(shape, BF16)
 
     def relations(rel, relacc, summed, shape, name):
-        return call(relations_kernel, [(width, kinds), shape], [all_pieces], smem=1, name=name)(
-            place, rel, relacc, *summed
-        )
+        return call(relations_kernel, [(width, kinds), shape], [all_pieces], name=name)(rel, relacc, *summed)
 
     summed = None
     for step in range(1, steps):
@@ -455,9 +452,8 @@
             functools.partial(next_kernel, step),
             [cut_terms, each, each, (rows, edges)],
             [pltpu.VMEM((PIECES, main, edges), F32), pltpu.VMEM((PIECES, 8, edges), F32)],
-            smem=1,
             name="next_step",
-        )(place, heads, turned, both, named, tail_sel, kind_sel, rel_rows, rel_state, mine, *summed[half:], rel_ids)
+        )(heads, turned, both, named, tail_sel, kind_sel, rel_rows, rel_state, mine, *summed[half:], rel_ids)
 
     def update(_):
         return *relations(rel, relacc, summed, (1, kinds), "relations"), *call(

time: 70.3 us -> 68.7 us (0.977)
  Pallas kernels: 14.3 us -> 12.1 us
    pallas_call x14, Pallas kernels: 10.6 us -> 8.99 us  [run(): pl.pallas_call(kernel, out_shape=[jax.ShapeDtypeStruct(shape, F32) if isi...]
where the time goes in v7:
time: 68.7 us; the launch traced here: 68.5 us
  waiting for transfers between devices  35.1 us (51%)
  starting transfers between devices  20.2 us (29%)
  Pallas kernels  12.1 us (18%)
  between operations  0.93 us (1%)
    ppermute x24, waiting for transfers between devices, swap(): return lax.ppermute(x, AXES, route)  33.4 us
    ppermute x24, starting transfers between devices, swap(): return lax.ppermute(x, AXES, route)  17.1 us
    pallas_call x14, Pallas kernels, run(): pl.pallas_call(kernel, out_shape=[jax.ShapeDtypeStruct(shape, F32) if isi...  8.99 us
    pallas_call x1, Pallas kernels, shards(): pl.pallas_call(first_kernel, out_shape=[jax.ShapeDtypeStruct(shape, F32)...  3.16 us
    ppermute x1, starting transfers between devices, from_behind(): return lax.ppermute(block, axis, [((i - 1) % n, i) for i in range(n)])  3.08 us
    ppermute x1, waiting for transfers between devices, from_behind(): return lax.ppermute(block, axis, [((i - 1) % n, i) for i in range(n)])  1.62 us
  transfers between devices with their start and end apart: 25, of which 20 were waited for; matrix products, arithmetic and copies ran while one was open for 0% of the time, Pallas kernels for 8%

profile of v7, /device:TPU:0, one launch (start us, length us, event | category | flops | bytes accessed | tf_op | source)
XLA Modules:
  0.0 68.5 jit_solution(12948469589077570846)
XLA Ops:
  0.6 3.2 %first_step.1 = (f32[408,128]{1,0:T(8,128)S(1)}, f32[8,104,128]{2,1,0:T(8,128)S(1)}, f32[400,256]{1,0:T(8,128)S(1)}) custom-call(s32[2,256]{1,0:T(2,128)} %hid_ref.3, s32[2,256]{1,0:T(2,128)} %tid_ref.1, s32[2,256]{1,0:T(2,128)} %refs_6_.1, s32[2,2,128]{2,1,0:T(2,128)} %nid_ref.1, f32[400,128]{1,0:T(8,128)} %bitcast.35, f32[400,128]{1,0:T(8,128)} %bitcast.38, ...), custom_call_target="tpu_custom_call" | custom-call | tf_op jit(solution)/shard_map/first_step/pallas_call | solution.py:412
  3.8 3.1 %collective-permute-start.2 = (f32[408,128]{1,0:T(8,128)S(1)}, f32[408,128]{1,0:T(8,128)S(1)}, u32[]{:S(2)}, u32[]{:S(2)}) collective-permute-start(f32[408,128]{1,0:T(8,128)S(1)} %get-tuple-element.58), channel_id=1, source_target_pairs={{12,0},{0,4},{4,8},{8,12},{13,1},{1,5},{5,9},{9,13},{14,2},{2,6},{... | collective-permute-start | bytes 626696 | tf_op jit(solution)/shard_map/ppermute | solution.py:395
  6.9 1.4 %collective-permute-done.other_ref = f32[4,104,128]{2,1,0:T(8,128)S(1)} collective-permute-done((f32[4,104,128]{2,1,0:T(8,128)S(1)}, f32[4,104,128]{2,1,0:T(8,128)S(1)}, u32[]{:S(2)}, u32[]{:S(2)}) %collective-permute-start) | collective-permute-done | bytes 213024 | tf_op jit(solution)/shard_map/ppermute | solution.py:361
  8.4 1.6 %collective-permute-start.1 = (f32[208,128]{1,0:T(8,128)S(1)}, f32[208,128]{1,0:T(8,128)S(1)}, u32[]{:S(2)}, u32[]{:S(2)}) collective-permute-start(f32[208,128]{1,0:T(8,128)S(1)} %pad_maximum_fusion), channel_id=1, source_target_pairs={{0,2},{1,3},{2,0},{3,1},{4,6},{5,7},{6,4},{7,5},{8,10},{9,11},{10,... | collective-permute-start | bytes 319496 | tf_op jit(solution)/shard_map/ppermute | solution.py:361
  10.0 1.6 %collective-permute-start.3 = (f32[208,128]{1,0:T(8,128)S(1)}, f32[208,128]{1,0:T(8,128)S(1)}, u32[]{:S(2)}, u32[]{:S(2)}) collective-permute-start(f32[208,128]{1,0:T(8,128)S(1)} %pad_maximum_fusion.1), channel_id=1, source_target_pairs={{0,6},{1,7},{2,4},{3,5},{4,2},{5,3},{6,0},{7,1},{8,14},{9,15},{10,... | collective-permute-start | bytes 319496 | tf_op jit(solution)/shard_map/ppermute | solution.py:361
  12.6 1.6 %collective-permute-done.2.right_ref = f32[408,128]{1,0:T(8,128)S(1)} collective-permute-done((f32[408,128]{1,0:T(8,128)S(1)}, f32[408,128]{1,0:T(8,128)S(1)}, u32[]{:S(2)}, u32[]{:S(2)}) %collective-permute-start.2) | collective-permute-done | bytes 208928 | tf_op jit(solution)/shard_map/ppermute | solution.py:395
  14.6 2.8 %collective-permute-done.3.terms_ref = f32[208,128]{1,0:T(8,128)S(1)} collective-permute-done((f32[208,128]{1,0:T(8,128)S(1)}, f32[208,128]{1,0:T(8,128)S(1)}, u32[]{:S(2)}, u32[]{:S(2)}) %collective-permute-start.3) | collective-permute-done | bytes 106528 | tf_op jit(solution)/shard_map/ppermute | solution.py:361
  17.8 0.9 %collective-permute-done.4.terms_ref = f32[208,128]{1,0:T(8,128)S(1)} collective-permute-done((f32[208,128]{1,0:T(8,128)S(1)}, f32[208,128]{1,0:T(8,128)S(1)}, u32[]{:S(2)}, u32[]{:S(2)}) %collective-permute-start.4) | collective-permute-done | bytes 106528 | tf_op jit(solution)/shard_map/ppermute | solution.py:361
  19.1 1.9 %collective-permute-start.5 = (f32[304,128]{1,0:T(8,128)S(1)}, f32[304,128]{1,0:T(8,128)S(1)}, u32[]{:S(2)}, u32[]{:S(2)}) collective-permute-start(f32[304,128]{1,0:T(8,128)S(1)} %more_terms.8), channel_id=1, source_target_pairs={{0,12},{1,13},{2,14},{3,15},{4,8},{5,9},{6,10},{7,11},{8,4},{9,5},... | collective-permute-start | bytes 466952 | tf_op jit(solution)/shard_map/ppermute | solution.py:361
  21.0 1.1 %ready.1 = (f32[400,128]{1,0:T(8,128)S(1)}, f32[1,128]{1,0:T(1,128)S(1)}, f32[400,256]{1,0:T(8,128)S(1)}, bf16[256,400]{1,0:T(8,128)(2,1)S(1)}, bf16[800,128]{1,...) custom-call(f32[400,128]{1,0:T(8,128)S(1)} %bitcast.36, ...), custom_call_target="tpu_custom_call" | custom-call | bytes 4957184 | tf_op jit(solution)/shard_map/ready/pallas_call | solution.py:335
  22.1 4.8 %collective-permute-done.5 = f32[304,128]{1,0:T(8,128)S(1)} collective-permute-done((f32[304,128]{1,0:T(8,128)S(1)}, f32[304,128]{1,0:T(8,128)S(1)}, u32[]{:S(2)}, u32[]{:S(2)}) %collective-permute-start.5) | collective-permute-done | bytes 155680 | tf_op jit(solution)/shard_map/ppermute | solution.py:361
  27.0 2.0 %collective-permute-start.8 = (f32[304,128]{1,0:T(8,128)S(1)}, f32[304,128]{1,0:T(8,128)S(1)}, u32[]{:S(2)}, u32[]{:S(2)}) collective-permute-start(f32[304,128]{1,0:T(8,128)S(1)} %add.6.refs_0_), channel_id=1, source_target_pairs={{0,6},{1,7},{2,4},{3,5},{4,2},{5,3},{6,0},{7,1},{8,14},{9,15},{10,... | collective-permute-start | bytes 466952 | tf_op jit(solution)/shard_map/ppermute | solution.py:361
  29.0 0.5 collective-permute-start.7
  29.5 1.1 %collective-permute-start.6 = (f32[304,128]{1,0:T(8,128)S(1)}, f32[304,128]{1,0:T(8,128)S(1)}, u32[]{:S(2)}, u32[]{:S(2)}) collective-permute-start(f32[304,128]{1,0:T(8,128)S(1)} %add.6.refs_0_), channel_id=1, source_target_pairs={{0,4},{1,5},{2,6},{3,7},{4,0},{5,1},{6,2},{7,3},{8,12},{9,13},{10,... | collective-permute-start | bytes 466952 | tf_op jit(solution)/shard_map/ppermute | solution.py:361
  30.6 4.2 %collective-permute-done.8.refs_3_ = f32[304,128]{1,0:T(8,128)S(1)} collective-permute-done((f32[304,128]{1,0:T(8,128)S(1)}, f32[304,128]{1,0:T(8,128)S(1)}, u32[]{:S(2)}, u32[]{:S(2)}) %collective-permute-start.8) | collective-permute-done | bytes 155680 | tf_op jit(solution)/shard_map/ppermute | solution.py:361
  34.7 0.8 %collective-permute-done.7.refs_2_ = f32[304,128]{1,0:T(8,128)S(1)} collective-permute-done((f32[304,128]{1,0:T(8,128)S(1)}, f32[304,128]{1,0:T(8,128)S(1)}, u32[]{:S(2)}, u32[]{:S(2)}) %collective-permute-start.7) | collective-permute-done | bytes 155680 | tf_op jit(solution)/shard_map/ppermute | solution.py:361
  35.5 0.9 %collective-permute-done.6.refs_1_ = f32[304,128]{1,0:T(8,128)S(1)} collective-permute-done((f32[304,128]{1,0:T(8,128)S(1)}, f32[304,128]{1,0:T(8,128)S(1)}, u32[]{:S(2)}, u32[]{:S(2)}) %collective-permute-start.6) | collective-permute-done | bytes 155680 | tf_op jit(solution)/shard_map/ppermute | solution.py:361
  36.9 0.9 %collective-permute-done.10.refs_3_.refs_5_ = f32[304,128]{1,0:T(8,128)S(1)} collective-permute-done((f32[304,128]{1,0:T(8,128)S(1)}, f32[304,128]{1,0:T(8,128)S(1)}, u32[]{:S(2)}, u32[]{:S(2)}) %collective-permute-start.10) | collective-permute-done | bytes 155680 | tf_op jit(solution)/shard_map/ppermute | solution.py:361
  37.8 1.4 %next_step.1 = (f32[8,104,128]{2,1,0:T(8,128)S(1)}, f32[400,256]{1,0:T(8,128)S(1)}, f32[400,256]{1,0:T(8,128)S(1)}, f32[128,256]{1,0:T(8,128)S(1)}) custom-call(f32[400,256]{1,0:T(8,128)S(1)} %get-tuple-element.72.heads_ref, bf16[256,400]{1,0:T(8,128)(2,1)S(1)} %get-tuple-element.73.turned_ref, bf16[800,128]{1,0:T(8,128)(2,1)S(1)} %get-tuple-element.74.right_ref, ...), custom_call_target="tpu_custom_call" | custom-call | bytes 4893696 | tf_op jit(solution)/shard_map/next_step/pallas_call | solution.py:335
  39.4 1.3 %collective-permute-done.13.other_ref = f32[4,104,128]{2,1,0:T(8,128)S(1)} collective-permute-done((f32[4,104,128]{2,1,0:T(8,128)S(1)}, f32[4,104,128]{2,1,0:T(8,128)S(1)}, u32[]{:S(2)}, u32[]{:S(2)}) %collective-permute-start.13) | collective-permute-done | bytes 213024 | tf_op jit(solution)/shard_map/ppermute | solution.py:361
  40.8 0.9 %collective-permute-start.14 = (f32[208,128]{1,0:T(8,128)S(1)}, f32[208,128]{1,0:T(8,128)S(1)}, u32[]{:S(2)}, u32[]{:S(2)}) collective-permute-start(f32[208,128]{1,0:T(8,128)S(1)} %pad_maximum_fusion.3), channel_id=1, source_target_pairs={{0,2},{1,3},{2,0},{3,1},{4,6},{5,7},{6,4},{7,5},{8,10},{9,11},{10,... | collective-permute-start | bytes 319496 | tf_op jit(solution)/shard_map/ppermute | solution.py:361
  41.7 1.2 %collective-permute-start.15 = (f32[208,128]{1,0:T(8,128)S(1)}, f32[208,128]{1,0:T(8,128)S(1)}, u32[]{:S(2)}, u32[]{:S(2)}) collective-permute-start(f32[208,128]{1,0:T(8,128)S(1)} %pad_maximum_fusion.4), channel_id=1, source_target_pairs={{0,6},{1,7},{2,4},{3,5},{4,2},{5,3},{6,0},{7,1},{8,14},{9,15},{10,... | collective-permute-start | bytes 319496 | tf_op jit(solution)/shard_map/ppermute | solution.py:361
  42.8 1.6 %collective-permute-start.16 = (f32[208,128]{1,0:T(8,128)S(1)}, f32[208,128]{1,0:T(8,128)S(1)}, u32[]{:S(2)}, u32[]{:S(2)}) collective-permute-start(f32[208,128]{1,0:T(8,128)S(1)} %pad_maximum_fusion.5), channel_id=1, source_target_pairs={{0,4},{1,5},{2,6},{3,7},{4,0},{5,1},{6,2},{7,3},{8,12},{9,13},{10,... | collective-permute-start | bytes 319496 | tf_op jit(solution)/shard_map/ppermute | solution.py:361
  44.9 2.9 %collective-permute-done.14.terms_ref = f32[208,128]{1,0:T(8,128)S(1)} collective-permute-done((f32[208,128]{1,0:T(8,128)S(1)}, f32[208,128]{1,0:T(8,128)S(1)}, u32[]{:S(2)}, u32[]{:S(2)}) %collective-permute-start.14) | collective-permute-done | bytes 106528 | tf_op jit(solution)/shard_map/ppermute | solution.py:361
  50.3 1.2 %last_update.1 = (f32[400,128]{1,0:T(8,128)}, f32[128]{0:T(128)}, f32[400,128]{1,0:T(8,128)}, f32[128]{0:T(128)}) custom-call(f32[400,128]{1,0:T(8,128)S(1)} %get-tuple-element.86.left_ref, f32[1,128]{1,0:T(1,128)S(1)} %get-tuple-element.87.lacc_ref, f32[400,256]{1,0:T(8,128)S(1)} %get-tuple-element.88.carry_ref, s32[2,256]{1,0:T(2,128)S(1)} %copy-done.2, ...), custom_call_target="tpu_custom_call" | custom-call | bytes 1777152 | tf_op jit(solution)/shard_map/last_update/pallas_call | solution.py:335
  51.9 5.0 %collective-permute-done.17 = f32[304,128]{1,0:T(8,128)S(1)} collective-permute-done((f32[304,128]{1,0:T(8,128)S(1)}, f32[304,128]{1,0:T(8,128)S(1)}, u32[]{:S(2)}, u32[]{:S(2)}) %collective-permute-start.17) | collective-permute-done | bytes 155680 | tf_op jit(solution)/shard_map/ppermute | solution.py:361
  57.0 2.5 %collective-permute-start.20 = (f32[304,128]{1,0:T(8,128)S(1)}, f32[304,128]{1,0:T(8,128)S(1)}, u32[]{:S(2)}, u32[]{:S(2)}) collective-permute-start(f32[304,128]{1,0:T(8,128)S(1)} %add.7.refs_0_), channel_id=1, source_target_pairs={{0,6},{1,7},{2,4},{3,5},{4,2},{5,3},{6,0},{7,1},{8,14},{9,15},{10,... | collective-permute-start | bytes 466952 | tf_op jit(solution)/shard_map/ppermute | solution.py:361
  59.5 1.0 %collective-permute-start.19 = (f32[304,128]{1,0:T(8,128)S(1)}, f32[304,128]{1,0:T(8,128)S(1)}, u32[]{:S(2)}, u32[]{:S(2)}) collective-permute-start(f32[304,128]{1,0:T(8,128)S(1)} %add.7.refs_0_), channel_id=1, source_target_pairs={{0,2},{1,3},{2,0},{3,1},{4,6},{5,7},{6,4},{7,5},{8,10},{9,11},{10,... | collective-permute-start | bytes 466952 | tf_op jit(solution)/shard_map/ppermute | solution.py:361
  60.6 3.0 %collective-permute-done.20.refs_3_ = f32[304,128]{1,0:T(8,128)S(1)} collective-permute-done((f32[304,128]{1,0:T(8,128)S(1)}, f32[304,128]{1,0:T(8,128)S(1)}, u32[]{:S(2)}, u32[]{:S(2)}) %collective-permute-start.20) | collective-permute-done | bytes 155680 | tf_op jit(solution)/shard_map/ppermute | solution.py:361
  63.6 1.6 %collective-permute-done.19.refs_2_ = f32[304,128]{1,0:T(8,128)S(1)} collective-permute-done((f32[304,128]{1,0:T(8,128)S(1)}, f32[304,128]{1,0:T(8,128)S(1)}, u32[]{:S(2)}, u32[]{:S(2)}) %collective-permute-start.19) | collective-permute-done | bytes 155680 | tf_op jit(solution)/shard_map/ppermute | solution.py:361
  65.7 0.9 %collective-permute-done.23.refs_6_ = f32[304,128]{1,0:T(8,128)S(1)} collective-permute-done((f32[304,128]{1,0:T(8,128)S(1)}, f32[304,128]{1,0:T(8,128)S(1)}, u32[]{:S(2)}, u32[]{:S(2)}) %collective-permute-start.23) | collective-permute-done | bytes 155680 | tf_op jit(solution)/shard_map/ppermute | solution.py:361
  67.1 1.4 %last_relations.1 = (f32[400,768]{1,0:T(8,128)}, f32[768]{0:T(1024)}) custom-call(f32[400,768]{1,0:T(8,128)S(1)} %get-tuple-element.99.rel_ref, f32[1,768]{1,0:T(1,128)S(1)} %get-tuple-element.100.relacc_ref, f32[304,128]{1,0:T(8,128)S(1)} %add.7.refs_0_, f32[304,128]{1,0:T(8,128)S(1)} %collective-permute-done.18.refs_1_, ...), custom_call_target="tpu_custom_call" | custom-call | bytes 3708928 | tf_op jit(solution)/shard_map/last_relations/pallas_call | solution.py:335
  (64 shorter events, 7.4 us)
Async XLA Ops:
  3.8 10.4 %collective-permute-start.2 = (f32[408,128]{1,0:T(8,128)S(1)}, f32[408,128]{1,0:T(8,128)S(1)}, u32[]{:S(2)}, u32[]{:S(2)}) collective-permute-start(f32[408,128]{1,0:T(8,128)S(1)} %get-tuple-element.58), channel_id=1, source_target_pairs={{12,0},{0,4},{4,8},{8,12},{13,1},{1,5},{5,9},{9,13},{14,2},{2,6},{... | collective-permute-start | bytes 626696 | tf_op jit(solution)/shard_map/ppermute | solution.py:395
  6.9 1.5 %collective-permute-start = (f32[4,104,128]{2,1,0:T(8,128)S(1)}, f32[4,104,128]{2,1,0:T(8,128)S(1)}, u32[]{:S(2)}, u32[]{:S(2)}) collective-permute-start(f32[4,104,128]{2,1,0:T(8,128)S(1)} %slice.42), channel_id=1, source_target_pairs={{0,1},{1,0},{2,3},{3,2},{4,5},{5,4},{6,7},{7,6},{8,9},{9,8},{10,11... | collective-permute-start | bytes 638984 | tf_op jit(solution)/shard_map/ppermute | solution.py:361
  8.4 5.8 %collective-permute-start.1 = (f32[208,128]{1,0:T(8,128)S(1)}, f32[208,128]{1,0:T(8,128)S(1)}, u32[]{:S(2)}, u32[]{:S(2)}) collective-permute-start(f32[208,128]{1,0:T(8,128)S(1)} %pad_maximum_fusion), channel_id=1, source_target_pairs={{0,2},{1,3},{2,0},{3,1},{4,6},{5,7},{6,4},{7,5},{8,10},{9,11},{10,... | collective-permute-start | bytes 319496 | tf_op jit(solution)/shard_map/ppermute | solution.py:361
  10.0 11.0 %copy-start = (f32[768,400]{0,1:T(8,128)S(1)}, f32[768,400]{0,1:T(8,128)}, u32[]{:S(2)}) copy-start(f32[768,400]{0,1:T(8,128)} %param.14) | copy-start | bytes 3686404
  10.0 11.0 %copy-start.1 = (f32[128,400]{0,1:T(8,128)S(1)}, f32[128,400]{0,1:T(8,128)}, u32[]{:S(2)}) copy-start(f32[128,400]{0,1:T(8,128)} %param.10) | copy-start | bytes 614404
  10.0 11.0 %copy-start.2 = (s32[2,256]{1,0:T(2,128)S(1)}, s32[2,256]{1,0:T(2,128)}, u32[]{:S(2)}) copy-start(s32[2,256]{1,0:T(2,128)} %hid_ref.3) | copy-start | bytes 6148
  10.0 11.0 %copy-start.3 = (s32[2,256]{1,0:T(2,128)S(1)}, s32[2,256]{1,0:T(2,128)}, u32[]{:S(2)}) copy-start(s32[2,256]{1,0:T(2,128)} %refs_6_.1) | copy-start | bytes 6148
  10.0 11.0 %copy-start.4 = (s32[2,256]{1,0:T(2,128)S(1)}, s32[2,256]{1,0:T(2,128)}, u32[]{:S(2)}) copy-start(s32[2,256]{1,0:T(2,128)} %tid_ref.1) | copy-start | bytes 6148
  10.0 11.0 %copy-start.5 = (s32[2,2,128]{2,1,0:T(2,128)S(1)}, s32[2,2,128]{2,1,0:T(2,128)}, u32[]{:S(2)}) copy-start(s32[2,2,128]{2,1,0:T(2,128)} %nid_ref.1) | copy-start | bytes 6148
  10.0 11.0 %copy-start.6 = (f32[128]{0:T(128)S(1)}, f32[128]{0:T(128)}, u32[]{:S(2)}) copy-start(f32[128]{0:T(128)} %param.11) | copy-start | bytes 1540
  10.0 7.4 %collective-permute-start.3 = (f32[208,128]{1,0:T(8,128)S(1)}, f32[208,128]{1,0:T(8,128)S(1)}, u32[]{:S(2)}, u32[]{:S(2)}) collective-permute-start(f32[208,128]{1,0:T(8,128)S(1)} %pad_maximum_fusion.1), channel_id=1, source_target_pairs={{0,6},{1,7},{2,4},{3,5},{4,2},{5,3},{6,0},{7,1},{8,14},{9,15},{10,... | collective-permute-start | bytes 319496 | tf_op jit(solution)/shard_map/ppermute | solution.py:361
  11.7 7.0 %collective-permute-start.4 = (f32[208,128]{1,0:T(8,128)S(1)}, f32[208,128]{1,0:T(8,128)S(1)}, u32[]{:S(2)}, u32[]{:S(2)}) collective-permute-start(f32[208,128]{1,0:T(8,128)S(1)} %pad_maximum_fusion.2), channel_id=1, source_target_pairs={{0,4},{1,5},{2,6},{3,7},{4,0},{5,1},{6,2},{7,3},{8,12},{9,13},{10,... | collective-permute-start | bytes 319496 | tf_op jit(solution)/shard_map/ppermute | solution.py:361
  19.1 7.9 %collective-permute-start.5 = (f32[304,128]{1,0:T(8,128)S(1)}, f32[304,128]{1,0:T(8,128)S(1)}, u32[]{:S(2)}, u32[]{:S(2)}) collective-permute-start(f32[304,128]{1,0:T(8,128)S(1)} %more_terms.8), channel_id=1, source_target_pairs={{0,12},{1,13},{2,14},{3,15},{4,8},{5,9},{6,10},{7,11},{8,4},{9,5},... | collective-permute-start | bytes 466952 | tf_op jit(solution)/shard_map/ppermute | solution.py:361
  27.0 7.7 %collective-permute-start.8 = (f32[304,128]{1,0:T(8,128)S(1)}, f32[304,128]{1,0:T(8,128)S(1)}, u32[]{:S(2)}, u32[]{:S(2)}) collective-permute-start(f32[304,128]{1,0:T(8,128)S(1)} %add.6.refs_0_), channel_id=1, source_target_pairs={{0,6},{1,7},{2,4},{3,5},{4,2},{5,3},{6,0},{7,1},{8,14},{9,15},{10,... | collective-permute-start | bytes 466952 | tf_op jit(solution)/shard_map/ppermute | solution.py:361
  29.0 6.5 %collective-permute-start.7 = (f32[304,128]{1,0:T(8,128)S(1)}, f32[304,128]{1,0:T(8,128)S(1)}, u32[]{:S(2)}, u32[]{:S(2)}) collective-permute-start(f32[304,128]{1,0:T(8,128)S(1)} %add.6.refs_0_), channel_id=1, source_target_pairs={{0,2},{1,3},{2,0},{3,1},{4,6},{5,7},{6,4},{7,5},{8,10},{9,11},{10,... | collective-permute-start | bytes 466952 | tf_op jit(solution)/shard_map/ppermute | solution.py:361
  29.5 6.9 %collective-permute-start.6 = (f32[304,128]{1,0:T(8,128)S(1)}, f32[304,128]{1,0:T(8,128)S(1)}, u32[]{:S(2)}, u32[]{:S(2)}) collective-permute-start(f32[304,128]{1,0:T(8,128)S(1)} %add.6.refs_0_), channel_id=1, source_target_pairs={{0,4},{1,5},{2,6},{3,7},{4,0},{5,1},{6,2},{7,3},{8,12},{9,13},{10,... | collective-permute-start | bytes 466952 | tf_op jit(solution)/shard_map/ppermute | solution.py:361
  30.6 6.2 %collective-permute-start.9 = (f32[304,128]{1,0:T(8,128)S(1)}, f32[304,128]{1,0:T(8,128)S(1)}, u32[]{:S(2)}, u32[]{:S(2)}) collective-permute-start(f32[304,128]{1,0:T(8,128)S(1)} %add.6.refs_0_), channel_id=1, source_target_pairs={{0,1},{1,0},{2,3},{3,2},{4,5},{5,4},{6,7},{7,6},{8,9},{9,8},{10,11... | collective-permute-start | bytes 466952 | tf_op jit(solution)/shard_map/ppermute | solution.py:361
  34.7 2.0 %collective-permute-start.12 = (f32[304,128]{1,0:T(8,128)S(1)}, f32[304,128]{1,0:T(8,128)S(1)}, u32[]{:S(2)}, u32[]{:S(2)}) collective-permute-start(f32[304,128]{1,0:T(8,128)S(1)} %collective-permute-done.8.refs_3_), channel_id=1, source_target_pairs={{0,1},{1,0},{2,3},{3,2},{4,5},{5,4},{6,7},{7,6},{8,9},{9,8},{10,11... | collective-permute-start | bytes 466952 | tf_op jit(solution)/shard_map/ppermute | solution.py:361
  35.5 1.4 %collective-permute-start.11 = (f32[304,128]{1,0:T(8,128)S(1)}, f32[304,128]{1,0:T(8,128)S(1)}, u32[]{:S(2)}, u32[]{:S(2)}) collective-permute-start(f32[304,128]{1,0:T(8,128)S(1)} %collective-permute-done.7.refs_2_), channel_id=1, source_target_pairs={{0,1},{1,0},{2,3},{3,2},{4,5},{5,4},{6,7},{7,6},{8,9},{9,8},{10,11... | collective-permute-start | bytes 466952 | tf_op jit(solution)/shard_map/ppermute | solution.py:361
  36.4 1.4 %collective-permute-start.10 = (f32[304,128]{1,0:T(8,128)S(1)}, f32[304,128]{1,0:T(8,128)S(1)}, u32[]{:S(2)}, u32[]{:S(2)}) collective-permute-start(f32[304,128]{1,0:T(8,128)S(1)} %collective-permute-done.6.refs_1_), channel_id=1, source_target_pairs={{0,1},{1,0},{2,3},{3,2},{4,5},{5,4},{6,7},{7,6},{8,9},{9,8},{10,11... | collective-permute-start | bytes 466952 | tf_op jit(solution)/shard_map/ppermute | solution.py:361
  39.2 1.5 %collective-permute-start.13 = (f32[4,104,128]{2,1,0:T(8,128)S(1)}, f32[4,104,128]{2,1,0:T(8,128)S(1)}, u32[]{:S(2)}, u32[]{:S(2)}) collective-permute-start(f32[4,104,128]{2,1,0:T(8,128)S(1)} %slice.49), channel_id=1, source_target_pairs={{0,1},{1,0},{2,3},{3,2},{4,5},{5,4},{6,7},{7,6},{8,9},{9,8},{10,11... | collective-permute-start | bytes 638984 | tf_op jit(solution)/shard_map/ppermute | solution.py:361
  40.8 7.0 %collective-permute-start.14 = (f32[208,128]{1,0:T(8,128)S(1)}, f32[208,128]{1,0:T(8,128)S(1)}, u32[]{:S(2)}, u32[]{:S(2)}) collective-permute-start(f32[208,128]{1,0:T(8,128)S(1)} %pad_maximum_fusion.3), channel_id=1, source_target_pairs={{0,2},{1,3},{2,0},{3,1},{4,6},{5,7},{6,4},{7,5},{8,10},{9,11},{10,... | collective-permute-start | bytes 319496 | tf_op jit(solution)/shard_map/ppermute | solution.py:361
  41.7 6.8 %collective-permute-start.15 = (f32[208,128]{1,0:T(8,128)S(1)}, f32[208,128]{1,0:T(8,128)S(1)}, u32[]{:S(2)}, u32[]{:S(2)}) collective-permute-start(f32[208,128]{1,0:T(8,128)S(1)} %pad_maximum_fusion.4), channel_id=1, source_target_pairs={{0,6},{1,7},{2,4},{3,5},{4,2},{5,3},{6,0},{7,1},{8,14},{9,15},{10,... | collective-permute-start | bytes 319496 | tf_op jit(solution)/shard_map/ppermute | solution.py:361
  42.8 6.6 %collective-permute-start.16 = (f32[208,128]{1,0:T(8,128)S(1)}, f32[208,128]{1,0:T(8,128)S(1)}, u32[]{:S(2)}, u32[]{:S(2)}) collective-permute-start(f32[208,128]{1,0:T(8,128)S(1)} %pad_maximum_fusion.5), channel_id=1, source_target_pairs={{0,4},{1,5},{2,6},{3,7},{4,0},{5,1},{6,2},{7,3},{8,12},{9,13},{10,... | collective-permute-start | bytes 319496 | tf_op jit(solution)/shard_map/ppermute | solution.py:361
  49.8 7.1 %collective-permute-start.17 = (f32[304,128]{1,0:T(8,128)S(1)}, f32[304,128]{1,0:T(8,128)S(1)}, u32[]{:S(2)}, u32[]{:S(2)}) collective-permute-start(f32[304,128]{1,0:T(8,128)S(1)} %more_terms.11), channel_id=1, source_target_pairs={{0,12},{1,13},{2,14},{3,15},{4,8},{5,9},{6,10},{7,11},{8,4},{9,5},... | collective-permute-start | bytes 466952 | tf_op jit(solution)/shard_map/ppermute | solution.py:361
  57.0 6.6 %collective-permute-start.20 = (f32[304,128]{1,0:T(8,128)S(1)}, f32[304,128]{1,0:T(8,128)S(1)}, u32[]{:S(2)}, u32[]{:S(2)}) collective-permute-start(f32[304,128]{1,0:T(8,128)S(1)} %add.7.refs_0_), channel_id=1, source_target_pairs={{0,6},{1,7},{2,4},{3,5},{4,2},{5,3},{6,0},{7,1},{8,14},{9,15},{10,... | collective-permute-start | bytes 466952 | tf_op jit(solution)/shard_map/ppermute | solution.py:361
  59.5 5.7 %collective-permute-start.19 = (f32[304,128]{1,0:T(8,128)S(1)}, f32[304,128]{1,0:T(8,128)S(1)}, u32[]{:S(2)}, u32[]{:S(2)}) collective-permute-start(f32[304,128]{1,0:T(8,128)S(1)} %add.7.refs_0_), channel_id=1, source_target_pairs={{0,2},{1,3},{2,0},{3,1},{4,6},{5,7},{6,4},{7,5},{8,10},{9,11},{10,... | collective-permute-start | bytes 466952 | tf_op jit(solution)/shard_map/ppermute | solution.py:361
  60.5 5.2 %collective-permute-start.18 = (f32[304,128]{1,0:T(8,128)S(1)}, f32[304,128]{1,0:T(8,128)S(1)}, u32[]{:S(2)}, u32[]{:S(2)}) collective-permute-start(f32[304,128]{1,0:T(8,128)S(1)} %add.7.refs_0_), channel_id=1, source_target_pairs={{0,4},{1,5},{2,6},{3,7},{4,0},{5,1},{6,2},{7,3},{8,12},{9,13},{10,... | collective-permute-start | bytes 466952 | tf_op jit(solution)/shard_map/ppermute | solution.py:361
  60.6 5.2 %collective-permute-start.21 = (f32[304,128]{1,0:T(8,128)S(1)}, f32[304,128]{1,0:T(8,128)S(1)}, u32[]{:S(2)}, u32[]{:S(2)}) collective-permute-start(f32[304,128]{1,0:T(8,128)S(1)} %add.7.refs_0_), channel_id=1, source_target_pairs={{0,1},{1,0},{2,3},{3,2},{4,5},{5,4},{6,7},{7,6},{8,9},{9,8},{10,11... | collective-permute-start | bytes 466952 | tf_op jit(solution)/shard_map/ppermute | solution.py:361
  63.6 2.1 %collective-permute-start.24 = (f32[304,128]{1,0:T(8,128)S(1)}, f32[304,128]{1,0:T(8,128)S(1)}, u32[]{:S(2)}, u32[]{:S(2)}) collective-permute-start(f32[304,128]{1,0:T(8,128)S(1)} %collective-permute-done.20.refs_3_), channel_id=1, source_target_pairs={{0,1},{1,0},{2,3},{3,2},{4,5},{5,4},{6,7},{7,6},{8,9},{9,8},{10,11... | collective-permute-start | bytes 466952 | tf_op jit(solution)/shard_map/ppermute | solution.py:361
  65.2 1.4 %collective-permute-start.23 = (f32[304,128]{1,0:T(8,128)S(1)}, f32[304,128]{1,0:T(8,128)S(1)}, u32[]{:S(2)}, u32[]{:S(2)}) collective-permute-start(f32[304,128]{1,0:T(8,128)S(1)} %collective-permute-done.19.refs_2_), channel_id=1, source_target_pairs={{0,1},{1,0},{2,3},{3,2},{4,5},{5,4},{6,7},{7,6},{8,9},{9,8},{10,11... | collective-permute-start | bytes 466952 | tf_op jit(solution)/shard_map/ppermute | solution.py:361
  65.7 1.4 %collective-permute-start.22 = (f32[304,128]{1,0:T(8,128)S(1)}, f32[304,128]{1,0:T(8,128)S(1)}, u32[]{:S(2)}, u32[]{:S(2)}) collective-permute-start(f32[304,128]{1,0:T(8,128)S(1)} %collective-permute-done.18.refs_1_), channel_id=1, source_target_pairs={{0,1},{1,0},{2,3},{3,2},{4,5},{5,4},{6,7},{7,6},{8,9},{9,8},{10,11... | collective-permute-start | bytes 466952 | tf_op jit(solution)/shard_map/ppermute | solution.py:361
  (1 other events, 11.0 us)

commit v8 on v7

--- a/solution.py
+++ b/solution.py
@@ -189,12 +189,21 @@
     )
 
 
-def next_accum(relacc_ref, all_ref, width):
+def next_accum(relacc_ref, piece_refs, width):
     squares = []
+    main, rest = cut(width)
     blocks = relacc_ref.shape[1] // LANES
     for j in range(blocks):
-        grad = take_rel_grad(all_ref, j, width, blocks)
-        squares.append(jnp.sum(grad * grad, axis=0, keepdims=True))
+        tiles, rests = None, None
+        for ref in piece_refs:
+            whole = ref[main * j : main * (j + 1)].reshape(-1, 8, LANES)
+            whole = jnp.sum(whole * whole, axis=0)
+            first = main * blocks + rest * j
+            below = ref[first : first + rest]
+            below = below * below
+            tiles = whole if tiles is None else tiles + whole
+            rests = below if rests is None else rests + below
+        squares.append(jnp.sum(tiles, axis=0, keepdims=True) + jnp.sum(rests, axis=0, keepdims=True))
     accum = relacc_ref[...] + jnp.concatenate(squares, axis=1) * (1.0 / width)
     return accum, RATE / jnp.sqrt(accum)
 
@@ -296,7 +305,7 @@
     piece_refs, (rel_out, relacc_out, all_ref) = refs[:PIECES], refs[PIECES:]
     width = rel_ref.shape[0]
     order_pieces(piece_refs, all_ref)
-    accum, rate = next_accum(relacc_ref, all_ref, width)
+    accum, rate = next_accum(relacc_ref, piece_refs, width)
     relacc_out[...] = accum[0] if len(relacc_out.shape) == 1 else accum
     blocks = rel_ref.shape[1] // LANES
     for j in range(blocks):

time: 68.7 us -> 68.7 us (level)
  no operation moved by 1% of the time
where the time goes in v8:
time: 68.7 us; the launch traced here: 68.5 us
  waiting for transfers between devices  35.1 us (51%)
  starting transfers between devices  20.2 us (29%)
  Pallas kernels  12.1 us (18%)
  between operations  0.93 us (1%)
    ppermute x24, waiting for transfers between devices, swap(): return lax.ppermute(x, AXES, route)  33.4 us
    ppermute x24, starting transfers between devices, swap(): return lax.ppermute(x, AXES, route)  17.1 us
    pallas_call x14, Pallas kernels, run(): pl.pallas_call(kernel, out_shape=[jax.ShapeDtypeStruct(shape, F32) if isi...  8.99 us
    pallas_call x1, Pallas kernels, shards(): pl.pallas_call(first_kernel, out_shape=[jax.ShapeDtypeStruct(shape, F32)...  3.16 us
    ppermute x1, starting transfers between devices, from_behind(): return lax.ppermute(block, axis, [((i - 1) % n, i) for i in range(n)])  3.08 us
    ppermute x1, waiting for transfers between devices, from_behind(): return lax.ppermute(block, axis, [((i - 1) % n, i) for i in range(n)])  1.62 us
  transfers between devices with their start and end apart: 25, of which 20 were waited for; matrix products, arithmetic and copies ran while one was open for 0% of the time, Pallas kernels for 8%

profile of v8, /device:TPU:0, one launch (start us, length us, event | category | flops | bytes accessed | tf_op | source)
XLA Modules:
  0.0 68.5 jit_solution(6123948215233750849)
XLA Ops:
  0.6 3.2 %first_step.1 = (f32[408,128]{1,0:T(8,128)S(1)}, f32[8,104,128]{2,1,0:T(8,128)S(1)}, f32[400,256]{1,0:T(8,128)S(1)}) custom-call(s32[2,256]{1,0:T(2,128)} %hid_ref.3, s32[2,256]{1,0:T(2,128)} %tid_ref.1, s32[2,256]{1,0:T(2,128)} %refs_6_.1, s32[2,2,128]{2,1,0:T(2,128)} %nid_ref.1, f32[400,128]{1,0:T(8,128)} %bitcast.35, f32[400,128]{1,0:T(8,128)} %bitcast.38, ...), custom_call_target="tpu_custom_call" | custom-call | tf_op jit(solution)/shard_map/first_step/pallas_call | solution.py:421
  3.8 3.1 %collective-permute-start.2 = (f32[408,128]{1,0:T(8,128)S(1)}, f32[408,128]{1,0:T(8,128)S(1)}, u32[]{:S(2)}, u32[]{:S(2)}) collective-permute-start(f32[408,128]{1,0:T(8,128)S(1)} %get-tuple-element.58), channel_id=1, source_target_pairs={{12,0},{0,4},{4,8},{8,12},{13,1},{1,5},{5,9},{9,13},{14,2},{2,6},{... | collective-permute-start | bytes 626696 | tf_op jit(solution)/shard_map/ppermute | solution.py:404
  6.9 1.4 %collective-permute-done.other_ref = f32[4,104,128]{2,1,0:T(8,128)S(1)} collective-permute-done((f32[4,104,128]{2,1,0:T(8,128)S(1)}, f32[4,104,128]{2,1,0:T(8,128)S(1)}, u32[]{:S(2)}, u32[]{:S(2)}) %collective-permute-start) | collective-permute-done | bytes 213024 | tf_op jit(solution)/shard_map/ppermute | solution.py:370
  8.4 1.6 %collective-permute-start.1 = (f32[208,128]{1,0:T(8,128)S(1)}, f32[208,128]{1,0:T(8,128)S(1)}, u32[]{:S(2)}, u32[]{:S(2)}) collective-permute-start(f32[208,128]{1,0:T(8,128)S(1)} %pad_maximum_fusion), channel_id=1, source_target_pairs={{0,2},{1,3},{2,0},{3,1},{4,6},{5,7},{6,4},{7,5},{8,10},{9,11},{10,... | collective-permute-start | bytes 319496 | tf_op jit(solution)/shard_map/ppermute | solution.py:370
  10.0 1.6 %collective-permute-start.3 = (f32[208,128]{1,0:T(8,128)S(1)}, f32[208,128]{1,0:T(8,128)S(1)}, u32[]{:S(2)}, u32[]{:S(2)}) collective-permute-start(f32[208,128]{1,0:T(8,128)S(1)} %pad_maximum_fusion.1), channel_id=1, source_target_pairs={{0,6},{1,7},{2,4},{3,5},{4,2},{5,3},{6,0},{7,1},{8,14},{9,15},{10,... | collective-permute-start | bytes 319496 | tf_op jit(solution)/shard_map/ppermute | solution.py:370
  12.6 1.6 %collective-permute-done.2.right_ref = f32[408,128]{1,0:T(8,128)S(1)} collective-permute-done((f32[408,128]{1,0:T(8,128)S(1)}, f32[408,128]{1,0:T(8,128)S(1)}, u32[]{:S(2)}, u32[]{:S(2)}) %collective-permute-start.2) | collective-permute-done | bytes 208928 | tf_op jit(solution)/shard_map/ppermute | solution.py:404
  14.6 2.8 %collective-permute-done.3.terms_ref = f32[208,128]{1,0:T(8,128)S(1)} collective-permute-done((f32[208,128]{1,0:T(8,128)S(1)}, f32[208,128]{1,0:T(8,128)S(1)}, u32[]{:S(2)}, u32[]{:S(2)}) %collective-permute-start.3) | collective-permute-done | bytes 106528 | tf_op jit(solution)/shard_map/ppermute | solution.py:370
  17.8 0.9 %collective-permute-done.4.terms_ref = f32[208,128]{1,0:T(8,128)S(1)} collective-permute-done((f32[208,128]{1,0:T(8,128)S(1)}, f32[208,128]{1,0:T(8,128)S(1)}, u32[]{:S(2)}, u32[]{:S(2)}) %collective-permute-start.4) | collective-permute-done | bytes 106528 | tf_op jit(solution)/shard_map/ppermute | solution.py:370
  19.1 1.9 %collective-permute-start.5 = (f32[304,128]{1,0:T(8,128)S(1)}, f32[304,128]{1,0:T(8,128)S(1)}, u32[]{:S(2)}, u32[]{:S(2)}) collective-permute-start(f32[304,128]{1,0:T(8,128)S(1)} %more_terms.8), channel_id=1, source_target_pairs={{0,12},{1,13},{2,14},{3,15},{4,8},{5,9},{6,10},{7,11},{8,4},{9,5},... | collective-permute-start | bytes 466952 | tf_op jit(solution)/shard_map/ppermute | solution.py:370
  21.0 1.1 %ready.1 = (f32[400,128]{1,0:T(8,128)S(1)}, f32[1,128]{1,0:T(1,128)S(1)}, f32[400,256]{1,0:T(8,128)S(1)}, bf16[256,400]{1,0:T(8,128)(2,1)S(1)}, bf16[800,128]{1,...) custom-call(f32[400,128]{1,0:T(8,128)S(1)} %bitcast.36, ...), custom_call_target="tpu_custom_call" | custom-call | bytes 4957184 | tf_op jit(solution)/shard_map/ready/pallas_call | solution.py:344
  22.1 4.8 %collective-permute-done.5 = f32[304,128]{1,0:T(8,128)S(1)} collective-permute-done((f32[304,128]{1,0:T(8,128)S(1)}, f32[304,128]{1,0:T(8,128)S(1)}, u32[]{:S(2)}, u32[]{:S(2)}) %collective-permute-start.5) | collective-permute-done | bytes 155680 | tf_op jit(solution)/shard_map/ppermute | solution.py:370
  27.0 2.0 %collective-permute-start.8 = (f32[304,128]{1,0:T(8,128)S(1)}, f32[304,128]{1,0:T(8,128)S(1)}, u32[]{:S(2)}, u32[]{:S(2)}) collective-permute-start(f32[304,128]{1,0:T(8,128)S(1)} %add.6.refs_0_), channel_id=1, source_target_pairs={{0,6},{1,7},{2,4},{3,5},{4,2},{5,3},{6,0},{7,1},{8,14},{9,15},{10,... | collective-permute-start | bytes 466952 | tf_op jit(solution)/shard_map/ppermute | solution.py:370
  29.0 0.5 collective-permute-start.7
  29.5 1.1 %collective-permute-start.6 = (f32[304,128]{1,0:T(8,128)S(1)}, f32[304,128]{1,0:T(8,128)S(1)}, u32[]{:S(2)}, u32[]{:S(2)}) collective-permute-start(f32[304,128]{1,0:T(8,128)S(1)} %add.6.refs_0_), channel_id=1, source_target_pairs={{0,4},{1,5},{2,6},{3,7},{4,0},{5,1},{6,2},{7,3},{8,12},{9,13},{10,... | collective-permute-start | bytes 466952 | tf_op jit(solution)/shard_map/ppermute | solution.py:370
  30.6 4.2 %collective-permute-done.8.refs_3_ = f32[304,128]{1,0:T(8,128)S(1)} collective-permute-done((f32[304,128]{1,0:T(8,128)S(1)}, f32[304,128]{1,0:T(8,128)S(1)}, u32[]{:S(2)}, u32[]{:S(2)}) %collective-permute-start.8) | collective-permute-done | bytes 155680 | tf_op jit(solution)/shard_map/ppermute | solution.py:370
  34.7 0.8 %collective-permute-done.7.refs_2_ = f32[304,128]{1,0:T(8,128)S(1)} collective-permute-done((f32[304,128]{1,0:T(8,128)S(1)}, f32[304,128]{1,0:T(8,128)S(1)}, u32[]{:S(2)}, u32[]{:S(2)}) %collective-permute-start.7) | collective-permute-done | bytes 155680 | tf_op jit(solution)/shard_map/ppermute | solution.py:370
  35.5 0.9 %collective-permute-done.6.refs_1_ = f32[304,128]{1,0:T(8,128)S(1)} collective-permute-done((f32[304,128]{1,0:T(8,128)S(1)}, f32[304,128]{1,0:T(8,128)S(1)}, u32[]{:S(2)}, u32[]{:S(2)}) %collective-permute-start.6) | collective-permute-done | bytes 155680 | tf_op jit(solution)/shard_map/ppermute | solution.py:370
  36.9 0.9 %collective-permute-done.10.refs_3_.refs_5_ = f32[304,128]{1,0:T(8,128)S(1)} collective-permute-done((f32[304,128]{1,0:T(8,128)S(1)}, f32[304,128]{1,0:T(8,128)S(1)}, u32[]{:S(2)}, u32[]{:S(2)}) %collective-permute-start.10) | collective-permute-done | bytes 155680 | tf_op jit(solution)/shard_map/ppermute | solution.py:370
  37.8 1.4 %next_step.1 = (f32[8,104,128]{2,1,0:T(8,128)S(1)}, f32[400,256]{1,0:T(8,128)S(1)}, f32[400,256]{1,0:T(8,128)S(1)}, f32[128,256]{1,0:T(8,128)S(1)}) custom-call(f32[400,256]{1,0:T(8,128)S(1)} %get-tuple-element.72.heads_ref, bf16[256,400]{1,0:T(8,128)(2,1)S(1)} %get-tuple-element.73.turned_ref, bf16[800,128]{1,0:T(8,128)(2,1)S(1)} %get-tuple-element.74.right_ref, ...), custom_call_target="tpu_custom_call" | custom-call | bytes 4893696 | tf_op jit(solution)/shard_map/next_step/pallas_call | solution.py:344
  39.4 1.3 %collective-permute-done.13.other_ref = f32[4,104,128]{2,1,0:T(8,128)S(1)} collective-permute-done((f32[4,104,128]{2,1,0:T(8,128)S(1)}, f32[4,104,128]{2,1,0:T(8,128)S(1)}, u32[]{:S(2)}, u32[]{:S(2)}) %collective-permute-start.13) | collective-permute-done | bytes 213024 | tf_op jit(solution)/shard_map/ppermute | solution.py:370
  40.8 0.9 %collective-permute-start.14 = (f32[208,128]{1,0:T(8,128)S(1)}, f32[208,128]{1,0:T(8,128)S(1)}, u32[]{:S(2)}, u32[]{:S(2)}) collective-permute-start(f32[208,128]{1,0:T(8,128)S(1)} %pad_maximum_fusion.3), channel_id=1, source_target_pairs={{0,2},{1,3},{2,0},{3,1},{4,6},{5,7},{6,4},{7,5},{8,10},{9,11},{10,... | collective-permute-start | bytes 319496 | tf_op jit(solution)/shard_map/ppermute | solution.py:370
  41.7 1.2 %collective-permute-start.15 = (f32[208,128]{1,0:T(8,128)S(1)}, f32[208,128]{1,0:T(8,128)S(1)}, u32[]{:S(2)}, u32[]{:S(2)}) collective-permute-start(f32[208,128]{1,0:T(8,128)S(1)} %pad_maximum_fusion.4), channel_id=1, source_target_pairs={{0,6},{1,7},{2,4},{3,5},{4,2},{5,3},{6,0},{7,1},{8,14},{9,15},{10,... | collective-permute-start | bytes 319496 | tf_op jit(solution)/shard_map/ppermute | solution.py:370
  42.8 1.6 %collective-permute-start.16 = (f32[208,128]{1,0:T(8,128)S(1)}, f32[208,128]{1,0:T(8,128)S(1)}, u32[]{:S(2)}, u32[]{:S(2)}) collective-permute-start(f32[208,128]{1,0:T(8,128)S(1)} %pad_maximum_fusion.5), channel_id=1, source_target_pairs={{0,4},{1,5},{2,6},{3,7},{4,0},{5,1},{6,2},{7,3},{8,12},{9,13},{10,... | collective-permute-start | bytes 319496 | tf_op jit(solution)/shard_map/ppermute | solution.py:370
  44.9 2.9 %collective-permute-done.14.terms_ref = f32[208,128]{1,0:T(8,128)S(1)} collective-permute-done((f32[208,128]{1,0:T(8,128)S(1)}, f32[208,128]{1,0:T(8,128)S(1)}, u32[]{:S(2)}, u32[]{:S(2)}) %collective-permute-start.14) | collective-permute-done | bytes 106528 | tf_op jit(solution)/shard_map/ppermute | solution.py:370
  50.3 1.2 %last_update.1 = (f32[400,128]{1,0:T(8,128)}, f32[128]{0:T(128)}, f32[400,128]{1,0:T(8,128)}, f32[128]{0:T(128)}) custom-call(f32[400,128]{1,0:T(8,128)S(1)} %get-tuple-element.86.left_ref, f32[1,128]{1,0:T(1,128)S(1)} %get-tuple-element.87.lacc_ref, f32[400,256]{1,0:T(8,128)S(1)} %get-tuple-element.88.carry_ref, s32[2,256]{1,0:T(2,128)S(1)} %copy-done.2, ...), custom_call_target="tpu_custom_call" | custom-call | bytes 1777152 | tf_op jit(solution)/shard_map/last_update/pallas_call | solution.py:344
  51.9 5.0 %collective-permute-done.17 = f32[304,128]{1,0:T(8,128)S(1)} collective-permute-done((f32[304,128]{1,0:T(8,128)S(1)}, f32[304,128]{1,0:T(8,128)S(1)}, u32[]{:S(2)}, u32[]{:S(2)}) %collective-permute-start.17) | collective-permute-done | bytes 155680 | tf_op jit(solution)/shard_map/ppermute | solution.py:370
  57.0 2.5 %collective-permute-start.20 = (f32[304,128]{1,0:T(8,128)S(1)}, f32[304,128]{1,0:T(8,128)S(1)}, u32[]{:S(2)}, u32[]{:S(2)}) collective-permute-start(f32[304,128]{1,0:T(8,128)S(1)} %add.7.refs_0_), channel_id=1, source_target_pairs={{0,6},{1,7},{2,4},{3,5},{4,2},{5,3},{6,0},{7,1},{8,14},{9,15},{10,... | collective-permute-start | bytes 466952 | tf_op jit(solution)/shard_map/ppermute | solution.py:370
  59.5 1.0 %collective-permute-start.19 = (f32[304,128]{1,0:T(8,128)S(1)}, f32[304,128]{1,0:T(8,128)S(1)}, u32[]{:S(2)}, u32[]{:S(2)}) collective-permute-start(f32[304,128]{1,0:T(8,128)S(1)} %add.7.refs_0_), channel_id=1, source_target_pairs={{0,2},{1,3},{2,0},{3,1},{4,6},{5,7},{6,4},{7,5},{8,10},{9,11},{10,... | collective-permute-start | bytes 466952 | tf_op jit(solution)/shard_map/ppermute | solution.py:370
  60.6 3.0 %collective-permute-done.20.refs_3_ = f32[304,128]{1,0:T(8,128)S(1)} collective-permute-done((f32[304,128]{1,0:T(8,128)S(1)}, f32[304,128]{1,0:T(8,128)S(1)}, u32[]{:S(2)}, u32[]{:S(2)}) %collective-permute-start.20) | collective-permute-done | bytes 155680 | tf_op jit(solution)/shard_map/ppermute | solution.py:370
  63.6 1.6 %collective-permute-done.19.refs_2_ = f32[304,128]{1,0:T(8,128)S(1)} collective-permute-done((f32[304,128]{1,0:T(8,128)S(1)}, f32[304,128]{1,0:T(8,128)S(1)}, u32[]{:S(2)}, u32[]{:S(2)}) %collective-permute-start.19) | collective-permute-done | bytes 155680 | tf_op jit(solution)/shard_map/ppermute | solution.py:370
  65.7 0.9 %collective-permute-done.23.refs_6_ = f32[304,128]{1,0:T(8,128)S(1)} collective-permute-done((f32[304,128]{1,0:T(8,128)S(1)}, f32[304,128]{1,0:T(8,128)S(1)}, u32[]{:S(2)}, u32[]{:S(2)}) %collective-permute-start.23) | collective-permute-done | bytes 155680 | tf_op jit(solution)/shard_map/ppermute | solution.py:370
  67.1 1.4 %last_relations.1 = (f32[400,768]{1,0:T(8,128)}, f32[768]{0:T(1024)}) custom-call(f32[400,768]{1,0:T(8,128)S(1)} %get-tuple-element.99.rel_ref, f32[1,768]{1,0:T(1,128)S(1)} %get-tuple-element.100.relacc_ref, f32[304,128]{1,0:T(8,128)S(1)} %add.7.refs_0_, f32[304,128]{1,0:T(8,128)S(1)} %collective-permute-done.18.refs_1_, ...), custom_call_target="tpu_custom_call" | custom-call | bytes 3708928 | tf_op jit(solution)/shard_map/last_relations/pallas_call | solution.py:344
  (64 shorter events, 7.4 us)
Async XLA Ops:
  3.8 10.4 %collective-permute-start.2 = (f32[408,128]{1,0:T(8,128)S(1)}, f32[408,128]{1,0:T(8,128)S(1)}, u32[]{:S(2)}, u32[]{:S(2)}) collective-permute-start(f32[408,128]{1,0:T(8,128)S(1)} %get-tuple-element.58), channel_id=1, source_target_pairs={{12,0},{0,4},{4,8},{8,12},{13,1},{1,5},{5,9},{9,13},{14,2},{2,6},{... | collective-permute-start | bytes 626696 | tf_op jit(solution)/shard_map/ppermute | solution.py:404
  6.9 1.5 %collective-permute-start = (f32[4,104,128]{2,1,0:T(8,128)S(1)}, f32[4,104,128]{2,1,0:T(8,128)S(1)}, u32[]{:S(2)}, u32[]{:S(2)}) collective-permute-start(f32[4,104,128]{2,1,0:T(8,128)S(1)} %slice.42), channel_id=1, source_target_pairs={{0,1},{1,0},{2,3},{3,2},{4,5},{5,4},{6,7},{7,6},{8,9},{9,8},{10,11... | collective-permute-start | bytes 638984 | tf_op jit(solution)/shard_map/ppermute | solution.py:370
  8.4 5.8 %collective-permute-start.1 = (f32[208,128]{1,0:T(8,128)S(1)}, f32[208,128]{1,0:T(8,128)S(1)}, u32[]{:S(2)}, u32[]{:S(2)}) collective-permute-start(f32[208,128]{1,0:T(8,128)S(1)} %pad_maximum_fusion), channel_id=1, source_target_pairs={{0,2},{1,3},{2,0},{3,1},{4,6},{5,7},{6,4},{7,5},{8,10},{9,11},{10,... | collective-permute-start | bytes 319496 | tf_op jit(solution)/shard_map/ppermute | solution.py:370
  10.0 11.0 %copy-start = (f32[768,400]{0,1:T(8,128)S(1)}, f32[768,400]{0,1:T(8,128)}, u32[]{:S(2)}) copy-start(f32[768,400]{0,1:T(8,128)} %param.14) | copy-start | bytes 3686404
  10.0 11.0 %copy-start.1 = (f32[128,400]{0,1:T(8,128)S(1)}, f32[128,400]{0,1:T(8,128)}, u32[]{:S(2)}) copy-start(f32[128,400]{0,1:T(8,128)} %param.10) | copy-start | bytes 614404
  10.0 11.0 %copy-start.2 = (s32[2,256]{1,0:T(2,128)S(1)}, s32[2,256]{1,0:T(2,128)}, u32[]{:S(2)}) copy-start(s32[2,256]{1,0:T(2,128)} %hid_ref.3) | copy-start | bytes 6148
  10.0 11.0 %copy-start.3 = (s32[2,256]{1,0:T(2,128)S(1)}, s32[2,256]{1,0:T(2,128)}, u32[]{:S(2)}) copy-start(s32[2,256]{1,0:T(2,128)} %refs_6_.1) | copy-start | bytes 6148
  10.0 11.0 %copy-start.4 = (s32[2,256]{1,0:T(2,128)S(1)}, s32[2,256]{1,0:T(2,128)}, u32[]{:S(2)}) copy-start(s32[2,256]{1,0:T(2,128)} %tid_ref.1) | copy-start | bytes 6148
  10.0 11.0 %copy-start.5 = (s32[2,2,128]{2,1,0:T(2,128)S(1)}, s32[2,2,128]{2,1,0:T(2,128)}, u32[]{:S(2)}) copy-start(s32[2,2,128]{2,1,0:T(2,128)} %nid_ref.1) | copy-start | bytes 6148
  10.0 11.0 %copy-start.6 = (f32[128]{0:T(128)S(1)}, f32[128]{0:T(128)}, u32[]{:S(2)}) copy-start(f32[128]{0:T(128)} %param.11) | copy-start | bytes 1540
  10.0 7.4 %collective-permute-start.3 = (f32[208,128]{1,0:T(8,128)S(1)}, f32[208,128]{1,0:T(8,128)S(1)}, u32[]{:S(2)}, u32[]{:S(2)}) collective-permute-start(f32[208,128]{1,0:T(8,128)S(1)} %pad_maximum_fusion.1), channel_id=1, source_target_pairs={{0,6},{1,7},{2,4},{3,5},{4,2},{5,3},{6,0},{7,1},{8,14},{9,15},{10,... | collective-permute-start | bytes 319496 | tf_op jit(solution)/shard_map/ppermute | solution.py:370
  11.7 7.0 %collective-permute-start.4 = (f32[208,128]{1,0:T(8,128)S(1)}, f32[208,128]{1,0:T(8,128)S(1)}, u32[]{:S(2)}, u32[]{:S(2)}) collective-permute-start(f32[208,128]{1,0:T(8,128)S(1)} %pad_maximum_fusion.2), channel_id=1, source_target_pairs={{0,4},{1,5},{2,6},{3,7},{4,0},{5,1},{6,2},{7,3},{8,12},{9,13},{10,... | collective-permute-start | bytes 319496 | tf_op jit(solution)/shard_map/ppermute | solution.py:370
  19.1 7.9 %collective-permute-start.5 = (f32[304,128]{1,0:T(8,128)S(1)}, f32[304,128]{1,0:T(8,128)S(1)}, u32[]{:S(2)}, u32[]{:S(2)}) collective-permute-start(f32[304,128]{1,0:T(8,128)S(1)} %more_terms.8), channel_id=1, source_target_pairs={{0,12},{1,13},{2,14},{3,15},{4,8},{5,9},{6,10},{7,11},{8,4},{9,5},... | collective-permute-start | bytes 466952 | tf_op jit(solution)/shard_map/ppermute | solution.py:370
  27.0 7.7 %collective-permute-start.8 = (f32[304,128]{1,0:T(8,128)S(1)}, f32[304,128]{1,0:T(8,128)S(1)}, u32[]{:S(2)}, u32[]{:S(2)}) collective-permute-start(f32[304,128]{1,0:T(8,128)S(1)} %add.6.refs_0_), channel_id=1, source_target_pairs={{0,6},{1,7},{2,4},{3,5},{4,2},{5,3},{6,0},{7,1},{8,14},{9,15},{10,... | collective-permute-start | bytes 466952 | tf_op jit(solution)/shard_map/ppermute | solution.py:370
  29.0 6.5 %collective-permute-start.7 = (f32[304,128]{1,0:T(8,128)S(1)}, f32[304,128]{1,0:T(8,128)S(1)}, u32[]{:S(2)}, u32[]{:S(2)}) collective-permute-start(f32[304,128]{1,0:T(8,128)S(1)} %add.6.refs_0_), channel_id=1, source_target_pairs={{0,2},{1,3},{2,0},{3,1},{4,6},{5,7},{6,4},{7,5},{8,10},{9,11},{10,... | collective-permute-start | bytes 466952 | tf_op jit(solution)/shard_map/ppermute | solution.py:370
  29.5 6.9 %collective-permute-start.6 = (f32[304,128]{1,0:T(8,128)S(1)}, f32[304,128]{1,0:T(8,128)S(1)}, u32[]{:S(2)}, u32[]{:S(2)}) collective-permute-start(f32[304,128]{1,0:T(8,128)S(1)} %add.6.refs_0_), channel_id=1, source_target_pairs={{0,4},{1,5},{2,6},{3,7},{4,0},{5,1},{6,2},{7,3},{8,12},{9,13},{10,... | collective-permute-start | bytes 466952 | tf_op jit(solution)/shard_map/ppermute | solution.py:370
  30.6 6.2 %collective-permute-start.9 = (f32[304,128]{1,0:T(8,128)S(1)}, f32[304,128]{1,0:T(8,128)S(1)}, u32[]{:S(2)}, u32[]{:S(2)}) collective-permute-start(f32[304,128]{1,0:T(8,128)S(1)} %add.6.refs_0_), channel_id=1, source_target_pairs={{0,1},{1,0},{2,3},{3,2},{4,5},{5,4},{6,7},{7,6},{8,9},{9,8},{10,11... | collective-permute-start | bytes 466952 | tf_op jit(solution)/shard_map/ppermute | solution.py:370
  34.7 2.0 %collective-permute-start.12 = (f32[304,128]{1,0:T(8,128)S(1)}, f32[304,128]{1,0:T(8,128)S(1)}, u32[]{:S(2)}, u32[]{:S(2)}) collective-permute-start(f32[304,128]{1,0:T(8,128)S(1)} %collective-permute-done.8.refs_3_), channel_id=1, source_target_pairs={{0,1},{1,0},{2,3},{3,2},{4,5},{5,4},{6,7},{7,6},{8,9},{9,8},{10,11... | collective-permute-start | bytes 466952 | tf_op jit(solution)/shard_map/ppermute | solution.py:370
  35.5 1.4 %collective-permute-start.11 = (f32[304,128]{1,0:T(8,128)S(1)}, f32[304,128]{1,0:T(8,128)S(1)}, u32[]{:S(2)}, u32[]{:S(2)}) collective-permute-start(f32[304,128]{1,0:T(8,128)S(1)} %collective-permute-done.7.refs_2_), channel_id=1, source_target_pairs={{0,1},{1,0},{2,3},{3,2},{4,5},{5,4},{6,7},{7,6},{8,9},{9,8},{10,11... | collective-permute-start | bytes 466952 | tf_op jit(solution)/shard_map/ppermute | solution.py:370
  36.4 1.4 %collective-permute-start.10 = (f32[304,128]{1,0:T(8,128)S(1)}, f32[304,128]{1,0:T(8,128)S(1)}, u32[]{:S(2)}, u32[]{:S(2)}) collective-permute-start(f32[304,128]{1,0:T(8,128)S(1)} %collective-permute-done.6.refs_1_), channel_id=1, source_target_pairs={{0,1},{1,0},{2,3},{3,2},{4,5},{5,4},{6,7},{7,6},{8,9},{9,8},{10,11... | collective-permute-start | bytes 466952 | tf_op jit(solution)/shard_map/ppermute | solution.py:370
  39.2 1.5 %collective-permute-start.13 = (f32[4,104,128]{2,1,0:T(8,128)S(1)}, f32[4,104,128]{2,1,0:T(8,128)S(1)}, u32[]{:S(2)}, u32[]{:S(2)}) collective-permute-start(f32[4,104,128]{2,1,0:T(8,128)S(1)} %slice.49), channel_id=1, source_target_pairs={{0,1},{1,0},{2,3},{3,2},{4,5},{5,4},{6,7},{7,6},{8,9},{9,8},{10,11... | collective-permute-start | bytes 638984 | tf_op jit(solution)/shard_map/ppermute | solution.py:370
  40.8 7.0 %collective-permute-start.14 = (f32[208,128]{1,0:T(8,128)S(1)}, f32[208,128]{1,0:T(8,128)S(1)}, u32[]{:S(2)}, u32[]{:S(2)}) collective-permute-start(f32[208,128]{1,0:T(8,128)S(1)} %pad_maximum_fusion.3), channel_id=1, source_target_pairs={{0,2},{1,3},{2,0},{3,1},{4,6},{5,7},{6,4},{7,5},{8,10},{9,11},{10,... | collective-permute-start | bytes 319496 | tf_op jit(solution)/shard_map/ppermute | solution.py:370
  41.7 6.8 %collective-permute-start.15 = (f32[208,128]{1,0:T(8,128)S(1)}, f32[208,128]{1,0:T(8,128)S(1)}, u32[]{:S(2)}, u32[]{:S(2)}) collective-permute-start(f32[208,128]{1,0:T(8,128)S(1)} %pad_maximum_fusion.4), channel_id=1, source_target_pairs={{0,6},{1,7},{2,4},{3,5},{4,2},{5,3},{6,0},{7,1},{8,14},{9,15},{10,... | collective-permute-start | bytes 319496 | tf_op jit(solution)/shard_map/ppermute | solution.py:370
  42.8 6.6 %collective-permute-start.16 = (f32[208,128]{1,0:T(8,128)S(1)}, f32[208,128]{1,0:T(8,128)S(1)}, u32[]{:S(2)}, u32[]{:S(2)}) collective-permute-start(f32[208,128]{1,0:T(8,128)S(1)} %pad_maximum_fusion.5), channel_id=1, source_target_pairs={{0,4},{1,5},{2,6},{3,7},{4,0},{5,1},{6,2},{7,3},{8,12},{9,13},{10,... | collective-permute-start | bytes 319496 | tf_op jit(solution)/shard_map/ppermute | solution.py:370
  49.8 7.1 %collective-permute-start.17 = (f32[304,128]{1,0:T(8,128)S(1)}, f32[304,128]{1,0:T(8,128)S(1)}, u32[]{:S(2)}, u32[]{:S(2)}) collective-permute-start(f32[304,128]{1,0:T(8,128)S(1)} %more_terms.11), channel_id=1, source_target_pairs={{0,12},{1,13},{2,14},{3,15},{4,8},{5,9},{6,10},{7,11},{8,4},{9,5},... | collective-permute-start | bytes 466952 | tf_op jit(solution)/shard_map/ppermute | solution.py:370
  57.0 6.6 %collective-permute-start.20 = (f32[304,128]{1,0:T(8,128)S(1)}, f32[304,128]{1,0:T(8,128)S(1)}, u32[]{:S(2)}, u32[]{:S(2)}) collective-permute-start(f32[304,128]{1,0:T(8,128)S(1)} %add.7.refs_0_), channel_id=1, source_target_pairs={{0,6},{1,7},{2,4},{3,5},{4,2},{5,3},{6,0},{7,1},{8,14},{9,15},{10,... | collective-permute-start | bytes 466952 | tf_op jit(solution)/shard_map/ppermute | solution.py:370
  59.5 5.7 %collective-permute-start.19 = (f32[304,128]{1,0:T(8,128)S(1)}, f32[304,128]{1,0:T(8,128)S(1)}, u32[]{:S(2)}, u32[]{:S(2)}) collective-permute-start(f32[304,128]{1,0:T(8,128)S(1)} %add.7.refs_0_), channel_id=1, source_target_pairs={{0,2},{1,3},{2,0},{3,1},{4,6},{5,7},{6,4},{7,5},{8,10},{9,11},{10,... | collective-permute-start | bytes 466952 | tf_op jit(solution)/shard_map/ppermute | solution.py:370
  60.5 5.2 %collective-permute-start.18 = (f32[304,128]{1,0:T(8,128)S(1)}, f32[304,128]{1,0:T(8,128)S(1)}, u32[]{:S(2)}, u32[]{:S(2)}) collective-permute-start(f32[304,128]{1,0:T(8,128)S(1)} %add.7.refs_0_), channel_id=1, source_target_pairs={{0,4},{1,5},{2,6},{3,7},{4,0},{5,1},{6,2},{7,3},{8,12},{9,13},{10,... | collective-permute-start | bytes 466952 | tf_op jit(solution)/shard_map/ppermute | solution.py:370
  60.6 5.2 %collective-permute-start.21 = (f32[304,128]{1,0:T(8,128)S(1)}, f32[304,128]{1,0:T(8,128)S(1)}, u32[]{:S(2)}, u32[]{:S(2)}) collective-permute-start(f32[304,128]{1,0:T(8,128)S(1)} %add.7.refs_0_), channel_id=1, source_target_pairs={{0,1},{1,0},{2,3},{3,2},{4,5},{5,4},{6,7},{7,6},{8,9},{9,8},{10,11... | collective-permute-start | bytes 466952 | tf_op jit(solution)/shard_map/ppermute | solution.py:370
  63.6 2.1 %collective-permute-start.24 = (f32[304,128]{1,0:T(8,128)S(1)}, f32[304,128]{1,0:T(8,128)S(1)}, u32[]{:S(2)}, u32[]{:S(2)}) collective-permute-start(f32[304,128]{1,0:T(8,128)S(1)} %collective-permute-done.20.refs_3_), channel_id=1, source_target_pairs={{0,1},{1,0},{2,3},{3,2},{4,5},{5,4},{6,7},{7,6},{8,9},{9,8},{10,11... | collective-permute-start | bytes 466952 | tf_op jit(solution)/shard_map/ppermute | solution.py:370
  65.2 1.4 %collective-permute-start.23 = (f32[304,128]{1,0:T(8,128)S(1)}, f32[304,128]{1,0:T(8,128)S(1)}, u32[]{:S(2)}, u32[]{:S(2)}) collective-permute-start(f32[304,128]{1,0:T(8,128)S(1)} %collective-permute-done.19.refs_2_), channel_id=1, source_target_pairs={{0,1},{1,0},{2,3},{3,2},{4,5},{5,4},{6,7},{7,6},{8,9},{9,8},{10,11... | collective-permute-start | bytes 466952 | tf_op jit(solution)/shard_map/ppermute | solution.py:370
  65.7 1.4 %collective-permute-start.22 = (f32[304,128]{1,0:T(8,128)S(1)}, f32[304,128]{1,0:T(8,128)S(1)}, u32[]{:S(2)}, u32[]{:S(2)}) collective-permute-start(f32[304,128]{1,0:T(8,128)S(1)} %collective-permute-done.18.refs_1_), channel_id=1, source_target_pairs={{0,1},{1,0},{2,3},{3,2},{4,5},{5,4},{6,7},{7,6},{8,9},{9,8},{10,11... | collective-permute-start | bytes 466952 | tf_op jit(solution)/shard_map/ppermute | solution.py:370
  (1 other events, 11.0 us)
